TPU v7x, 256 devices: a whole 4x4x8 slice. The times are simulated.
256 devices in a mesh: dp: 32 (over z_hi, x, core), sp: 8 (over y, z_lo).
Axes of the slice: x: 4, y: 4, z: 8 (z_hi: 4, z_lo: 2; z = z_hi * 2 + z_lo), core: 2. Of those that a mesh axis runs over, the one named last changes fastest.
Arguments:
- qkv_video: bfloat16 [64, 3, 768, 2048], P('dp', None, 'sp'), may hold values from -6 to 6
- qkv_text: bfloat16 [64, 3, 128, 2048], P('dp', None, None, 'sp'), may hold values from -6 to 6
- qk_gains: float32 [2, 2, 128], replicated, may hold values from 0.5 to 9
- text_len: int32 [64], P('dp'), may hold values from 32 to 128, as said below
- w_out_video: bfloat16 [2048, 3072], P('sp', 'dp'), may hold values from -0.125 to 0.125
- w_out_text: bfloat16 [2048, 3072], P('sp', 'dp'), may hold values from -0.125 to 0.125
- cot_video: bfloat16 [64, 768, 3072], P('dp', 'sp'), may hold values from -6 to 6
- cot_text: bfloat16 [64, 128, 3072], P('dp', None, 'sp'), may hold values from -6 to 6
Outputs:
- grad_qkv_video: bfloat16 [64, 3, 768, 2048], P('dp', None, 'sp')
- grad_qkv_text: bfloat16 [64, 3, 128, 2048], P('dp', None, None, 'sp')
- grad_w_video: float32 [2048, 3072], P('sp', 'dp')
- grad_w_text: float32 [2048, 3072], P('sp', 'dp')
Inputs may be any that keep to these rules, and one draw needn't show every extreme that they name: `text_len`: the first clip holds 128 unpadded text tokens.
All inputs are finite; a program needn't handle non-finite values.
Results may differ from a plain program's by a relative error of at most 0.006.
The roundings to bfloat16 on the way count: a program that leaves them out, or rounds other values in their place, can miss the bound.
Values may be sent and summed in bfloat16 or wider, within the bound.
No kernel may reach another device: no remote copies, remote signals or barrier semaphores. Data moves between devices by JAX's collectives and lax.ppermute only.
A program may use at most 128 MiB of HBM per device.

v0:
```python
import jax
import jax.numpy as jnp
from jax import lax
from jax.sharding import PartitionSpec as P

DH = 128


def norm_forward(raw_rows, gain_vec):
    per_head = raw_rows.astype(jnp.float32).reshape(raw_rows.shape[0], -1, DH)
    inverse = lax.rsqrt(jnp.mean(per_head * per_head, axis=-1, keepdims=True) + 1e-06)
    unit_vec = per_head * inverse
    return (unit_vec, inverse, (unit_vec * gain_vec).astype(jnp.bfloat16))


def norm_backward(unit_vec, inverse, gain_vec, incoming):
    scaled = incoming * gain_vec
    return inverse * (scaled - unit_vec * jnp.mean(scaled * unit_vec, axis=-1, keepdims=True))


def attend_both(video, text, length, gains, grad_out):
    video_len = video.shape[1]
    query_video = norm_forward(video[0], gains[0, 0])
    key_video = norm_forward(video[1], gains[0, 1])
    query_text = norm_forward(text[0], gains[1, 0])
    key_text = norm_forward(text[1], gains[1, 1])
    queries = jnp.concatenate([query_video[2], query_text[2]], axis=0)
    all_keys = jnp.concatenate([key_video[2], key_text[2]], axis=0)
    all_values = jnp.concatenate([video[2], text[2]], axis=0)
    all_values = all_values.reshape(all_values.shape[0], -1, DH)
    seq_len = queries.shape[0]
    visible = jnp.arange(seq_len, dtype=jnp.int32) < video_len + length
    scores = jnp.einsum(
        "qhd,khd->hqk", queries, all_keys, preferred_element_type=jnp.float32
    ) * DH ** (-0.5)
    scores = jnp.where(visible[None, None, :], scores, -1e30)
    highest = jnp.max(scores, axis=-1, keepdims=True)
    powers = jnp.exp(scores - highest)
    probability = powers / jnp.sum(powers, axis=-1, keepdims=True)
    prob_low = probability.astype(jnp.bfloat16)
    attended = jnp.einsum("hqk,khd->qhd", prob_low, all_values, preferred_element_type=jnp.float32)
    attended = attended.reshape(attended.shape[0], -1).astype(jnp.bfloat16)
    grad_rows = grad_out.reshape(grad_out.shape[0], -1, DH)
    grad_prob = jnp.einsum(
        "qhd,khd->hqk", grad_rows, all_values, preferred_element_type=jnp.float32
    )
    grad_score = (
        probability
        * (grad_prob - jnp.sum(probability * grad_prob, axis=-1, keepdims=True))
        * DH ** (-0.5)
    )
    score_low = grad_score.astype(jnp.bfloat16)
    grad_query = jnp.einsum("hqk,khd->qhd", score_low, all_keys, preferred_element_type=jnp.float32)
    grad_key = jnp.einsum("hqk,qhd->khd", score_low, queries, preferred_element_type=jnp.float32)
    grad_value = jnp.einsum("hqk,qhd->khd", prob_low, grad_rows, preferred_element_type=jnp.float32)
    video_grad = jnp.stack(
        [
            norm_backward(query_video[0], query_video[1], gains[0, 0], grad_query[:video_len]),
            norm_backward(key_video[0], key_video[1], gains[0, 1], grad_key[:video_len]),
            grad_value[:video_len],
        ]
    )
    text_grad = jnp.stack(
        [
            norm_backward(query_text[0], query_text[1], gains[1, 0], grad_query[video_len:]),
            norm_backward(key_text[0], key_text[1], gains[1, 1], grad_key[video_len:]),
            grad_value[video_len:],
        ]
    )
    video_grad = video_grad.reshape(3, video_len, -1).astype(jnp.bfloat16)
    text_grad = text_grad.reshape(3, text.shape[1], -1).astype(jnp.bfloat16)
    return (attended, video_grad, text_grad)


def body(qkv_video, qkv_text, qk_gains, text_len, w_out_video, w_out_text, cot_video, cot_text):
    video_heads = lax.all_to_all(qkv_video, "sp", split_axis=3, concat_axis=2, tiled=True)
    rows_video, rows_text = (
        lax.all_gather(w_out_video, "dp", axis=1, tiled=True),
        lax.all_gather(w_out_text, "dp", axis=1, tiled=True),
    )
    text_full = lax.all_gather(cot_text, "sp", axis=2, tiled=True)
    video_full = lax.all_gather(cot_video, "sp", axis=1, tiled=True)
    grad_out_text = jnp.einsum(
        "ctd,hd->cth", text_full, rows_text, preferred_element_type=jnp.float32
    ).astype(jnp.bfloat16)
    grad_out_video = jnp.einsum(
        "cvd,hd->cvh", video_full, rows_video, preferred_element_type=jnp.float32
    ).astype(jnp.bfloat16)
    grad_out = jnp.concatenate([grad_out_video, grad_out_text], axis=1)

    def clip_step(packed):
        return attend_both(packed[0], packed[1], packed[2], qk_gains, packed[3])

    attended, grad_heads, grad_qkv_text = lax.map(
        clip_step, (video_heads, qkv_text, text_len, grad_out)
    )
    video_len = video_heads.shape[2]
    attended_video = attended[:, :video_len]
    attended_text = attended[:, video_len:]
    video_share = jnp.einsum(
        "cvh,cvd->hd", attended_video, video_full, preferred_element_type=jnp.float32
    )
    text_share = jnp.einsum(
        "cth,ctd->hd", attended_text, text_full, preferred_element_type=jnp.float32
    )
    grad_w_video, grad_w_text = (
        lax.psum_scatter(video_share, "dp", scatter_dimension=1, tiled=True),
        lax.psum_scatter(text_share, "dp", scatter_dimension=1, tiled=True),
    )
    grad_qkv_video = lax.all_to_all(grad_heads, "sp", split_axis=2, concat_axis=3, tiled=True)
    return (grad_qkv_video, grad_qkv_text, grad_w_video, grad_w_text)


def solution(mesh):
    return jax.shard_map(
        body,
        mesh=mesh,
        in_specs=(
            P("dp", None, "sp", None),
            P("dp", None, None, "sp"),
            P(),
            P("dp"),
            P("sp", "dp"),
            P("sp", "dp"),
            P("dp", "sp", None),
            P("dp", None, "sp"),
        ),
        out_specs=(
            P("dp", None, "sp", None),
            P("dp", None, None, "sp"),
            P("sp", "dp"),
            P("sp", "dp"),
        ),
        check_vma=False,
    )
```

profile of v0, /device:TPU:8, one launch (start us, length us, event | category | flops | bytes accessed | tf_op | source)
XLA Modules:
  0.0 728.9 jit_solution(1082423814642260231)
XLA Ops:
  10.0 7.1 copy.132
  17.0 6.6 all-to-all-start
  23.6 61.6 %all-gather.9.cloned.1.call-done = bf16[2,128,3072]{2,1,0:T(8,128)(2,1)} async-done(((bf16[2,128,384]{2,1,0:T(8,128)(2,1)}), bf16[2,128,3072]{2,1,0:T(8,128)(2,1)}) %all-gather.9.cloned.1.call-update) | async-done | bytes 1572880 | tf_op jit(solution)/shard_map/all_gather | solution.py:81
  85.2 56.5 %all-gather.11.cloned.1.call-done = bf16[256,3072]{0,1:T(8,128)(2,1)} async-done(((bf16[256,96]{0,1:T(8,128)(2,1)}), bf16[256,3072]{0,1:T(8,128)(2,1)}) %all-gather.11.cloned.1.call-update) | async-done | bytes 1572880 | tf_op jit(solution)/shard_map/all_gather | solution.py:79
  141.7 2.4 fusion.59
  144.2 6.9 copy.157
  151.1 43.5 %all-gather.7.cloned.1.call-done = bf16[256,3072]{0,1:T(8,128)(2,1)} async-done(((bf16[256,96]{0,1:T(8,128)(2,1)}), bf16[256,3072]{0,1:T(8,128)(2,1)}) %all-gather.7.cloned.1.call-update) | async-done | bytes 1572880 | tf_op jit(solution)/shard_map/all_gather | solution.py:78
  194.6 189.5 %all-gather.5.cloned.1.call-done = bf16[2,768,3072]{2,1,0:T(8,128)(2,1)} async-done(((bf16[2,96,3072]{2,1,0:T(8,128)(2,1)}), bf16[2,768,3072]{2,1,0:T(8,128)(2,1)}) %all-gather.5.cloned.1.call-update) | async-done | bytes 9437200 | tf_op jit(solution)/shard_map/all_gather | solution.py:82
  384.1 6.7 fusion.56
  391.8 125.9 %while.14 = (s32[]{:T(128)}, bf16[2,896,256]{2,1,0:T(8,128)(2,1)}, bf16[2,3,768,256]{2,3,1,0:T(8,128)(2,1)}, bf16[2,3,128,256]{3,2,1,0:T(8,128)(2,1)}, bf16[2,3,...) while((s32[]{:T(128)}, bf16[2,896,256]{2,1,0:T(8,128)(2,1)}, ...), condition=%wide.region_12.13_spmd, body=%wide.region_0.12_spmd.sunk | while | flops 2518624768 | bytes 95525712 | solution.py:94
  399.8 4.9 fusion.89
  404.9 3.6 fusion.90
  408.7 1.9 constant_dynamic-slice_fusion.12
  410.9 3.7 fusion.92
  414.6 10.3 %fusion.94 = f32[896,2,128]{2,0,1:T(8,128)S(1)} fusion(f32[2,896,896]{1,2,0:T(8,128)} %fusion.92, bf16[128,2,128]{2,0,1:T(8,128)(2,1)S(1)} %multiply_convert_fusion.17, bf16[768,2,128]{2,0,1:T(8,128)(2,1)} %copy-done.3, f32[2,896,896]{1,2,0:T(8,128)} %get-tuple-element.232, f32[2,896]{1,0:T(2,128)S(1)} %get-tuple-element.233), kind=kOutput, calls=%fused_computation.18.clone.1 | convolution fusion | flops 423201408 | bytes 14228480 | tf_op jit(solution)/shard_map/while/body/eval_jaxpr/hqk,khd->qhd/dot_general | solution.py:53
  426.0 10.4 %fusion.93 = f32[896,2,128]{2,0,1:T(8,128)S(1)} fusion(f32[2,896,896]{1,2,0:T(8,128)} %fusion.92, bf16[128,2,128]{2,0,1:T(8,128)(2,1)} %copy-done.5, bf16[768,2,128]{2,0,1:T(8,128)(2,1)} %copy-done.2, f32[2,896,896]{1,2,0:T(8,128)} %get-tuple-element.232, f32[2,896]{1,0:T(2,128)} %copy-done.13), kind=kOutput, calls=%fused_computation.19.clone.1 | convolution fusion | flops 423201408 | bytes 14228480 | tf_op jit(solution)/shard_map/while/body/eval_jaxpr/hqk,qhd->khd/dot_general | solution.py:54
  439.7 4.0 fusion.91
  445.2 1.7 copy.205
  462.7 4.9 fusion.89
  467.9 3.6 fusion.90
  471.7 1.9 constant_dynamic-slice_fusion.12
  473.8 3.7 fusion.92
  477.5 10.3 %fusion.94 = f32[896,2,128]{2,0,1:T(8,128)S(1)} fusion(f32[2,896,896]{1,2,0:T(8,128)} %fusion.92, bf16[128,2,128]{2,0,1:T(8,128)(2,1)S(1)} %multiply_convert_fusion.17, bf16[768,2,128]{2,0,1:T(8,128)(2,1)} %copy-done.3, f32[2,896,896]{1,2,0:T(8,128)} %get-tuple-element.232, f32[2,896]{1,0:T(2,128)S(1)} %get-tuple-element.233), kind=kOutput, calls=%fused_computation.18.clone.1 | convolution fusion | flops 423201408 | bytes 14228480 | tf_op jit(solution)/shard_map/while/body/eval_jaxpr/hqk,khd->qhd/dot_general | solution.py:53
  488.9 10.4 %fusion.93 = f32[896,2,128]{2,0,1:T(8,128)S(1)} fusion(f32[2,896,896]{1,2,0:T(8,128)} %fusion.92, bf16[128,2,128]{2,0,1:T(8,128)(2,1)} %copy-done.5, bf16[768,2,128]{2,0,1:T(8,128)(2,1)} %copy-done.2, f32[2,896,896]{1,2,0:T(8,128)} %get-tuple-element.232, f32[2,896]{1,0:T(2,128)} %copy-done.13), kind=kOutput, calls=%fused_computation.19.clone.1 | convolution fusion | flops 423201408 | bytes 14228480 | tf_op jit(solution)/shard_map/while/body/eval_jaxpr/hqk,qhd->khd/dot_general | solution.py:54
  502.6 4.0 fusion.91
  508.1 1.7 copy.205
  517.7 9.5 %convolution_bitcast_fusion.1 = f32[256,3072]{0,1:T(8,128)} fusion(bf16[2,768,3072]{2,1,0:T(8,128)(2,1)} %all-gather.5.cloned.1.call-done, bf16[2,896,256]{2,1,0:T(8,128)(2,1)} %get-tuple-element.55), kind=kOutput, calls=%fused_computation.86 | convolution fusion | flops 2415919104 | bytes 13369344 | tf_op jit(solution)/shard_map/cvh,cvd->hd/dot_general | solution.py:100
  527.3 3.3 convolution_bitcast_fusion
  530.6 6.1 copy.138
  536.7 33.4 %all_to_all.36 = bf16[2,3,768,256]{3,0,1,2:T(2,128)(2,1)S(1)} all-to-all(bf16[2,3,768,256]{3,0,1,2:T(2,128)(2,1)S(1)} %copy.138), channel_id=1, replica_groups=mesh['dp'=32,'sp'=8] {'sp'}, dimensions={2} | all-to-all | bytes 4718592 | tf_op jit(solution)/shard_map/all_to_all | solution.py:110
  572.2 51.9 %reduce-scatter.3.cloned.1.call-done = f32[256,96]{0,1:T(8,128)} async-done(((f32[256,3072]{0,1:T(8,128)}), f32[256,96]{0,1:T(8,128)}) %reduce-scatter.3.cloned.1.call-update) | async-done | bytes 98320 | tf_op jit(solution)/shard_map/reduce_scatter | solution.py:107
  624.0 98.0 %reduce-scatter.5.cloned.1.call-done = f32[256,96]{0,1:T(8,128)} async-done(((f32[256,3072]{0,1:T(8,128)}), f32[256,96]{0,1:T(8,128)}) %reduce-scatter.5.cloned.1.call-update) | async-done | bytes 98320 | tf_op jit(solution)/shard_map/reduce_scatter | solution.py:108
  (173 shorter events, 48.8 us)
Async XLA Ops:
  7.2 78.1 %all-gather.9.cloned.1.call-start = ((), (), s32[]{:S(2)}) async-start(), calls=%async_computation.6 | async-start | bytes 1769472 | tf_op jit(solution)/shard_map/all_gather | solution.py:81
  7.9 133.8 %all-gather.11.cloned.1.call-start = ((), (), s32[]{:S(2)}) async-start(), calls=%async_computation.7 | async-start | bytes 1622016 | tf_op jit(solution)/shard_map/all_gather | solution.py:79
  8.6 186.0 %all-gather.7.cloned.1.call-start = ((), (), s32[]{:S(2)}) async-start(), calls=%async_computation.5 | async-start | bytes 1622016 | tf_op jit(solution)/shard_map/all_gather | solution.py:78
  9.4 374.7 %all-gather.5.cloned.1.call-start = ((), (), s32[]{:S(2)}) async-start(), calls=%async_computation.4 | async-start | bytes 10616832 | tf_op jit(solution)/shard_map/all_gather | solution.py:82
  17.0 127.2 %all-to-all-start = ((bf16[2,3,96,2048]{2,1,0,3:T(4,128)(2,1)}), bf16[2,3,96,2048]{2,1,0,3:T(4,128)(2,1)}, u32[]{:S(2)}, u32[]{:S(2)}) async-start(bf16[2,3,96,2048]{2,1,0,3:T(4,128)(2,1)} %copy.132), calls=%async_computation | async-start | bytes 8388608 | tf_op jit(solution)/shard_map/all_to_all | solution.py:76
  23.6 600.4 %reduce-scatter.3.cloned.1.call-start = ((), (), s32[]{:S(2)}) async-start(), calls=%async_computation.8 | async-start | bytes 3244032 | tf_op jit(solution)/shard_map/reduce_scatter | solution.py:107
  394.3 0.6 copy-start.10
  394.3 1.2 copy-start.8
  394.4 3.2 copy-start.12
  394.6 10.0 %copy-start.2 = (bf16[768,2,128]{2,0,1:T(8,128)(2,1)}, bf16[768,2,128]{2,0,1:T(8,128)(2,1)S(1)}, u32[]{:S(2)}) copy-start(bf16[768,2,128]{2,0,1:T(8,128)(2,1)S(1)} %multiply_convert_fusion.20) | copy-start | bytes 1179652 | tf_op jit(solution)/shard_map/while
  395.5 9.1 %copy-start.3 = (bf16[768,2,128]{2,0,1:T(8,128)(2,1)}, bf16[768,2,128]{2,0,1:T(8,128)(2,1)S(1)}, u32[]{:S(2)}) copy-start(bf16[768,2,128]{2,0,1:T(8,128)(2,1)S(1)} %multiply_convert_fusion.18) | copy-start | bytes 1179652 | tf_op jit(solution)/shard_map/while
  397.8 7.0 copy-start.5
  404.6 9.9 %copy-start.13 = (f32[2,896]{1,0:T(2,128)}, f32[2,896]{1,0:T(2,128)S(1)}, u32[]{:S(2)}) copy-start(f32[2,896]{1,0:T(2,128)S(1)} %get-tuple-element.233) | copy-start | bytes 21508 | tf_op jit(solution)/shard_map/while
  410.8 15.1 %copy-start = (bf16[1,896,256]{1,2,0:T(8,128)(2,1)}, bf16[1,896,256]{1,2,0:T(8,128)(2,1)S(1)}, u32[]{:S(2)}) copy-start(bf16[1,896,256]{1,2,0:T(8,128)(2,1)S(1)} %copy.200) | copy-start | bytes 1376260 | tf_op jit(solution)/shard_map/while
  439.6 4.8 copy-start.4
  439.6 8.9 %copy-start.11 = (f32[128]{0:T(128)S(1)}, f32[128]{0:T(128)}, u32[]{:S(2)}) copy-start(f32[128]{0:T(128)} %copy-done.10) | copy-start | bytes 1540 | tf_op jit(solution)/shard_map/while
  439.6 11.8 %copy-start.9 = (f32[128]{0:T(128)S(1)}, f32[128]{0:T(128)}, u32[]{:S(2)}) copy-start(f32[128]{0:T(128)} %copy-done.8) | copy-start | bytes 1540 | tf_op jit(solution)/shard_map/while
  443.7 0.8 copy-start.1
  457.3 0.6 copy-start.10
  457.3 1.2 copy-start.8
  457.3 3.2 copy-start.12
  457.6 10.0 %copy-start.2 = (bf16[768,2,128]{2,0,1:T(8,128)(2,1)}, bf16[768,2,128]{2,0,1:T(8,128)(2,1)S(1)}, u32[]{:S(2)}) copy-start(bf16[768,2,128]{2,0,1:T(8,128)(2,1)S(1)} %multiply_convert_fusion.20) | copy-start | bytes 1179652 | tf_op jit(solution)/shard_map/while
  458.5 9.1 %copy-start.3 = (bf16[768,2,128]{2,0,1:T(8,128)(2,1)}, bf16[768,2,128]{2,0,1:T(8,128)(2,1)S(1)}, u32[]{:S(2)}) copy-start(bf16[768,2,128]{2,0,1:T(8,128)(2,1)S(1)} %multiply_convert_fusion.18) | copy-start | bytes 1179652 | tf_op jit(solution)/shard_map/while
  460.8 7.0 copy-start.5
  467.6 9.9 %copy-start.13 = (f32[2,896]{1,0:T(2,128)}, f32[2,896]{1,0:T(2,128)S(1)}, u32[]{:S(2)}) copy-start(f32[2,896]{1,0:T(2,128)S(1)} %get-tuple-element.233) | copy-start | bytes 21508 | tf_op jit(solution)/shard_map/while
  473.8 15.1 %copy-start = (bf16[1,896,256]{1,2,0:T(8,128)(2,1)}, bf16[1,896,256]{1,2,0:T(8,128)(2,1)S(1)}, u32[]{:S(2)}) copy-start(bf16[1,896,256]{1,2,0:T(8,128)(2,1)S(1)} %copy.200) | copy-start | bytes 1376260 | tf_op jit(solution)/shard_map/while
  502.6 4.8 copy-start.4
  502.6 8.9 %copy-start.11 = (f32[128]{0:T(128)S(1)}, f32[128]{0:T(128)}, u32[]{:S(2)}) copy-start(f32[128]{0:T(128)} %copy-done.10) | copy-start | bytes 1540 | tf_op jit(solution)/shard_map/while
  502.6 11.8 %copy-start.9 = (f32[128]{0:T(128)S(1)}, f32[128]{0:T(128)}, u32[]{:S(2)}) copy-start(f32[128]{0:T(128)} %copy-done.8) | copy-start | bytes 1540 | tf_op jit(solution)/shard_map/while
  506.6 0.8 copy-start.1
  517.7 9.5 %copy-start.6 = (bf16[2,128,3072]{2,1,0:T(8,128)(2,1)S(1)}, bf16[2,128,3072]{2,1,0:T(8,128)(2,1)}, u32[]{:S(2)}) copy-start(bf16[2,128,3072]{2,1,0:T(8,128)(2,1)} %all-gather.9.cloned.1.call-done) | copy-start | bytes 4718596
  527.2 194.9 %reduce-scatter.5.cloned.1.call-start = ((), (), s32[]{:S(2)}) async-start(), calls=%async_computation.9 | async-start | bytes 3244032 | tf_op jit(solution)/shard_map/reduce_scatter | solution.py:108
  (2 other events, 1.1 us)
Sparse Core Ops, SparseCore 0:
  9.8 75.3 all-gather.8
  87.8 53.9 all-gather.10
  144.3 50.2 all-gather.6
  196.3 187.7 all-gather.4
  527.3 96.6 reduce-scatter.2
  628.9 93.1 reduce-scatter.4
where the time goes:
time: 730 us; the launch traced here: 729 us
  waiting for transfers between devices  504 us (69%)
  matrix products  95.7 us (13%)
  local copies, waits for them, and re-layouts  55.9 us (8%)
  blocking collectives  33.4 us (5%)
  other arithmetic  17.4 us (2%)
  between operations  14.2 us (2%)
    all_gather x1, waiting for transfers between devices, body(): video_full = lax.all_gather(cot_video, 'sp', axis=1, tiled=True)  189 us
    reduce_scatter x1, waiting for transfers between devices, body(): lax.psum_scatter(text_share, 'dp', scatter_dimension=1, tiled=True)  98 us
    all_gather x1, waiting for transfers between devices, body(): text_full = lax.all_gather(cot_text, 'sp', axis=2, tiled=True)  61.6 us
    all_gather x1, waiting for transfers between devices, body(): lax.all_gather(w_out_text, 'dp', axis=1, tiled=True)  56.5 us
    reduce_scatter x1, waiting for transfers between devices, body(): lax.psum_scatter(video_share, 'dp', scatter_dimension=1, tiled=True)  51.9 us
    all_gather x1, waiting for transfers between devices, body(): lax.all_gather(w_out_video, 'dp', axis=1, tiled=True)  43.5 us
    all_to_all x1, blocking collectives, body(): lax.all_to_all(grad_heads, 'sp', split_axis=2, concat_axis=3, tiled=True)  33.4 us
    dot_general x2, matrix products, attend_both(): jnp.einsum('hqk,qhd->khd', score_low, queries, preferred_element_type=jnp...  20.8 us
  transfers between devices with their start and end apart: 7, of which 6 were waited for; matrix products, arithmetic and copies ran while one was open for 4% of the time, Pallas kernels for 0%

commit v1 on v0

v1 whole, which is shorter than its diff:
```python
import functools

import jax
import jax.numpy as jnp
from jax import lax
from jax.experimental import pallas as pl
from jax.experimental.pallas import tpu as pltpu
from jax.sharding import PartitionSpec as P

DH = 128
VID = 768
TXT = 128
SEQ = VID + TXT
BLK = 96
BF = jnp.bfloat16
F32 = jnp.float32
SCALE = DH ** (-0.5)
RELS = [(dy, dz) for dy in range(4) for dz in range(2)]
ANY = pl.BlockSpec(memory_space=pl.ANY)
SMEM = pl.BlockSpec(memory_space=pltpu.SMEM)
MB = 1024 * 1024


def shape_of(*dims, dtype=BF):
    return jax.ShapeDtypeStruct(dims, dtype)


def params(mb):
    return pltpu.CompilerParams(vmem_limit_bytes=mb * MB)


def cost(flops, nbytes, exps=0):
    return pl.CostEstimate(flops=flops, bytes_accessed=nbytes, transcendentals=exps)


def sp_perm(dy, dz):
    return [(y * 2 + z, ((y + dy) % 4) * 2 + (z + dz) % 2) for y in range(4) for z in range(2)]


def send_sp(value, dy, dz):
    return lax.ppermute(value, "sp", sp_perm(dy, dz))


def dp_perm(dh, dx, dc):
    return [
        ((h * 4 + x) * 2 + c, (((h + dh) % 4) * 4 + (x + dx) % 4) * 2 + (c + dc) % 2)
        for h in range(4)
        for x in range(4)
        for c in range(2)
    ]


def send_dp(value, dh, dx, dc):
    return lax.ppermute(value, "dp", dp_perm(dh, dx, dc))


def head_cols(yy, zz, half):
    return pl.multiple_of(yy * 512 + lax.rem(zz + half, 2) * 256, 256)


def relative_places(idx):
    y, zl = idx[0], idx[1]
    for k, (dy, dz) in enumerate(RELS):
        yy, zz = lax.rem(y + dy, 4), lax.rem(zl + dz, 2)
        for half in range(2):
            yield k, zz, half, pl.ds(head_cols(yy, zz, half), 256)


def pack_kernel(idx, qkv, cot, qt, ct, *rest):
    outs, held, sem_in, sem_out = rest[:14], rest[14:18], rest[18], rest[19]
    zl = idx[1]
    ins = [
        pltpu.make_async_copy(source, place, sem_in.at[n])
        for n, (source, place) in enumerate(zip((qkv, cot, qt, ct), held))
    ]
    for n in (3, 1, 2, 0):
        ins[n].start()
    out = []

    def leave(source, target):
        copy = pltpu.make_async_copy(source, target, sem_out.at[len(out)])
        copy.start()
        out.append(copy)

    for n in (3, 1, 2):
        ins[n].wait()
        leave(held[n].at[1 - zl], outs[7 + 2 * n])
        leave(held[n].at[zl], outs[6 + 2 * n])
    ins[0].wait()
    for k, zz, half, cols in relative_places(idx):
        leave(held[0].at[zz, :, :, cols], outs[k].at[:, :, pl.ds(256 * half, 256)])
    for copy in out:
        copy.wait()


def pack(idx, qkv, cot, qt, ct):
    outs = [shape_of(3, BLK, 512)] * 8
    outs += [shape_of(BLK, 3072)] * 2 + [shape_of(3, TXT, 256)] * 2 + [shape_of(TXT, 384)] * 2
    return pl.pallas_call(
        pack_kernel,
        out_shape=outs,
        in_specs=[SMEM, ANY, ANY, ANY, ANY],
        out_specs=[ANY] * len(outs),
        scratch_shapes=[pltpu.VMEM(v.shape, BF) for v in (qkv, cot, qt, ct)]
        + [pltpu.SemaphoreType.DMA((4,)), pltpu.SemaphoreType.DMA((22,))],
        compiler_params=params(60),
        cost_estimate=cost(0, 9 * MB),
        name="pack",
    )(idx, qkv, cot, qt, ct)


def unpack_kernel(idx, *rest):
    chunks, own, other = rest[:8], rest[8], rest[9]
    out_video, out_text, video, text, sem = rest[10:]
    zl = idx[1]
    copies = []

    def enter(source, target):
        copy = pltpu.make_async_copy(source, target, sem.at[len(copies)])
        copy.start()
        copies.append(copy)

    for k, zz, half, cols in relative_places(idx):
        enter(chunks[k].at[:, :, pl.ds(256 * half, 256)], video.at[zz, :, :, cols])
    enter(own, text.at[zl])
    enter(other, text.at[1 - zl])
    for copy in copies:
        copy.wait()
    copies = [
        pltpu.make_async_copy(video, out_video, sem.at[0]),
        pltpu.make_async_copy(text, out_text, sem.at[1]),
    ]
    for copy in copies:
        copy.start()
    for copy in copies:
        copy.wait()


def unpack(idx, chunks, own, other):
    outs = [shape_of(2, 3, BLK, 2048), shape_of(2, 3, TXT, 256)]
    return pl.pallas_call(
        unpack_kernel,
        out_shape=outs,
        in_specs=[SMEM] + [ANY] * 10,
        out_specs=[ANY] * 2,
        scratch_shapes=[pltpu.VMEM(v.shape, BF) for v in outs]
        + [pltpu.SemaphoreType.DMA((18,))],
        compiler_params=params(60),
        cost_estimate=cost(0, 6 * MB),
        name="unpack",
    )(idx, *chunks, own, other)


def join_text_kernel(idx, *rest):
    chunks, out, held, sem = rest[:8], rest[8], rest[9], rest[10]
    y, zl = idx[0], idx[1]
    copies = []
    for k, (dy, dz) in enumerate(RELS):
        s = lax.rem(y + 4 - dy, 4) * 2 + lax.rem(zl + dz, 2)
        cols = pl.ds(pl.multiple_of(s * 384, 384), 384)
        copies.append(pltpu.make_async_copy(chunks[k], held.at[:, cols], sem.at[k]))
    for copy in copies:
        copy.start()
    for copy in copies:
        copy.wait()
    copy = pltpu.make_async_copy(held, out, sem.at[0])
    copy.start()
    copy.wait()


def join_text(idx, chunks):
    return pl.pallas_call(
        join_text_kernel,
        out_shape=shape_of(TXT, 3072),
        in_specs=[SMEM] + [ANY] * 8,
        out_specs=ANY,
        scratch_shapes=[pltpu.VMEM((TXT, 3072), BF), pltpu.SemaphoreType.DMA((8,))],
        compiler_params=params(60),
        cost_estimate=cost(0, 2 * MB),
        name="join_text",
    )(idx, *chunks)


def normed_rows(raw, gain):
    wide = raw.astype(F32)
    inverse = lax.rsqrt(jnp.mean(wide * wide, axis=-1, keepdims=True) + 1e-6)
    unit = wide * inverse
    return unit, inverse, (unit * gain).astype(BF)


def joint_rows(chunks, text, part):
    return jnp.concatenate([c[part] for c in chunks], axis=0), text[part]


def dot(a, b, dims):
    return lax.dot_general(a, b, (dims, ((), ())), preferred_element_type=F32)


NN = ((1,), (0,))
NT = ((1,), (1,))
TN = ((0,), (0,))


def forward_kernel(length, gains, *rest):
    chunks, own, other = rest[:8], rest[8], rest[9]
    prob_out, att_video, att_text = rest[10:]
    text = jnp.where(pl.program_id(0) < 2, own[...], other[...])
    normed = []
    for part in range(2):
        video_raw, text_raw = joint_rows(chunks, text, part)
        normed.append(
            jnp.concatenate(
                [
                    normed_rows(video_raw, gains[0, part : part + 1])[2],
                    normed_rows(text_raw, gains[1, part : part + 1])[2],
                ],
                axis=0,
            )
        )
    values = jnp.concatenate(joint_rows(chunks, text, 2), axis=0)
    scores = dot(normed[0], normed[1], NT) * SCALE
    seen = lax.broadcasted_iota(jnp.int32, (SEQ, TXT), 1) < length[0]
    scores = jnp.concatenate(
        [scores[:, :VID], jnp.where(seen, scores[:, VID:], -1e30)], axis=1
    )
    powers = jnp.exp(scores - jnp.max(scores, axis=-1, keepdims=True))
    prob = powers * (1.0 / jnp.sum(powers, axis=-1, keepdims=True))
    prob_out[0] = prob
    attended = dot(prob.astype(BF), values, NN).astype(BF)
    att_video[...] = attended[:VID]
    att_text[...] = attended[VID:]


CHUNK = pl.BlockSpec((3, BLK, DH), lambda h: (0, 0, h))
FIRST = pl.BlockSpec((3, TXT, DH), lambda h: (0, 0, jnp.minimum(h, 1)))
LATER = pl.BlockSpec((3, TXT, DH), lambda h: (0, 0, jnp.maximum(h - 2, 0)))
GAINS = pl.BlockSpec((2, 2, DH), lambda h: (0, 0, 0))
PROB = pl.BlockSpec((1, SEQ, SEQ), lambda h: (h, 0, 0))


def forward(length, gains, chunks, own, other):
    return pl.pallas_call(
        forward_kernel,
        grid=(4,),
        out_shape=[shape_of(4, SEQ, SEQ, dtype=F32), shape_of(VID, 512), shape_of(TXT, 512)],
        in_specs=[SMEM, GAINS] + [CHUNK] * 8 + [FIRST, LATER],
        out_specs=[
            PROB,
            pl.BlockSpec((VID, DH), lambda h: (0, h)),
            pl.BlockSpec((TXT, DH), lambda h: (0, h)),
        ],
        compiler_params=params(60),
        cost_estimate=cost(4 * 4 * SEQ * SEQ * DH, 18 * MB, 4 * SEQ * SEQ),
        name="forward",
    )(length, gains, *chunks, own, other)


def norm_back(unit, inverse, gain, incoming):
    scaled = incoming * gain
    return inverse * (scaled - unit * jnp.mean(scaled * unit, axis=-1, keepdims=True))


def backward_kernel(gains, prob_ref, grad_out, *rest):
    chunks, own, other = rest[:8], rest[8], rest[9]
    outs, out_own, out_other = rest[10:18], rest[18], rest[19]
    head = pl.program_id(0)
    text = jnp.where(head < 2, own[...], other[...])
    units = []
    normed = []
    for part in range(2):
        video_raw, text_raw = joint_rows(chunks, text, part)
        v = normed_rows(video_raw, gains[0, part : part + 1])
        t = normed_rows(text_raw, gains[1, part : part + 1])
        units.append((v, t))
        normed.append(jnp.concatenate([v[2], t[2]], axis=0))
    values = jnp.concatenate(joint_rows(chunks, text, 2), axis=0)
    prob = prob_ref[0]
    rows = grad_out[...]
    grad_prob = dot(rows, values, NT)
    inner = jnp.sum(prob * grad_prob, axis=-1, keepdims=True)
    low = (prob * (grad_prob - inner) * SCALE).astype(BF)
    grad_q = dot(low, normed[1], NN)
    grad_k = dot(normed[0], low, TN).T
    grad_v = dot(rows, prob.astype(BF), TN).T
    results = []
    for part, grad in enumerate((grad_q, grad_k)):
        v, t = units[part]
        results.append(
            (
                norm_back(v[0], v[1], gains[0, part : part + 1], grad[:VID]).astype(BF),
                norm_back(t[0], t[1], gains[1, part : part + 1], grad[VID:]).astype(BF),
            )
        )
    results.append((grad_v[:VID].astype(BF), grad_v[VID:].astype(BF)))
    for part in range(3):
        for k in range(8):
            outs[k][part] = results[part][0][k * BLK : (k + 1) * BLK]

    @pl.when(head < 2)
    def _():
        for part in range(3):
            out_own[part] = results[part][1]

    @pl.when(head >= 2)
    def _():
        for part in range(3):
            out_other[part] = results[part][1]


def backward(gains, prob, grad_out, chunks, own, other):
    return pl.pallas_call(
        backward_kernel,
        grid=(4,),
        out_shape=[shape_of(3, BLK, 512)] * 8 + [shape_of(3, TXT, 256)] * 2,
        in_specs=[GAINS, PROB, pl.BlockSpec((SEQ, DH), lambda h: (0, h))]
        + [CHUNK] * 8
        + [FIRST, LATER],
        out_specs=[CHUNK] * 8 + [FIRST, LATER],
        compiler_params=params(60),
        cost_estimate=cost(4 * 8 * SEQ * SEQ * DH, 20 * MB),
        name="backward",
    )(gains, prob, grad_out, *chunks, own, other)


def grad_out_kernel(*refs):
    cots, cot_text, w_video, w_text, out, acc = refs[:8], *refs[8:]
    step = pl.program_id(0)
    video = jnp.concatenate([c[...] for c in cots], axis=0)
    text = cot_text[...]
    for half in range(2):
        cols = slice(256 * half, 256 * half + 256)
        part_v = dot(video, w_video[:, half].reshape(768, 256), NN)
        part_t = dot(text, w_text[:, half].reshape(768, 256), NN)

        @pl.when(step == 0)
        def _():
            acc[:VID, cols] = part_v
            acc[VID:, cols] = part_t

        @pl.when(step > 0)
        def _():
            acc[:VID, cols] += part_v
            acc[VID:, cols] += part_t

    @pl.when(step == 3)
    def _():
        out[...] = acc[...].astype(BF)


def project_back(cots, cot_text, weights):
    def weight_spec(stream):
        return pl.BlockSpec((8, 2, None, BLK, 256), lambda i: (i, 0, stream, 0, 0))

    return pl.pallas_call(
        grad_out_kernel,
        grid=(4,),
        out_shape=shape_of(SEQ, 512),
        in_specs=[pl.BlockSpec((BLK, 768), lambda i: (0, i))] * 8
        + [pl.BlockSpec((TXT, 768), lambda i: (0, i)), weight_spec(0), weight_spec(1)],
        out_specs=pl.BlockSpec((SEQ, 512), lambda i: (0, 0)),
        scratch_shapes=[pltpu.VMEM((SEQ, 512), F32)],
        compiler_params=params(60),
        cost_estimate=cost(2 * SEQ * 512 * 3072, 13 * MB),
        name="project_back",
    )(*cots, cot_text, weights, weights)


def weight_grad_kernel(idx, att, *refs):
    cots, keep, send = refs[:-2], refs[-2], refs[-1]
    cot = jnp.concatenate([c[...] for c in cots], axis=0) if len(cots) > 1 else cots[0][...]
    part = dot(cot, att[...], TN).reshape(2, 2, BLK, 512)
    first = idx[2] == 0
    keep[...] = jnp.where(first, part[:, 0], part[:, 1]).astype(BF)
    send[...] = jnp.where(first, part[:, 1], part[:, 0]).astype(BF)


def weight_grad(idx, att, cots, name):
    rows, per = att.shape[0], cots[0].shape[0]
    out = pl.BlockSpec((2, BLK, 512), lambda i: (i, 0, 0))
    return pl.pallas_call(
        weight_grad_kernel,
        grid=(8,),
        out_shape=[shape_of(16, BLK, 512)] * 2,
        in_specs=[SMEM, pl.BlockSpec((rows, 512), lambda i: (0, 0))]
        + [pl.BlockSpec((per, 384), lambda i: (0, i))] * len(cots),
        out_specs=[out, out],
        compiler_params=params(60),
        cost_estimate=cost(2 * rows * 512 * 3072, 8 * MB),
        name=name,
    )(idx, att, *cots)


def wide_sum(parts):
    return functools.reduce(jnp.add, [p.astype(F32) for p in parts])


def reduce_weight(idx, keep, send):
    zh, x = idx[3], idx[4]
    got = send_dp(send, 0, 0, 1)
    keep = keep.reshape(4, 4, BLK, 512)
    got = got.reshape(4, 4, BLK, 512)

    def share(step):
        at = lax.rem(x + step, 4)
        return wide_sum(
            [lax.dynamic_index_in_dim(v, at, axis=1, keepdims=False) for v in (keep, got)]
        )

    arrived = [send_dp(share(step).astype(BF), 0, step, 0) for step in (2, 1, 3)]
    total = wide_sum([share(0)] + arrived).astype(BF)

    def slab(step):
        return lax.dynamic_index_in_dim(total, lax.rem(zh + step, 4), axis=0, keepdims=False)

    arrived = [send_dp(slab(step), step, 0, 0) for step in (2, 1, 3)]
    total = wide_sum([slab(0)] + arrived)
    last = send_sp(total[:, 256:].astype(BF), 0, 1)
    return wide_sum([total[:, :256], last]).T


def body(qkv_video, qkv_text, qk_gains, text_len, w_out_video, w_out_text, cot_video, cot_text):
    sp, dp = lax.axis_index("sp"), lax.axis_index("dp")
    y, zl = sp // 2, sp % 2
    idx = jnp.stack([y, zl, dp % 2, dp // 8, (dp // 2) % 4]).astype(jnp.int32)
    length = lax.dynamic_slice(text_len, (zl,), (1,))

    packed = pack(idx, qkv_video, cot_video, qkv_text, cot_text)
    sent = packed[:8]
    cot_own, cot_send, text_own, text_send, ct_own, ct_send = packed[8:]

    w_own = jnp.stack([w_out_video.T, w_out_text.T])
    w_pair = jnp.stack([w_own, send_sp(w_own, 0, 1)])
    weights = lax.all_gather(w_pair, "dp", axis=0)

    text_other = send_sp(text_send, 0, 1)
    ct_pair = jnp.stack([ct_own, send_sp(ct_send, 0, 1)])
    ct_all = [ct_pair] + [send_sp(ct_pair, dy, 0) for dy in range(1, 4)]
    text_cot = join_text(idx, [c[n] for c in ct_all for n in range(2)])

    chunks = [sent[0]] + [send_sp(sent[k], *RELS[k]) for k in range(1, 8)]

    near = [cot_own, send_sp(cot_send, 0, 1)]
    below = [send_sp(c, 1, 0) for c in near]
    above = [send_sp(c, 3, 0) for c in near]

    prob, att_video, att_text = forward(length, qk_gains, chunks, text_own, text_other)
    text_parts = weight_grad(idx, att_text, [text_cot], "weight_text")
    passed = lax.optimization_barrier((below[0], above[1], att_video, text_parts))
    att_video, text_parts = passed[2], passed[3]
    far = [send_sp(passed[0], 1, 0), send_sp(passed[1], 3, 0)]
    cots = near + below + far + above

    grad_w_text = reduce_weight(idx, *text_parts)
    video_parts = weight_grad(idx, att_video, cots, "weight_video")
    text_cot, video_parts = lax.optimization_barrier((text_cot, video_parts))
    grad_w_video = reduce_weight(idx, *video_parts)
    grad_out = project_back(cots, text_cot, weights)
    grads = backward(qk_gains, prob, grad_out, chunks, text_own, text_other)
    back = [grads[0]] + [
        send_sp(grads[k], -RELS[k][0], RELS[k][1]) for k in range(1, 8)
    ]
    grad_qkv_video, grad_qkv_text = unpack(idx, back, grads[8], send_sp(grads[9], 0, 1))
    return (grad_qkv_video, grad_qkv_text, grad_w_video, grad_w_text)


def solution(mesh):
    return jax.shard_map(
        body,
        mesh=mesh,
        in_specs=(
            P("dp", None, "sp", None),
            P("dp", None, None, "sp"),
            P(),
            P("dp"),
            P("sp", "dp"),
            P("sp", "dp"),
            P("dp", "sp", None),
            P("dp", None, "sp"),
        ),
        out_specs=(
            P("dp", None, "sp", None),
            P("dp", None, None, "sp"),
            P("sp", "dp"),
            P("sp", "dp"),
        ),
        check_vma=False,
    )
```

time: 730 us -> 309 us (0.42)
  waiting for transfers between devices: 504 us -> 122 us
  matrix products: 95.7 us -> 0 us
  starting transfers between devices: 6.81 us -> 85.5 us
  Pallas kernels: 0 us -> 63.4 us
  local copies, waits for them, and re-layouts: 55.9 us -> 6.79 us
  blocking collectives: 33.4 us -> 0 us
    all_gather x4 -> x1, waiting for transfers between devices: 351 us -> 0.01 us  [body(): weights = lax.all_gather(w_pair, 'dp', axis=0)]
    reduce_scatter x2 -> x0, waiting for transfers between devices: 150 us -> none  [the longest x1 98 us: body(): lax.psum_scatter(text_share, 'dp', scatter_dimension=1, tiled=True)]
    ppermute x0 -> x44, waiting for transfers between devices: none -> 122 us  [the longest x30 95 us: send_sp(): return lax.ppermute(value, 'sp', sp_perm(dy, dz))]
    dot_general x14 -> x0, matrix products: 85.9 us -> none  [the longest x2 20.8 us: attend_both(): jnp.einsum('hqk,qhd->khd', score_low, queries, preferred_element_type=jnp...]
    ppermute x0 -> x44, starting transfers between devices: none -> 85.5 us  [the longest x30 49.1 us: send_sp(): return lax.ppermute(value, 'sp', sp_perm(dy, dz))]
    pallas_call x0 -> x8, Pallas kernels: none -> 63.4 us  [the longest x2 15.5 us: weight_grad(): pl.pallas_call(weight_grad_kernel, grid=(8,), out_shape=[shape_of(16, BLK...]
    all_to_all x1 -> x0, blocking collectives: 33.4 us -> none  [body(): lax.all_to_all(grad_heads, 'sp', split_axis=2, concat_axis=3, tiled=True)]
    while x65 -> x0, local copies, waits for them, and re-layouts: 10.5 us -> none  [the longest x1 6.1 us: body(): lax.map(clip_step, (video_heads, qkv_text, text_len, grad_out))]
  transfers between devices with their start and end apart: 7 -> 45, of which waited for: 6 -> 21; matrix products, arithmetic and copies ran while one was open for 4% -> 4% of each run, Pallas kernels for 0% -> 20%
where the time goes in v1:
time: 309 us; the launch traced here: 303 us
  waiting for transfers between devices  122 us (39%)
  starting transfers between devices  85.5 us (28%)
  Pallas kernels  63.4 us (21%)
  between operations  14.6 us (5%)
  other arithmetic  10.2 us (3%)
  local copies, waits for them, and re-layouts  6.79 us (2%)
    ppermute x30, waiting for transfers between devices, send_sp(): return lax.ppermute(value, 'sp', sp_perm(dy, dz))  95 us
    ppermute x30, starting transfers between devices, send_sp(): return lax.ppermute(value, 'sp', sp_perm(dy, dz))  49.1 us
    ppermute x14, starting transfers between devices, send_dp(): return lax.ppermute(value, 'dp', dp_perm(dh, dx, dc))  36.3 us
    ppermute x14, waiting for transfers between devices, send_dp(): return lax.ppermute(value, 'dp', dp_perm(dh, dx, dc))  27 us
    pallas_call x2, Pallas kernels, weight_grad(): pl.pallas_call(weight_grad_kernel, grid=(8,), out_shape=[shape_of(16, BLK...  15.5 us
    pallas_call x1, Pallas kernels, backward(): pl.pallas_call(backward_kernel, grid=(4,), out_shape=[shape_of(3, BLK, 51...  13.4 us
    pallas_call x1, Pallas kernels, forward(): pl.pallas_call(forward_kernel, grid=(4,), out_shape=[shape_of(4, SEQ, SEQ...  12.8 us
    pallas_call x1, Pallas kernels, project_back(): pl.pallas_call(grad_out_kernel, grid=(4,), out_shape=shape_of(SEQ, 512),...  9.94 us
  transfers between devices with their start and end apart: 45, of which 21 were waited for; matrix products, arithmetic and copies ran while one was open for 4% of the time, Pallas kernels for 20%

profile of v1, /device:TPU:8, one launch (start us, length us, event | category | flops | bytes accessed | tf_op | source)
XLA Modules:
  0.0 302.6 jit_solution(17722397505332535755)
XLA Ops:
  10.1 2.8 collective-permute-done.19
  14.2 4.7 %pack.1 = (bf16[3,96,512]{2,1,0:T(8,128)(2,1)}, bf16[3,96,512]{2,1,0:T(8,128)(2,1)}, bf16[3,96,512]{2,1,0:T(8,128)(2,1)}, bf16[3,96,512]{2,1,0:T(8,128)(2,1)}, b...) custom-call(s32[5]{0:T(128)} %stack.50.idx, ...), custom_call_target="tpu_custom_call" | custom-call | bytes 9437184 | tf_op jit(solution)/shard_map/pack/pallas_call | solution.py:99
  33.4 3.3 %collective-permute-start.1 = (bf16[3,96,512]{2,1,0:T(8,128)(2,1)}, bf16[3,96,512]{2,1,0:T(8,128)(2,1)S(1)}, u32[]{:S(2)}, u32[]{:S(2)}) collective-permute-start(bf16[3,96,512]{2,1,0:T(8,128)(2,1)} %get-tuple-element.47), channel_id=1, source_target_pairs={{0,2},{1,3},{2,4},{3,5},{4,6},{5,7},{6,0},{7,1},{8,10},{9,11},{10,... | collective-permute-start | bytes 884744 | tf_op jit(solution)/shard_map/ppermute | solution.py:41
  36.7 2.8 collective-permute-done.13
  39.4 2.9 collective-permute-start.3
  43.6 10.8 %collective-permute-done.rest_1_ = bf16[3,96,512]{2,1,0:T(8,128)(2,1)S(1)} collective-permute-done((bf16[3,96,512]{2,1,0:T(8,128)(2,1)}, bf16[3,96,512]{2,1,0:T(8,128)(2,1)S(1)}, u32[]{:S(2)}, u32[]{:S(2)}) %collective-permute-start) | collective-permute-done | bytes 294944 | tf_op jit(solution)/shard_map/ppermute | solution.py:41
  54.4 3.7 %collective-permute-start.4 = (bf16[3,96,512]{2,1,0:T(8,128)(2,1)}, bf16[3,96,512]{2,1,0:T(8,128)(2,1)}, u32[]{:S(2)}, u32[]{:S(2)}) collective-permute-start(bf16[3,96,512]{2,1,0:T(8,128)(2,1)} %get-tuple-element.50), channel_id=1, source_target_pairs={{0,5},{1,4},{2,7},{3,6},{4,1},{5,0},{6,3},{7,2},{8,13},{9,12},{10,... | collective-permute-start | bytes 884744 | tf_op jit(solution)/shard_map/ppermute | solution.py:41
  59.4 11.2 %collective-permute-done.2.rest_3_ = bf16[3,96,512]{2,1,0:T(8,128)(2,1)S(1)} collective-permute-done((bf16[3,96,512]{2,1,0:T(8,128)(2,1)}, bf16[3,96,512]{2,1,0:T(8,128)(2,1)S(1)}, u32[]{:S(2)}, u32[]{:S(2)}) %collective-permute-start.2) | collective-permute-done | bytes 294944 | tf_op jit(solution)/shard_map/ppermute | solution.py:41
  70.6 5.6 %collective-permute-start.6 = (bf16[3,96,512]{2,1,0:T(8,128)(2,1)}, bf16[3,96,512]{2,1,0:T(8,128)(2,1)}, u32[]{:S(2)}, u32[]{:S(2)}) collective-permute-start(bf16[3,96,512]{2,1,0:T(8,128)(2,1)} %get-tuple-element.52), channel_id=1, source_target_pairs={{0,7},{1,6},{2,1},{3,0},{4,3},{5,2},{6,5},{7,4},{8,15},{9,14},{10,... | collective-permute-start | bytes 884744 | tf_op jit(solution)/shard_map/ppermute | solution.py:41
  80.7 2.9 join_text.1.refs_0_.refs_8_
  83.6 6.0 %collective-permute-done.4.rest_5_ = bf16[3,96,512]{2,1,0:T(8,128)(2,1)} collective-permute-done((bf16[3,96,512]{2,1,0:T(8,128)(2,1)}, bf16[3,96,512]{2,1,0:T(8,128)(2,1)}, u32[]{:S(2)}, u32[]{:S(2)}) %collective-permute-start.4) | collective-permute-done | bytes 294944 | tf_op jit(solution)/shard_map/ppermute | solution.py:41
  90.6 7.4 %collective-permute-done.6.rest_7_ = bf16[3,96,512]{2,1,0:T(8,128)(2,1)} collective-permute-done((bf16[3,96,512]{2,1,0:T(8,128)(2,1)}, bf16[3,96,512]{2,1,0:T(8,128)(2,1)}, u32[]{:S(2)}, u32[]{:S(2)}) %collective-permute-start.6) | collective-permute-done | bytes 294944 | tf_op jit(solution)/shard_map/ppermute | solution.py:41
  98.1 12.8 %forward.1 = (f32[4,896,896]{2,1,0:T(8,128)}, bf16[768,512]{1,0:T(8,128)(2,1)}, bf16[128,512]{1,0:T(8,128)(2,1)}) custom-call(s32[1]{0:T(128)} %dynamic_slice.77.length, f32[2,2,128]{2,1,0:T(2,128)} %gains.3, bf16[3,96,512]{2,1,0:T(8,128)(2,1)} %get-tuple-element.45.rest_0_, bf16[3,96,512]{2,1,0:T(8,128)(2,1)} %copy-done.17, bf16[3,96,512]{2,1,0:T(8,128)(2,1)} %copy-done.18, ...), custom_call_target="tpu_custom_call" | custom-call | flops 1644167168 | bytes 18874368 | tf_op jit(solution)/shard_map/forward/pallas_call | solution.py:242
  110.9 6.7 %weight_text.1 = (bf16[16,96,512]{2,1,0:T(8,128)(2,1)}, bf16[16,96,512]{2,1,0:T(8,128)(2,1)}) custom-call(s32[5]{0:T(128)} %stack.50.idx, bf16[128,512]{1,0:T(8,128)(2,1)} %get-tuple-element.59.att, bf16[128,3072]{1,0:T(8,128)(2,1)} %join_text.1.refs_0_.refs_8_), custom_call_target="tpu_custom_call" | custom-call | flops 402653184 | bytes 8388608 | tf_op jit(solution)/shard_map/weight_text/pallas_call | solution.py:380
  121.7 12.1 %collective-permute-done.10.refs_3_ = bf16[96,3072]{1,0:T(8,128)(2,1)S(1)} collective-permute-done((bf16[96,3072]{1,0:T(8,128)(2,1)S(1)}, bf16[96,3072]{1,0:T(8,128)(2,1)S(1)}, u32[]{:S(2)}, u32[]{:S(2)}) %collective-permute-start.10) | collective-permute-done | bytes 589856 | tf_op jit(solution)/shard_map/ppermute | solution.py:41
  133.9 9.0 %collective-permute-done.16.refs_4_ = bf16[96,3072]{1,0:T(8,128)(2,1)S(1)} collective-permute-done((bf16[96,3072]{1,0:T(8,128)(2,1)S(1)}, bf16[96,3072]{1,0:T(8,128)(2,1)S(1)}, u32[]{:S(2)}, u32[]{:S(2)}) %collective-permute-start.16) | collective-permute-done | bytes 589856 | tf_op jit(solution)/shard_map/ppermute | solution.py:41
  143.7 8.8 %weight_video.1 = (bf16[16,96,512]{2,1,0:T(8,128)(2,1)}, bf16[16,96,512]{2,1,0:T(8,128)(2,1)}) custom-call(s32[5]{0:T(128)} %stack.50.idx, bf16[768,512]{1,0:T(8,128)(2,1)} %get-tuple-element.66.att, bf16[96,3072]{1,0:T(8,128)(2,1)} %get-tuple-element.56.refs_0_, bf16[96,3072]{1,0:T(8,128)(2,1)} %copy-done.4, bf16[96,3072]{1,0:T(8,128)(2,1)} %copy-done.5, ...), custom_call_target="tpu_custom_call" | custom-call | flops 2415919104 | bytes 8388608 | tf_op jit(solution)/shard_map/weight_video/pallas_call | solution.py:380
  155.3 3.1 %collective-permute-start.37 = (bf16[4,96,512]{2,1,0:T(8,128)(2,1)S(1)}, bf16[4,96,512]{2,1,0:T(8,128)(2,1)S(1)}, u32[]{:S(2)}, u32[]{:S(2)}) collective-permute-start(bf16[4,96,512]{2,1,0:T(8,128)(2,1)S(1)} %get-tuple-element.86), channel_id=1, source_target_pairs={{0,32},{8,40},{16,48},{24,56},{32,0},{40,8},{48,16},{56,24},{64,96... | collective-permute-start | bytes 1179656 | tf_op jit(solution)/shard_map/ppermute | solution.py:54
  164.0 4.7 %collective-permute-done.37 = bf16[4,96,512]{2,1,0:T(8,128)(2,1)S(1)} collective-permute-done((bf16[4,96,512]{2,1,0:T(8,128)(2,1)S(1)}, bf16[4,96,512]{2,1,0:T(8,128)(2,1)S(1)}, u32[]{:S(2)}, u32[]{:S(2)}) %collective-permute-start.37) | collective-permute-done | bytes 393248 | tf_op jit(solution)/shard_map/ppermute | solution.py:54
  168.7 2.8 collective-permute-start.31
  171.6 5.7 %collective-permute-done.38 = bf16[4,96,512]{2,1,0:T(8,128)(2,1)} collective-permute-done((bf16[4,96,512]{2,1,0:T(8,128)(2,1)}, bf16[4,96,512]{2,1,0:T(8,128)(2,1)}, u32[]{:S(2)}, u32[]{:S(2)}) %collective-permute-start.38) | collective-permute-done | bytes 393248 | tf_op jit(solution)/shard_map/ppermute | solution.py:54
  177.4 8.2 %collective-permute-done.29 = bf16[4,96,512]{2,1,0:T(8,128)(2,1)S(1)} collective-permute-done((bf16[4,96,512]{2,1,0:T(8,128)(2,1)}, bf16[4,96,512]{2,1,0:T(8,128)(2,1)S(1)}, u32[]{:S(2)}, u32[]{:S(2)}) %collective-permute-start.29) | collective-permute-done | bytes 393248 | tf_op jit(solution)/shard_map/ppermute | solution.py:54
  185.6 7.9 %collective-permute-done.30 = bf16[4,96,512]{2,1,0:T(8,128)(2,1)S(1)} collective-permute-done((bf16[4,96,512]{2,1,0:T(8,128)(2,1)}, bf16[4,96,512]{2,1,0:T(8,128)(2,1)S(1)}, u32[]{:S(2)}, u32[]{:S(2)}) %collective-permute-start.30) | collective-permute-done | bytes 393248 | tf_op jit(solution)/shard_map/ppermute | solution.py:54
  196.0 16.8 %collective-permute-start.40 = (bf16[96,512]{1,0:T(8,128)(2,1)S(1)}, bf16[96,512]{1,0:T(8,128)(2,1)S(1)}, u32[]{:S(2)}, u32[]{:S(2)}) collective-permute-start(bf16[96,512]{1,0:T(8,128)(2,1)S(1)} %get-tuple-element.92), channel_id=1, source_target_pairs={{0,128},{8,136},{16,144},{24,152},{32,160},{40,168},{48,176},{56,1... | collective-permute-start | bytes 294920 | tf_op jit(solution)/shard_map/ppermute | solution.py:54
  219.4 9.9 %project_back.1.grad_out = bf16[896,512]{1,0:T(8,128)(2,1)} custom-call(bf16[96,3072]{1,0:T(8,128)(2,1)} %get-tuple-element.56.refs_0_, bf16[96,3072]{1,0:T(8,128)(2,1)} %copy-done.4, bf16[96,3072]{1,0:T(8,128)(2,1)} %copy-done.5, bf16[96,3072]{1,0:T(8,128)(2,1)} %copy-done.7, bf16[96,3072]{1,0:T(8,128)(2,1)} %copy-done.8, ...), custom_call_target="tpu_custom_call" | custom-call | flops 2818572288 | bytes 13631488 | tf_op jit(solution)/shard_map/project_back/pallas_call | solution.py:354
  229.3 13.4 %backward.1 = (bf16[3,96,512]{2,1,0:T(8,128)(2,1)}, bf16[3,96,512]{2,1,0:T(8,128)(2,1)}, bf16[3,96,512]{2,1,0:T(8,128)(2,1)}, bf16[3,96,512]{2,1,0:T(8,128)(2,1)...) custom-call(f32[2,2,128]{2,1,0:T(2,128)} %gains.3, ...), custom_call_target="tpu_custom_call" | custom-call | flops 3288334336 | bytes 20971520 | tf_op jit(solution)/shard_map/backward/pallas_call | solution.py:311
  242.8 2.9 collective-permute-start.34
  252.9 6.1 %collective-permute-done.43 = bf16[96,256]{1,0:T(8,128)(2,1)S(1)} collective-permute-done((bf16[96,256]{1,0:T(8,128)(2,1)S(1)}, bf16[96,256]{1,0:T(8,128)(2,1)S(1)}, u32[]{:S(2)}, u32[]{:S(2)}) %collective-permute-start.43) | collective-permute-done | bytes 49184 | tf_op jit(solution)/shard_map/ppermute | solution.py:41
  259.7 4.6 %collective-permute-done.35 = bf16[96,256]{1,0:T(8,128)(2,1)S(1)} collective-permute-done((bf16[96,256]{1,0:T(8,128)(2,1)S(1)}, bf16[96,256]{1,0:T(8,128)(2,1)S(1)}, u32[]{:S(2)}, u32[]{:S(2)}) %collective-permute-start.35) | collective-permute-done | bytes 49184 | tf_op jit(solution)/shard_map/ppermute | solution.py:41
  271.7 10.6 %collective-permute-done.23.rest_4_ = bf16[3,96,512]{2,1,0:T(8,128)(2,1)S(1)} collective-permute-done((bf16[3,96,512]{2,1,0:T(8,128)(2,1)}, bf16[3,96,512]{2,1,0:T(8,128)(2,1)S(1)}, u32[]{:S(2)}, u32[]{:S(2)}) %collective-permute-start.23) | collective-permute-done | bytes 294944 | tf_op jit(solution)/shard_map/ppermute | solution.py:41
  282.3 8.2 %collective-permute-done.25.rest_6_ = bf16[3,96,512]{2,1,0:T(8,128)(2,1)S(1)} collective-permute-done((bf16[3,96,512]{2,1,0:T(8,128)(2,1)}, bf16[3,96,512]{2,1,0:T(8,128)(2,1)S(1)}, u32[]{:S(2)}, u32[]{:S(2)}) %collective-permute-start.25) | collective-permute-done | bytes 294944 | tf_op jit(solution)/shard_map/ppermute | solution.py:41
  291.4 4.2 %unpack.1 = (bf16[2,3,96,2048]{3,2,1,0:T(8,128)(2,1)}, bf16[2,3,128,256]{3,2,1,0:T(8,128)(2,1)}) custom-call(s32[5]{0:T(128)} %stack.50.idx, bf16[3,96,512]{2,1,0:T(8,128)(2,1)} %get-tuple-element.70.rest_0_, bf16[3,96,512]{2,1,0:T(8,128)(2,1)} %copy-done.10, bf16[3,96,512]{2,1,0:T(8,128)(2,1)} %copy-done.11, bf16[3,96,512]{2,1,0:T(8,128)(2,1)} %copy-done.12, ...), custom_call_target="tpu_custom_call" | custom-call | bytes 6291456 | tf_op jit(solution)/shard_map/unpack/pallas_call | solution.py:141
  (134 shorter events, 65.2 us)
Async XLA Ops:
  7.2 212.2 %all-gather.3.cloned.1.call-start = ((), (), s32[]{:S(2)}) async-start(), calls=%async_computation | async-start | bytes 6488064 | tf_op jit(solution)/shard_map/all_gather | solution.py:433
  21.1 55.2 %collective-permute-start.8 = (bf16[96,3072]{1,0:T(8,128)(2,1)}, bf16[96,3072]{1,0:T(8,128)(2,1)S(1)}, u32[]{:S(2)}, u32[]{:S(2)}) collective-permute-start(bf16[96,3072]{1,0:T(8,128)(2,1)} %get-tuple-element.57), channel_id=1, source_target_pairs={{0,1},{1,0},{2,3},{3,2},{4,5},{5,4},{6,7},{7,6},{8,9},{9,8},{10,11... | collective-permute-start | bytes 1769480 | tf_op jit(solution)/shard_map/ppermute | solution.py:41
  30.3 24.1 %collective-permute-start = (bf16[3,96,512]{2,1,0:T(8,128)(2,1)}, bf16[3,96,512]{2,1,0:T(8,128)(2,1)S(1)}, u32[]{:S(2)}, u32[]{:S(2)}) collective-permute-start(bf16[3,96,512]{2,1,0:T(8,128)(2,1)} %get-tuple-element.46), channel_id=1, source_target_pairs={{0,1},{1,0},{2,3},{3,2},{4,5},{5,4},{6,7},{7,6},{8,9},{9,8},{10,11... | collective-permute-start | bytes 884744 | tf_op jit(solution)/shard_map/ppermute | solution.py:41
  33.4 24.6 %collective-permute-start.1 = (bf16[3,96,512]{2,1,0:T(8,128)(2,1)}, bf16[3,96,512]{2,1,0:T(8,128)(2,1)S(1)}, u32[]{:S(2)}, u32[]{:S(2)}) collective-permute-start(bf16[3,96,512]{2,1,0:T(8,128)(2,1)} %get-tuple-element.47), channel_id=1, source_target_pairs={{0,2},{1,3},{2,4},{3,5},{4,6},{5,7},{6,0},{7,1},{8,10},{9,11},{10,... | collective-permute-start | bytes 884744 | tf_op jit(solution)/shard_map/ppermute | solution.py:41
  39.4 31.2 %collective-permute-start.2 = (bf16[3,96,512]{2,1,0:T(8,128)(2,1)}, bf16[3,96,512]{2,1,0:T(8,128)(2,1)S(1)}, u32[]{:S(2)}, u32[]{:S(2)}) collective-permute-start(bf16[3,96,512]{2,1,0:T(8,128)(2,1)} %get-tuple-element.48), channel_id=1, source_target_pairs={{0,3},{1,2},{2,5},{3,4},{4,7},{5,6},{6,1},{7,0},{8,11},{9,10},{10,... | collective-permute-start | bytes 884744 | tf_op jit(solution)/shard_map/ppermute | solution.py:41
  39.4 36.8 %collective-permute-start.3 = (bf16[3,96,512]{2,1,0:T(8,128)(2,1)}, bf16[3,96,512]{2,1,0:T(8,128)(2,1)S(1)}, u32[]{:S(2)}, u32[]{:S(2)}) collective-permute-start(bf16[3,96,512]{2,1,0:T(8,128)(2,1)} %get-tuple-element.49), channel_id=1, source_target_pairs={{0,4},{1,5},{2,6},{3,7},{4,0},{5,1},{6,2},{7,3},{8,12},{9,13},{10,... | collective-permute-start | bytes 884744 | tf_op jit(solution)/shard_map/ppermute | solution.py:41
  54.4 35.2 %collective-permute-start.4 = (bf16[3,96,512]{2,1,0:T(8,128)(2,1)}, bf16[3,96,512]{2,1,0:T(8,128)(2,1)}, u32[]{:S(2)}, u32[]{:S(2)}) collective-permute-start(bf16[3,96,512]{2,1,0:T(8,128)(2,1)} %get-tuple-element.50), channel_id=1, source_target_pairs={{0,5},{1,4},{2,7},{3,6},{4,1},{5,0},{6,3},{7,2},{8,13},{9,12},{10,... | collective-permute-start | bytes 884744 | tf_op jit(solution)/shard_map/ppermute | solution.py:41
  58.1 32.6 %collective-permute-start.5 = (bf16[3,96,512]{2,1,0:T(8,128)(2,1)}, bf16[3,96,512]{2,1,0:T(8,128)(2,1)}, u32[]{:S(2)}, u32[]{:S(2)}) collective-permute-start(bf16[3,96,512]{2,1,0:T(8,128)(2,1)} %get-tuple-element.51), channel_id=1, source_target_pairs={{0,6},{1,7},{2,0},{3,1},{4,2},{5,3},{6,4},{7,5},{8,14},{9,15},{10,... | collective-permute-start | bytes 884744 | tf_op jit(solution)/shard_map/ppermute | solution.py:41
  70.6 27.4 %collective-permute-start.6 = (bf16[3,96,512]{2,1,0:T(8,128)(2,1)}, bf16[3,96,512]{2,1,0:T(8,128)(2,1)}, u32[]{:S(2)}, u32[]{:S(2)}) collective-permute-start(bf16[3,96,512]{2,1,0:T(8,128)(2,1)} %get-tuple-element.52), channel_id=1, source_target_pairs={{0,7},{1,6},{2,1},{3,0},{4,3},{5,2},{6,5},{7,4},{8,15},{9,14},{10,... | collective-permute-start | bytes 884744 | tf_op jit(solution)/shard_map/ppermute | solution.py:41
  76.3 42.6 %collective-permute-start.9 = (bf16[96,3072]{1,0:T(8,128)(2,1)}, bf16[96,3072]{1,0:T(8,128)(2,1)S(1)}, u32[]{:S(2)}, u32[]{:S(2)}) collective-permute-start(bf16[96,3072]{1,0:T(8,128)(2,1)} %get-tuple-element.56.refs_0_), channel_id=1, source_target_pairs={{0,2},{1,3},{2,4},{3,5},{4,6},{5,7},{6,0},{7,1},{8,10},{9,11},{10,... | collective-permute-start | bytes 1769480 | tf_op jit(solution)/shard_map/ppermute | solution.py:41
  76.3 42.6 %collective-permute-start.11 = (bf16[96,3072]{1,0:T(8,128)(2,1)S(1)}, bf16[96,3072]{1,0:T(8,128)(2,1)S(1)}, u32[]{:S(2)}, u32[]{:S(2)}) collective-permute-start(bf16[96,3072]{1,0:T(8,128)(2,1)S(1)} %collective-permute-done.8.refs_1_), channel_id=1, source_target_pairs={{0,6},{1,7},{2,0},{3,1},{4,2},{5,3},{6,4},{7,5},{8,14},{9,15},{10,... | collective-permute-start | bytes 1769480 | tf_op jit(solution)/shard_map/ppermute | solution.py:41
  89.6 32.2 %collective-permute-start.18 = (bf16[96,3072]{1,0:T(8,128)(2,1)S(1)}, bf16[96,3072]{1,0:T(8,128)(2,1)}, u32[]{:S(2)}, u32[]{:S(2)}) collective-permute-start(bf16[96,3072]{1,0:T(8,128)(2,1)S(1)} %copy-done.3), channel_id=1, source_target_pairs={{0,6},{1,7},{2,0},{3,1},{4,2},{5,3},{6,4},{7,5},{8,14},{9,15},{10,... | collective-permute-start | bytes 1769480 | tf_op jit(solution)/shard_map/ppermute | solution.py:41
  117.6 16.3 %collective-permute-start.10 = (bf16[96,3072]{1,0:T(8,128)(2,1)S(1)}, bf16[96,3072]{1,0:T(8,128)(2,1)S(1)}, u32[]{:S(2)}, u32[]{:S(2)}) collective-permute-start(bf16[96,3072]{1,0:T(8,128)(2,1)S(1)} %collective-permute-done.8.refs_1_), channel_id=1, source_target_pairs={{0,2},{1,3},{2,4},{3,5},{4,6},{5,7},{6,0},{7,1},{8,10},{9,11},{10,... | collective-permute-start | bytes 1769480 | tf_op jit(solution)/shard_map/ppermute | solution.py:41
  119.7 23.2 %collective-permute-start.16 = (bf16[96,3072]{1,0:T(8,128)(2,1)S(1)}, bf16[96,3072]{1,0:T(8,128)(2,1)S(1)}, u32[]{:S(2)}, u32[]{:S(2)}) collective-permute-start(bf16[96,3072]{1,0:T(8,128)(2,1)S(1)} %collective-permute-done.9.refs_2_), channel_id=1, source_target_pairs={{0,2},{1,3},{2,4},{3,5},{4,6},{5,7},{6,0},{7,1},{8,10},{9,11},{10,... | collective-permute-start | bytes 1769480 | tf_op jit(solution)/shard_map/ppermute | solution.py:41
  119.9 23.8 %collective-permute-start.17 = (bf16[96,3072]{1,0:T(8,128)(2,1)}, bf16[96,3072]{1,0:T(8,128)(2,1)}, u32[]{:S(2)}, u32[]{:S(2)}) collective-permute-start(bf16[96,3072]{1,0:T(8,128)(2,1)} %copy-done.6), channel_id=1, source_target_pairs={{0,6},{1,7},{2,0},{3,1},{4,2},{5,3},{6,4},{7,5},{8,14},{9,15},{10,... | collective-permute-start | bytes 1769480 | tf_op jit(solution)/shard_map/ppermute | solution.py:41
  121.7 30.9 %collective-permute-start.36 = (bf16[16,96,512]{2,1,0:T(8,128)(2,1)}, bf16[16,96,512]{2,1,0:T(8,128)(2,1)}, u32[]{:S(2)}, u32[]{:S(2)}) collective-permute-start(bf16[16,96,512]{2,1,0:T(8,128)(2,1)} %get-tuple-element.85), channel_id=1, source_target_pairs={{0,8},{8,0},{16,24},{24,16},{32,40},{40,32},{48,56},{56,48},{64,72... | collective-permute-start | bytes 4718600 | tf_op jit(solution)/shard_map/ppermute | solution.py:54
  158.3 19.0 %collective-permute-start.38 = (bf16[4,96,512]{2,1,0:T(8,128)(2,1)}, bf16[4,96,512]{2,1,0:T(8,128)(2,1)}, u32[]{:S(2)}, u32[]{:S(2)}) collective-permute-start(bf16[4,96,512]{2,1,0:T(8,128)(2,1)} %get-tuple-element.87), channel_id=1, source_target_pairs={{0,16},{8,24},{16,32},{24,40},{32,48},{40,56},{48,0},{56,8},{64,80... | collective-permute-start | bytes 1179656 | tf_op jit(solution)/shard_map/ppermute | solution.py:54
  158.9 18.5 %collective-permute-start.39 = (bf16[4,96,512]{2,1,0:T(8,128)(2,1)}, bf16[4,96,512]{2,1,0:T(8,128)(2,1)}, u32[]{:S(2)}, u32[]{:S(2)}) collective-permute-start(bf16[4,96,512]{2,1,0:T(8,128)(2,1)} %get-tuple-element.88), channel_id=1, source_target_pairs={{0,48},{8,56},{16,0},{24,8},{32,16},{40,24},{48,32},{56,40},{64,11... | collective-permute-start | bytes 1179656 | tf_op jit(solution)/shard_map/ppermute | solution.py:54
  163.2 22.5 %collective-permute-start.29 = (bf16[4,96,512]{2,1,0:T(8,128)(2,1)}, bf16[4,96,512]{2,1,0:T(8,128)(2,1)S(1)}, u32[]{:S(2)}, u32[]{:S(2)}) collective-permute-start(bf16[4,96,512]{2,1,0:T(8,128)(2,1)} %get-tuple-element.89), channel_id=1, source_target_pairs={{0,32},{8,40},{16,48},{24,56},{32,0},{40,8},{48,16},{56,24},{64,96... | collective-permute-start | bytes 1179656 | tf_op jit(solution)/shard_map/ppermute | solution.py:54
  163.2 30.3 %collective-permute-start.30 = (bf16[4,96,512]{2,1,0:T(8,128)(2,1)}, bf16[4,96,512]{2,1,0:T(8,128)(2,1)S(1)}, u32[]{:S(2)}, u32[]{:S(2)}) collective-permute-start(bf16[4,96,512]{2,1,0:T(8,128)(2,1)} %get-tuple-element.90), channel_id=1, source_target_pairs={{0,16},{8,24},{16,32},{24,40},{32,48},{40,56},{48,0},{56,8},{64,80... | collective-permute-start | bytes 1179656 | tf_op jit(solution)/shard_map/ppermute | solution.py:54
  168.7 25.1 %collective-permute-start.31 = (bf16[4,96,512]{2,1,0:T(8,128)(2,1)}, bf16[4,96,512]{2,1,0:T(8,128)(2,1)}, u32[]{:S(2)}, u32[]{:S(2)}) collective-permute-start(bf16[4,96,512]{2,1,0:T(8,128)(2,1)} %get-tuple-element.91), channel_id=1, source_target_pairs={{0,48},{8,56},{16,0},{24,8},{32,16},{40,24},{48,32},{56,40},{64,11... | collective-permute-start | bytes 1179656 | tf_op jit(solution)/shard_map/ppermute | solution.py:54
  196.0 46.8 %collective-permute-start.40 = (bf16[96,512]{1,0:T(8,128)(2,1)S(1)}, bf16[96,512]{1,0:T(8,128)(2,1)S(1)}, u32[]{:S(2)}, u32[]{:S(2)}) collective-permute-start(bf16[96,512]{1,0:T(8,128)(2,1)S(1)} %get-tuple-element.92), channel_id=1, source_target_pairs={{0,128},{8,136},{16,144},{24,152},{32,160},{40,168},{48,176},{56,1... | collective-permute-start | bytes 294920 | tf_op jit(solution)/shard_map/ppermute | solution.py:54
  212.8 32.9 %collective-permute-start.41 = (bf16[96,512]{1,0:T(8,128)(2,1)S(1)}, bf16[96,512]{1,0:T(8,128)(2,1)S(1)}, u32[]{:S(2)}, u32[]{:S(2)}) collective-permute-start(bf16[96,512]{1,0:T(8,128)(2,1)S(1)} %get-tuple-element.94), channel_id=1, source_target_pairs={{0,64},{8,72},{16,80},{24,88},{32,96},{40,104},{48,112},{56,120},{... | collective-permute-start | bytes 294920 | tf_op jit(solution)/shard_map/ppermute | solution.py:54
  214.4 32.2 %collective-permute-start.42 = (bf16[96,512]{1,0:T(8,128)(2,1)S(1)}, bf16[96,512]{1,0:T(8,128)(2,1)S(1)}, u32[]{:S(2)}, u32[]{:S(2)}) collective-permute-start(bf16[96,512]{1,0:T(8,128)(2,1)S(1)} %get-tuple-element.93), channel_id=1, source_target_pairs={{0,192},{8,200},{16,208},{24,216},{32,224},{40,232},{48,240},{56,2... | collective-permute-start | bytes 294920 | tf_op jit(solution)/shard_map/ppermute | solution.py:54
  216.9 31.4 %collective-permute-start.32 = (bf16[96,512]{1,0:T(8,128)(2,1)S(1)}, bf16[96,512]{1,0:T(8,128)(2,1)S(1)}, u32[]{:S(2)}, u32[]{:S(2)}) collective-permute-start(bf16[96,512]{1,0:T(8,128)(2,1)S(1)} %get-tuple-element.95), channel_id=1, source_target_pairs={{0,128},{8,136},{16,144},{24,152},{32,160},{40,168},{48,176},{56,1... | collective-permute-start | bytes 294920 | tf_op jit(solution)/shard_map/ppermute | solution.py:54
  218.1 31.4 %collective-permute-start.33 = (bf16[96,512]{1,0:T(8,128)(2,1)S(1)}, bf16[96,512]{1,0:T(8,128)(2,1)S(1)}, u32[]{:S(2)}, u32[]{:S(2)}) collective-permute-start(bf16[96,512]{1,0:T(8,128)(2,1)S(1)} %get-tuple-element.97), channel_id=1, source_target_pairs={{0,64},{8,72},{16,80},{24,88},{32,96},{40,104},{48,112},{56,120},{... | collective-permute-start | bytes 294920 | tf_op jit(solution)/shard_map/ppermute | solution.py:54
  245.7 21.1 %collective-permute-start.20 = (bf16[3,96,512]{2,1,0:T(8,128)(2,1)}, bf16[3,96,512]{2,1,0:T(8,128)(2,1)S(1)}, u32[]{:S(2)}, u32[]{:S(2)}) collective-permute-start(bf16[3,96,512]{2,1,0:T(8,128)(2,1)} %get-tuple-element.71), channel_id=1, source_target_pairs={{0,1},{1,0},{2,3},{3,2},{4,5},{5,4},{6,7},{7,6},{8,9},{9,8},{10,11... | collective-permute-start | bytes 884744 | tf_op jit(solution)/shard_map/ppermute | solution.py:41
  246.6 21.5 %collective-permute-start.21 = (bf16[3,96,512]{2,1,0:T(8,128)(2,1)}, bf16[3,96,512]{2,1,0:T(8,128)(2,1)S(1)}, u32[]{:S(2)}, u32[]{:S(2)}) collective-permute-start(bf16[3,96,512]{2,1,0:T(8,128)(2,1)} %get-tuple-element.72), channel_id=1, source_target_pairs={{0,6},{1,7},{2,0},{3,1},{4,2},{5,3},{6,4},{7,5},{8,14},{9,15},{10,... | collective-permute-start | bytes 884744 | tf_op jit(solution)/shard_map/ppermute | solution.py:41
  264.3 18.0 %collective-permute-start.23 = (bf16[3,96,512]{2,1,0:T(8,128)(2,1)}, bf16[3,96,512]{2,1,0:T(8,128)(2,1)S(1)}, u32[]{:S(2)}, u32[]{:S(2)}) collective-permute-start(bf16[3,96,512]{2,1,0:T(8,128)(2,1)} %get-tuple-element.74), channel_id=1, source_target_pairs={{0,4},{1,5},{2,6},{3,7},{4,0},{5,1},{6,2},{7,3},{8,12},{9,13},{10,... | collective-permute-start | bytes 884744 | tf_op jit(solution)/shard_map/ppermute | solution.py:41
  265.3 17.0 %collective-permute-start.24 = (bf16[3,96,512]{2,1,0:T(8,128)(2,1)}, bf16[3,96,512]{2,1,0:T(8,128)(2,1)S(1)}, u32[]{:S(2)}, u32[]{:S(2)}) collective-permute-start(bf16[3,96,512]{2,1,0:T(8,128)(2,1)} %get-tuple-element.75), channel_id=1, source_target_pairs={{0,5},{1,4},{2,7},{3,6},{4,1},{5,0},{6,3},{7,2},{8,13},{9,12},{10,... | collective-permute-start | bytes 884744 | tf_op jit(solution)/shard_map/ppermute | solution.py:41
  266.8 23.7 %collective-permute-start.25 = (bf16[3,96,512]{2,1,0:T(8,128)(2,1)}, bf16[3,96,512]{2,1,0:T(8,128)(2,1)S(1)}, u32[]{:S(2)}, u32[]{:S(2)}) collective-permute-start(bf16[3,96,512]{2,1,0:T(8,128)(2,1)} %get-tuple-element.76), channel_id=1, source_target_pairs={{0,2},{1,3},{2,4},{3,5},{4,6},{5,7},{6,0},{7,1},{8,10},{9,11},{10,... | collective-permute-start | bytes 884744 | tf_op jit(solution)/shard_map/ppermute | solution.py:41
  268.1 22.5 %collective-permute-start.26 = (bf16[3,96,512]{2,1,0:T(8,128)(2,1)}, bf16[3,96,512]{2,1,0:T(8,128)(2,1)S(1)}, u32[]{:S(2)}, u32[]{:S(2)}) collective-permute-start(bf16[3,96,512]{2,1,0:T(8,128)(2,1)} %get-tuple-element.77), channel_id=1, source_target_pairs={{0,3},{1,2},{2,5},{3,4},{4,7},{5,6},{6,1},{7,0},{8,11},{9,10},{10,... | collective-permute-start | bytes 884744 | tf_op jit(solution)/shard_map/ppermute | solution.py:41
  (37 other events, 710.0 us)
Sparse Core Ops, SparseCore 0:
  13.7 86.6 all-gather.2

commit v2 on v1

v2 whole, which is shorter than its diff:
```python
import functools

import jax
import jax.numpy as jnp
from jax import lax
from jax.experimental import pallas as pl
from jax.experimental.pallas import tpu as pltpu
from jax.sharding import PartitionSpec as P

DH = 128
VID = 768
TXT = 128
SEQ = VID + TXT
BLK = 96
BF = jnp.bfloat16
F32 = jnp.float32
SCALE = DH ** (-0.5)
RELS = [(dy, dz) for dy in range(4) for dz in range(2)]
ANY = pl.BlockSpec(memory_space=pl.ANY)
SMEM = pl.BlockSpec(memory_space=pltpu.SMEM)
MB = 1024 * 1024


def shape_of(*dims, dtype=BF):
    return jax.ShapeDtypeStruct(dims, dtype)


def params(mb):
    return pltpu.CompilerParams(vmem_limit_bytes=mb * MB)


def cost(flops, nbytes, exps=0):
    return pl.CostEstimate(
        flops=flops // 1000, bytes_accessed=nbytes // 1000, transcendentals=exps // 1000
    )


def sp_perm(dy, dz):
    return [(y * 2 + z, ((y + dy) % 4) * 2 + (z + dz) % 2) for y in range(4) for z in range(2)]


def send_sp(value, dy, dz):
    return lax.ppermute(value, "sp", sp_perm(dy, dz))


def dp_perm(dh, dx, dc):
    return [
        ((h * 4 + x) * 2 + c, (((h + dh) % 4) * 4 + (x + dx) % 4) * 2 + (c + dc) % 2)
        for h in range(4)
        for x in range(4)
        for c in range(2)
    ]


def send_dp(value, dh, dx, dc):
    return lax.ppermute(value, "dp", dp_perm(dh, dx, dc))


def place_of(idx, k):
    dy, dz = RELS[k]
    return lax.rem(idx[0] + 4 - dy, 4) * 2 + lax.rem(idx[1] + dz, 2)


def head_pieces():
    for s in range(8):
        y, z = s // 2, s % 2
        for half in range(2):
            yield s, z, half, pl.ds(y * 512 + (z + half) % 2 * 256, 256)


def fold_text(wide):
    tail = [wide[BLK:, n * 128 : n * 128 + 128] for n in range(3)]
    return jnp.concatenate([wide[:BLK], jnp.concatenate(tail, axis=0)], axis=1)


def unfold_text(slab):
    tail = [slab[32 * n : 32 * n + 32, 384:] for n in range(3)]
    return jnp.concatenate([slab[:, :384], jnp.concatenate(tail, axis=1)], axis=0)


def pack_kernel(idx, qkv, qt, ct, *rest):
    out, own, other, held_qkv, held_qt, held_ct, slabs, sem_in, sem_out = rest
    zl = idx[1]
    ins = [
        pltpu.make_async_copy(source, place, sem_in.at[n])
        for n, (source, place) in enumerate(((ct, held_ct), (qt, held_qt), (qkv, held_qkv)))
    ]
    for copy in ins:
        copy.start()
    outs = []

    def leave(source, target):
        copy = pltpu.make_async_copy(source, target, sem_out.at[len(outs)])
        copy.start()
        outs.append(copy)

    ins[0].wait()
    for clip in range(2):
        slabs[clip] = fold_text(held_ct[clip])
    for s in range(8):
        leave(slabs.at[s % 2], out.at[s, 3])
    ins[1].wait()
    leave(held_qt.at[zl], own)
    leave(held_qt.at[1 - zl], other)
    ins[2].wait()
    for s, clip, half, cols in head_pieces():
        leave(
            held_qkv.at[clip, :, :, cols],
            out.at[s, pl.ds(0, 3), :, pl.ds(256 * half, 256)],
        )
    for copy in outs:
        copy.wait()


def pack(idx, qkv, qt, ct):
    return pl.pallas_call(
        pack_kernel,
        out_shape=[shape_of(8, 4, BLK, 512)] + [shape_of(3, TXT, 256)] * 2,
        in_specs=[SMEM, ANY, ANY, ANY],
        out_specs=[ANY] * 3,
        scratch_shapes=[pltpu.VMEM(v.shape, BF) for v in (qkv, qt, ct)]
        + [pltpu.VMEM((2, BLK, 512), BF)]
        + [pltpu.SemaphoreType.DMA((3,)), pltpu.SemaphoreType.DMA((26,))],
        compiler_params=params(60),
        cost_estimate=cost(0, 8 * MB),
        name="pack",
    )(idx, qkv, qt, ct)


def unpack_kernel(idx, chunks, own, other, *rest):
    out_video, out_text, video, text, sem = rest
    zl = idx[1]
    copies = []

    def enter(source, target):
        copy = pltpu.make_async_copy(source, target, sem.at[len(copies)])
        copy.start()
        copies.append(copy)

    for s, clip, half, cols in head_pieces():
        enter(chunks.at[s, :, :, pl.ds(256 * half, 256)], video.at[clip, :, :, cols])
    enter(own, text.at[zl])
    enter(other, text.at[1 - zl])
    for copy in copies:
        copy.wait()
    copies = [
        pltpu.make_async_copy(video, out_video, sem.at[0]),
        pltpu.make_async_copy(text, out_text, sem.at[1]),
    ]
    for copy in copies:
        copy.start()
    for copy in copies:
        copy.wait()


def unpack(idx, chunks, own, other):
    outs = [shape_of(2, 3, BLK, 2048), shape_of(2, 3, TXT, 256)]
    return pl.pallas_call(
        unpack_kernel,
        out_shape=outs,
        in_specs=[SMEM, ANY, ANY, ANY],
        out_specs=[ANY] * 2,
        scratch_shapes=[pltpu.VMEM(v.shape, BF) for v in outs]
        + [pltpu.SemaphoreType.DMA((18,))],
        compiler_params=params(60),
        cost_estimate=cost(0, 6 * MB),
        name="unpack",
    )(idx, chunks, own, other)


def normed_rows(raw, gain):
    wide = raw.astype(F32)
    inverse = lax.rsqrt(jnp.mean(wide * wide, axis=-1, keepdims=True) + 1e-6)
    unit = wide * inverse
    return unit, inverse, (unit * gain).astype(BF)


def joint_rows(idx, chunks, text, part):
    return jnp.concatenate([chunks[place_of(idx, k), part] for k in range(8)], axis=0), text[part]


def dot(a, b, dims):
    return lax.dot_general(a, b, (dims, ((), ())), preferred_element_type=F32)


NN = ((1,), (0,))
NT = ((1,), (1,))
TN = ((0,), (0,))


def forward_kernel(idx, length, gains, chunks, own, other, prob_out, att_video, att_text):
    text = jnp.where(pl.program_id(0) < 2, own[...], other[...])
    normed = []
    for part in range(2):
        video_raw, text_raw = joint_rows(idx, chunks, text, part)
        normed.append(
            jnp.concatenate(
                [
                    normed_rows(video_raw, gains[0, part : part + 1])[2],
                    normed_rows(text_raw, gains[1, part : part + 1])[2],
                ],
                axis=0,
            )
        )
    values = jnp.concatenate(joint_rows(idx, chunks, text, 2), axis=0)
    scores = dot(normed[0], normed[1], NT) * SCALE
    seen = lax.broadcasted_iota(jnp.int32, (SEQ, TXT), 1) < length[0]
    scores = jnp.concatenate(
        [scores[:, :VID], jnp.where(seen, scores[:, VID:], -1e30)], axis=1
    )
    powers = jnp.exp(scores - jnp.max(scores, axis=-1, keepdims=True))
    prob = powers * (1.0 / jnp.sum(powers, axis=-1, keepdims=True))
    prob_out[0] = prob
    attended = dot(prob.astype(BF), values, NN).astype(BF)
    att_video[...] = attended[:VID]
    att_text[...] = attended[VID:]


CHUNK = pl.BlockSpec((8, 3, BLK, DH), lambda h: (0, 0, 0, h))
FIRST = pl.BlockSpec((3, TXT, DH), lambda h: (0, 0, jnp.minimum(h, 1)))
LATER = pl.BlockSpec((3, TXT, DH), lambda h: (0, 0, jnp.maximum(h - 2, 0)))
GAINS = pl.BlockSpec((2, 2, DH), lambda h: (0, 0, 0))
PROB = pl.BlockSpec((1, SEQ, SEQ), lambda h: (h, 0, 0))


def forward(idx, length, gains, chunks, own, other):
    return pl.pallas_call(
        forward_kernel,
        grid=(4,),
        out_shape=[shape_of(4, SEQ, SEQ, dtype=F32), shape_of(VID, 512), shape_of(TXT, 512)],
        in_specs=[SMEM, SMEM, GAINS, CHUNK, FIRST, LATER],
        out_specs=[
            PROB,
            pl.BlockSpec((VID, DH), lambda h: (0, h)),
            pl.BlockSpec((TXT, DH), lambda h: (0, h)),
        ],
        compiler_params=params(60),
        cost_estimate=cost(4 * 4 * SEQ * SEQ * DH, 18 * MB, 4 * SEQ * SEQ),
        name="forward",
    )(idx, length, gains, chunks, own, other)


def norm_back(unit, inverse, gain, incoming):
    scaled = incoming * gain
    return inverse * (scaled - unit * jnp.mean(scaled * unit, axis=-1, keepdims=True))


def backward_kernel(
    idx, gains, prob_ref, grad_out, chunks, own, other, outs, out_own, out_other
):
    head = pl.program_id(0)
    text = jnp.where(head < 2, own[...], other[...])
    units = []
    normed = []
    for part in range(2):
        video_raw, text_raw = joint_rows(idx, chunks, text, part)
        v = normed_rows(video_raw, gains[0, part : part + 1])
        t = normed_rows(text_raw, gains[1, part : part + 1])
        units.append((v, t))
        normed.append(jnp.concatenate([v[2], t[2]], axis=0))
    values = jnp.concatenate(joint_rows(idx, chunks, text, 2), axis=0)
    prob = prob_ref[0]
    rows = grad_out[...]
    grad_prob = dot(rows, values, NT)
    inner = jnp.sum(prob * grad_prob, axis=-1, keepdims=True)
    low = (prob * (grad_prob - inner) * SCALE).astype(BF)
    grad_q = dot(low, normed[1], NN)
    grad_k = dot(normed[0], low, TN).T
    grad_v = dot(rows, prob.astype(BF), TN).T
    results = []
    for part, grad in enumerate((grad_q, grad_k)):
        v, t = units[part]
        results.append(
            (
                norm_back(v[0], v[1], gains[0, part : part + 1], grad[:VID]).astype(BF),
                norm_back(t[0], t[1], gains[1, part : part + 1], grad[VID:]).astype(BF),
            )
        )
    results.append((grad_v[:VID].astype(BF), grad_v[VID:].astype(BF)))
    for part in range(3):
        for k in range(8):
            outs[place_of(idx, k), part] = results[part][0][k * BLK : (k + 1) * BLK]

    @pl.when(head < 2)
    def _():
        for part in range(3):
            out_own[part] = results[part][1]

    @pl.when(head >= 2)
    def _():
        for part in range(3):
            out_other[part] = results[part][1]


def backward(idx, gains, prob, grad_out, chunks, own, other):
    return pl.pallas_call(
        backward_kernel,
        grid=(4,),
        out_shape=[shape_of(8, 3, BLK, 512)] + [shape_of(3, TXT, 256)] * 2,
        in_specs=[SMEM, GAINS, PROB, pl.BlockSpec((SEQ, DH), lambda h: (0, h))]
        + [CHUNK, FIRST, LATER],
        out_specs=[CHUNK, FIRST, LATER],
        compiler_params=params(60),
        cost_estimate=cost(4 * 8 * SEQ * SEQ * DH, 20 * MB),
        name="backward",
    )(idx, gains, prob, grad_out, chunks, own, other)


def grad_out_kernel(idx, *refs):
    cots, cot_text, mine, theirs, out, acc = refs[:8], *refs[8:]
    step = pl.program_id(0)
    video = jnp.concatenate([c[...] for c in cots], axis=0)
    text = jnp.concatenate([unfold_text(cot_text[n]) for n in range(2)], axis=1)

    def add(core_0, core_1):
        for half in range(2):
            cols = slice(256 * half, 256 * half + 256)
            for stream, rows, left in ((0, slice(0, VID), video), (1, slice(VID, SEQ), text)):
                weight = jnp.stack(
                    [core_0[:, half, stream], core_1[:, half, stream]], axis=1
                ).reshape(768, 256)
                part = dot(left, weight, NN)
                acc[rows, cols] = jnp.where(step == 0, part, acc[rows, cols] + part)

    @pl.when(idx[2] == 0)
    def _():
        add(mine, theirs)

    @pl.when(idx[2] == 1)
    def _():
        add(theirs, mine)

    @pl.when(step == 3)
    def _():
        out[...] = acc[...].astype(BF)


def project_back(idx, cots, cot_text, mine, theirs):
    weight = pl.BlockSpec((4, 2, 2, BLK, 256), lambda i: (i, 0, 0, 0, 0))
    return pl.pallas_call(
        grad_out_kernel,
        grid=(4,),
        in_specs=[SMEM]
        + [pl.BlockSpec((BLK, 768), lambda i: (0, i))] * 8
        + [pl.BlockSpec((2, None, BLK, 512), lambda i: (i, 3, 0, 0))]
        + [weight, weight],
        out_specs=pl.BlockSpec((SEQ, 512), lambda i: (0, 0)),
        scratch_shapes=[pltpu.VMEM((SEQ, 512), F32)],
        out_shape=shape_of(SEQ, 512),
        compiler_params=params(60),
        cost_estimate=cost(2 * SEQ * 512 * 3072, 13 * MB),
        name="project_back",
    )(idx, *cots, cot_text, mine, theirs)


def weight_grad_kernel(idx, att, *refs):
    cots, keep, send = refs[:-2], refs[-2], refs[-1]
    if len(cots) > 1:
        cot = jnp.concatenate([c[...] for c in cots], axis=0)
    else:
        cot = unfold_text(cots[0][...])
    part = dot(cot, att[...], TN).reshape(2, 2, BLK, 512)
    first = idx[2] == 0
    keep[...] = jnp.where(first, part[:, 0], part[:, 1]).astype(BF)
    send[...] = jnp.where(first, part[:, 1], part[:, 0]).astype(BF)


def weight_grad(idx, att, cots, name):
    rows = att.shape[0]
    out = pl.BlockSpec((2, BLK, 512), lambda i: (i, 0, 0))
    if len(cots) > 1:
        specs = [pl.BlockSpec((BLK, 384), lambda i: (0, i))] * len(cots)
    else:
        specs = [pl.BlockSpec((None, None, BLK, 512), lambda i: (i, 3, 0, 0))]
    return pl.pallas_call(
        weight_grad_kernel,
        grid=(8,),
        out_shape=[shape_of(16, BLK, 512)] * 2,
        in_specs=[SMEM, pl.BlockSpec((rows, 512), lambda i: (0, 0))] + specs,
        out_specs=[out, out],
        compiler_params=params(60),
        cost_estimate=cost(2 * rows * 512 * 3072, 8 * MB),
        name=name,
    )(idx, att, *cots)


def wide_sum(parts):
    return functools.reduce(jnp.add, [p.astype(F32) for p in parts])


def sum_cores(idx, keep, got):
    keep = keep.reshape(4, 4, BLK, 512)
    got = got.reshape(4, 4, BLK, 512)

    def share(step):
        at = lax.rem(idx[4] + step, 4)
        return wide_sum(
            [lax.dynamic_index_in_dim(v, at, axis=1, keepdims=False) for v in (keep, got)]
        )

    return [share(step).astype(BF) for step in range(4)]


def send_x(shares, steps):
    return [send_dp(shares[step], 0, step, 0) for step in steps]


def sum_far_and_near(idx, totals):
    zh = idx[3]

    def slab(step):
        at = lax.rem(zh + step, 4)
        return jnp.stack(
            [lax.dynamic_index_in_dim(t, at, axis=0, keepdims=False) for t in totals]
        )

    arrived = [send_dp(slab(step), step, 0, 0) for step in (2, 1, 3)]
    total = wide_sum([slab(0)] + arrived)
    last = send_sp(total[:, :, 256:].astype(BF), 0, 1)
    total = wide_sum([total[:, :, :256], last])
    return [total[n].T for n in range(2)]


def body(qkv_video, qkv_text, qk_gains, text_len, w_out_video, w_out_text, cot_video, cot_text):
    sp, dp = lax.axis_index("sp"), lax.axis_index("dp")
    y, zl = sp // 2, sp % 2
    idx = jnp.stack([y, zl, dp % 2, dp // 8, (dp // 2) % 4]).astype(jnp.int32)
    length = lax.dynamic_slice(text_len, (zl,), (1,))

    after = lax.optimization_barrier

    def of_clip(array, clip):
        return lax.dynamic_index_in_dim(array, clip, axis=0, keepdims=False)

    cot_own = of_clip(cot_video, zl)
    cot_send = of_clip(cot_video, 1 - zl)
    w_own = jnp.stack([w_out_video.T, w_out_text.T])
    cot_own, cot_send, w_own = after((cot_own, cot_send, w_own))

    near = [cot_own, send_sp(cot_send, 0, 1)]
    below, above = [send_sp(cot_own, 1, 0)], [send_sp(cot_own, 3, 0)]
    w_pair = jnp.stack([w_own, send_sp(w_own, 0, 1)])
    packed = pack(idx, qkv_video, qkv_text, cot_text)
    near, below, above, packed, w_pair = after((near, below, above, packed, w_pair))

    weights = lax.all_gather(
        w_pair,
        "dp",
        axis=0,
        axis_index_groups=[[2 * n + core for n in range(16)] for core in range(2)],
    )
    below = below + [send_sp(near[1], 1, 0)]
    above = above + [send_sp(near[1], 3, 0)]
    sent, text_own, text_send = packed
    text_other = send_sp(text_send, 0, 1)
    chunks = lax.all_to_all(sent, "sp", 0, 0, tiled=True)
    below, above, chunks, text_other = after((below, above, chunks, text_other))

    far = [send_sp(below[0], 1, 0), send_sp(above[1], 3, 0)]
    prob, att_video, att_text = forward(
        idx, length, qk_gains, chunks, text_own, text_other
    )
    att_video, att_text, far = after((att_video, att_text, far))

    cots = near + below + far + above

    text_keep, text_give = weight_grad(idx, att_text, [chunks], "weight_text")
    text_keep, text_give, weights = after((text_keep, text_give, weights))

    other_weights = send_dp(weights, 0, 0, 1)
    text_got = send_dp(text_give, 0, 0, 1)
    keep, give = weight_grad(idx, att_video, cots, "weight_video")
    text_got, keep, give, other_weights = after((text_got, keep, give, other_weights))

    text_shares = sum_cores(idx, text_keep, text_got)
    text_shares, give, cots = after((text_shares, give, cots))

    text_near = send_x(text_shares, (1, 3))
    got = send_dp(give, 0, 0, 1)
    grad_out = project_back(idx, cots, chunks, weights, other_weights)
    text_near, got, keep, grad_out = after((text_near, got, keep, grad_out))

    shares = sum_cores(idx, keep, got)
    shares, text_shares, grad_out = after((shares, text_shares, grad_out))

    near_sums = send_x(shares, (1, 3))
    text_far = send_x(text_shares, (2,))
    grads, own, other = backward(
        idx, qk_gains, prob, grad_out, chunks, text_own, text_other
    )
    near_sums, text_far, grads, other, shares = after(
        (near_sums, text_far, grads, other, shares)
    )

    far_sums = send_x(shares, (2,))
    grads = lax.all_to_all(grads, "sp", 0, 0, tiled=True)
    other = send_sp(other, 0, 1)
    text_total = wide_sum([text_shares[0]] + text_near + text_far).astype(BF)
    video_total = wide_sum([shares[0]] + near_sums + far_sums).astype(BF)
    grad_w_text, grad_w_video = sum_far_and_near(idx, (text_total, video_total))
    grad_qkv_video, grad_qkv_text = unpack(idx, grads, own, other)
    return (grad_qkv_video, grad_qkv_text, grad_w_video, grad_w_text)


def solution(mesh):
    return jax.shard_map(
        body,
        mesh=mesh,
        in_specs=(
            P("dp", None, "sp", None),
            P("dp", None, None, "sp"),
            P(),
            P("dp"),
            P("sp", "dp"),
            P("sp", "dp"),
            P("dp", "sp", None),
            P("dp", None, "sp"),
        ),
        out_specs=(
            P("dp", None, "sp", None),
            P("dp", None, None, "sp"),
            P("sp", "dp"),
            P("sp", "dp"),
        ),
        check_vma=False,
    )
```

time: 309 us -> 230 us (0.74); the launches traced: 303 us -> 227 us
  starting transfers between devices: 85.5 us -> 38.5 us
  waiting for transfers between devices: 122 us -> 99.6 us
  Pallas kernels: 63.4 us -> 57.1 us
    ppermute x30 -> x11, waiting for transfers between devices: 95 us -> 54.7 us  [send_sp(): return lax.ppermute(value, 'sp', sp_perm(dy, dz))]
    ppermute x30 -> x11, starting transfers between devices: 49.1 us -> 12.6 us  [send_sp(): return lax.ppermute(value, 'sp', sp_perm(dy, dz))]
    ppermute x14 -> x12, starting transfers between devices: 36.3 us -> 14.9 us  [send_dp(): return lax.ppermute(value, 'dp', dp_perm(dh, dx, dc))]
    ppermute x14 -> x12, waiting for transfers between devices: 27 us -> 38.7 us  [send_dp(): return lax.ppermute(value, 'dp', dp_perm(dh, dx, dc))]
    all_to_all x0 -> x2, starting transfers between devices: none -> 10.9 us  [the longest x1 6.09 us: body(): chunks = lax.all_to_all(sent, 'sp', 0, 0, tiled=True)]
    pallas_call x5 -> x4, Pallas kernels: 35.1 us -> 28.8 us  [the longest x1 12.4 us: backward(): pl.pallas_call(backward_kernel, grid=(4,), out_shape=[shape_of(8, 3, BLK,...]
    all_gather x1, waiting for transfers between devices: 0.01 us -> 5.54 us  [body(): lax.all_gather(w_pair, 'dp', axis=0, axis_index_groups=[[2 * n + core for...]
    convert_element_type x3 -> x4, other arithmetic: 6.3 us -> 8.37 us  [the longest x2 5.62 us: sum_cores(): return [share(step).astype(BF) for step in range(4)]]
  transfers between devices with their start and end apart: 45 -> 26, of which waited for: 21 -> 13; matrix products, arithmetic and copies ran while one was open for 4% -> 2% of each run, Pallas kernels for 20% -> 23%
where the time goes in v2:
time: 230 us; the launch traced here: 227 us
  waiting for transfers between devices  99.6 us (43%)
  Pallas kernels  57.1 us (25%)
  starting transfers between devices  38.5 us (17%)
  between operations  14.3 us (6%)
  other arithmetic  10.1 us (4%)
  local copies, waits for them, and re-layouts  7.57 us (3%)
    ppermute x11, waiting for transfers between devices, send_sp(): return lax.ppermute(value, 'sp', sp_perm(dy, dz))  54.7 us
    ppermute x12, waiting for transfers between devices, send_dp(): return lax.ppermute(value, 'dp', dp_perm(dh, dx, dc))  38.7 us
    pallas_call x2, Pallas kernels, weight_grad(): pl.pallas_call(weight_grad_kernel, grid=(8,), out_shape=[shape_of(16, BLK...  15.5 us
    ppermute x12, starting transfers between devices, send_dp(): return lax.ppermute(value, 'dp', dp_perm(dh, dx, dc))  14.9 us
    pallas_call x1, Pallas kernels, forward(): pl.pallas_call(forward_kernel, grid=(4,), out_shape=[shape_of(4, SEQ, SEQ...  12.8 us
    ppermute x11, starting transfers between devices, send_sp(): return lax.ppermute(value, 'sp', sp_perm(dy, dz))  12.6 us
    pallas_call x1, Pallas kernels, backward(): pl.pallas_call(backward_kernel, grid=(4,), out_shape=[shape_of(8, 3, BLK,...  12.4 us
    pallas_call x1, Pallas kernels, project_back(): pl.pallas_call(grad_out_kernel, grid=(4,), in_specs=[SMEM] + [pl.BlockSpe...  8.09 us
  transfers between devices with their start and end apart: 26, of which 13 were waited for; matrix products, arithmetic and copies ran while one was open for 2% of the time, Pallas kernels for 23%

profile of v2, /device:TPU:8, one launch (start us, length us, event | category | flops | bytes accessed | tf_op | source)
XLA Modules:
  0.0 227.1 jit_solution(4569258643118119460)
XLA Ops:
  9.4 2.0 collective-permute-start
  11.4 1.6 collective-permute-start.1
  14.3 4.2 %pack.1 = (bf16[8,4,96,512]{3,2,1,0:T(8,128)(2,1)}, bf16[3,128,256]{2,1,0:T(8,128)(2,1)}, bf16[3,128,256]{2,1,0:T(8,128)(2,1)}) custom-call(s32[5]{0:T(128)} %stack.61.idx, bf16[2,3,96,2048]{3,2,1,0:T(8,128)(2,1)} %qkv.1, bf16[2,3,128,256]{3,2,1,0:T(8,128)(2,1)} %qt.1, bf16[2,128,384]{2,1,0:T(8,128)(2,1)} %ct.1), custom_call_target="tpu_custom_call" | custom-call | bytes 8388 | tf_op jit(solution)/shard_map/pack/pallas_call | solution.py:116
  18.6 8.2 %collective-permute-done.3 = bf16[2,96,256]{2,1,0:T(8,128)(2,1)S(1)} collective-permute-done((bf16[2,96,256]{2,1,0:T(8,128)(2,1)S(1)}, bf16[2,96,256]{2,1,0:T(8,128)(2,1)S(1)}, u32[]{:S(2)}, u32[]{:S(2)}) %collective-permute-start.3) | collective-permute-done | bytes 98336 | tf_op jit(solution)/shard_map/ppermute | solution.py:43
  28.8 6.1 %all-to-all-start = ((bf16[8,4,96,512]{3,2,1,0:T(8,128)(2,1)}), bf16[8,4,96,512]{3,2,1,0:T(8,128)(2,1)S(1)}, u32[]{:S(2)}, u32[]{:S(2)}) async-start(bf16[8,4,96,512]{3,2,1,0:T(8,128)(2,1)} %get-tuple-element.88), calls=%async_computation | async-start | bytes 6291456 | tf_op jit(solution)/shard_map/all_to_all | solution.py:456
  35.6 1.5 collective-permute-start.4
  37.7 1.5 collective-permute-start.6
  39.1 40.9 %collective-permute-done.6.other = bf16[3,128,256]{2,1,0:T(8,128)(2,1)S(1)} collective-permute-done((bf16[3,128,256]{2,1,0:T(8,128)(2,1)S(1)}, bf16[3,128,256]{2,1,0:T(8,128)(2,1)S(1)}, u32[]{:S(2)}, u32[]{:S(2)}) %collective-permute-start.6) | collective-permute-done | bytes 196640 | tf_op jit(solution)/shard_map/ppermute | solution.py:43
  82.2 1.4 collective-permute-start.7
  85.5 12.8 %forward.1 = (f32[4,896,896]{2,1,0:T(8,128)}, bf16[768,512]{1,0:T(8,128)(2,1)}, bf16[128,512]{1,0:T(8,128)(2,1)}) custom-call(s32[5]{0:T(128)} %stack.61.idx, s32[1]{0:T(128)} %dynamic_slice.84.length, f32[2,2,128]{2,1,0:T(2,128)} %gains.3, bf16[8,4,96,512]{3,2,1,0:T(8,128)(2,1)} %copy-done, bf16[3,128,256]{2,1,0:T(8,128)(2,1)} %get-tuple-element.91.own, ...), custom_call_target="tpu_custom_call" | custom-call | flops 1644167 | bytes 18874 | tf_op jit(solution)/shard_map/forward/pallas_call | solution.py:227
  98.3 6.7 %weight_text.1 = (bf16[16,96,512]{2,1,0:T(8,128)(2,1)}, bf16[16,96,512]{2,1,0:T(8,128)(2,1)}) custom-call(s32[5]{0:T(128)} %stack.61.idx, bf16[128,512]{1,0:T(8,128)(2,1)} %get-tuple-element.97.att, bf16[8,4,96,512]{3,2,1,0:T(8,128)(2,1)} %copy-done), custom_call_target="tpu_custom_call" | custom-call | flops 402653 | bytes 8388 | tf_op jit(solution)/shard_map/weight_text/pallas_call | solution.py:375
  105.0 5.5 %all-gather.3.cloned.1.call-done = bf16[32,2,96,256]{3,2,1,0:T(8,128)(2,1)} async-done(((bf16[2,2,96,256]{3,2,1,0:T(8,128)(2,1)}), bf16[32,2,96,256]{3,2,1,0:T(8,128)(2,1)}) %all-gather.3.cloned.1.call-update) | async-done | bytes 3145744 | tf_op jit(solution)/shard_map/all_gather | solution.py:446
  111.0 8.8 %weight_video.1 = (bf16[16,96,512]{2,1,0:T(8,128)(2,1)}, bf16[16,96,512]{2,1,0:T(8,128)(2,1)}) custom-call(s32[5]{0:T(128)} %stack.61.idx, bf16[768,512]{1,0:T(8,128)(2,1)} %get-tuple-element.103.att, bf16[96,3072]{1,0:T(8,128)(2,1)} %copy-done.2, bf16[96,3072]{1,0:T(8,128)(2,1)} %copy-done.4, bf16[96,3072]{1,0:T(8,128)(2,1)} %copy-done.5, ...), custom_call_target="tpu_custom_call" | custom-call | flops 2415919 | bytes 8388 | tf_op jit(solution)/shard_map/weight_video/pallas_call | solution.py:375
  119.8 4.3 %fusion.3 = (bf16[4,96,512]{2,1,0:T(8,128)(2,1)}, bf16[4,96,512]{2,1,0:T(8,128)(2,1)}, bf16[4,96,512]{2,1,0:T(8,128)(2,1)}, bf16[4,96,512]{2,1,0:T(8,128)(2,1)S(1)}) fusion(bf16[4,4,96,512]{3,2,1,0:T(8,128)(2,1)} %bitcast.15, s32[]{:T(128)S(6)} %select_n.86, bf16[4,4,96,512]{3,2,1,0:T(8,128)(2,1)} %bitcast.80, s32[]{:T(128)S(6)} %select_n.85, ...), kind=kLoop, calls=%fused_computation.15 | loop fusion | flops 3145728 | bytes 4718608 | tf_op jit(solution)/shard_map/convert_element_type | solution.py:401
  124.4 1.5 collective-permute-start.11
  125.9 1.8 collective-permute-start.12
  127.7 8.1 %project_back.1.grad_out = bf16[896,512]{1,0:T(8,128)(2,1)} custom-call(s32[5]{0:T(128)} %stack.61.idx, bf16[96,3072]{1,0:T(8,128)(2,1)} %copy-done.2, bf16[96,3072]{1,0:T(8,128)(2,1)} %copy-done.4, bf16[96,3072]{1,0:T(8,128)(2,1)} %copy-done.5, bf16[96,3072]{1,0:T(8,128)(2,1)} %copy-done.7, bf16[96,3072]{1,0:T(8,128)(2,1)} %collective-permute-done.7.refs_4_, ...), custom_call_target="tpu_custom_call" | custom-call | flops 2818572 | bytes 13631 | tf_op jit(solution)/shard_map/project_back/pallas_call | solution.py:340
  135.8 1.5 collective-permute-done.11
  138.1 1.3 fusion.7
  140.2 2.4 %collective-permute-start.15 = (bf16[4,96,512]{2,1,0:T(8,128)(2,1)}, bf16[4,96,512]{2,1,0:T(8,128)(2,1)}, u32[]{:S(2)}, u32[]{:S(2)}) collective-permute-start(bf16[4,96,512]{2,1,0:T(8,128)(2,1)} %get-tuple-element.133), channel_id=1, source_target_pairs={{0,48},{8,56},{16,0},{24,8},{32,16},{40,24},{48,32},{56,40},{64,11... | collective-permute-start | bytes 1179656 | tf_op jit(solution)/shard_map/ppermute | solution.py:56
  143.5 12.4 %backward.1 = (bf16[8,3,96,512]{3,2,1,0:T(8,128)(2,1)}, bf16[3,128,256]{2,1,0:T(8,128)(2,1)}, bf16[3,128,256]{2,1,0:T(8,128)(2,1)}) custom-call(s32[5]{0:T(128)} %stack.61.idx, f32[2,2,128]{2,1,0:T(2,128)} %gains.3, f32[4,896,896]{2,1,0:T(8,128)} %get-tuple-element.135.prob_ref, bf16[896,512]{1,0:T(8,128)(2,1)} %project_back.1.grad_out, ...), custom_call_target="tpu_custom_call" | custom-call | flops 3288334 | bytes 20971 | tf_op jit(solution)/shard_map/backward/pallas_call | solution.py:296
  155.9 3.5 %collective-permute-done.15 = bf16[4,96,512]{2,1,0:T(8,128)(2,1)} collective-permute-done((bf16[4,96,512]{2,1,0:T(8,128)(2,1)}, bf16[4,96,512]{2,1,0:T(8,128)(2,1)}, u32[]{:S(2)}, u32[]{:S(2)}) %collective-permute-start.15) | collective-permute-done | bytes 393248 | tf_op jit(solution)/shard_map/ppermute | solution.py:56
  160.3 4.8 %all-to-all-start.1 = ((bf16[8,3,96,512]{3,2,1,0:T(8,128)(2,1)}), bf16[8,3,96,512]{3,2,1,0:T(8,128)(2,1)S(1)}, u32[]{:S(2)}, u32[]{:S(2)}) async-start(bf16[8,3,96,512]{3,2,1,0:T(8,128)(2,1)} %get-tuple-element.141), calls=%async_computation.1 | async-start | bytes 4718592 | tf_op jit(solution)/shard_map/all_to_all | solution.py:496
  165.6 1.4 add_convert_fusion.1
  167.1 8.6 %collective-permute-done.18 = bf16[4,96,512]{2,1,0:T(8,128)(2,1)S(1)} collective-permute-done((bf16[4,96,512]{2,1,0:T(8,128)(2,1)}, bf16[4,96,512]{2,1,0:T(8,128)(2,1)S(1)}, u32[]{:S(2)}, u32[]{:S(2)}) %collective-permute-start.18) | collective-permute-done | bytes 393248 | tf_op jit(solution)/shard_map/ppermute | solution.py:56
  177.1 3.4 %collective-permute-start.21 = (bf16[2,96,512]{2,1,0:T(8,128)(2,1)S(1)}, bf16[2,96,512]{2,1,0:T(8,128)(2,1)S(1)}, u32[]{:S(2)}, u32[]{:S(2)}) collective-permute-start(bf16[2,96,512]{2,1,0:T(8,128)(2,1)S(1)} %pad_maximum_fusion.3), channel_id=1, source_target_pairs={{0,192},{8,200},{16,208},{24,216},{32,224},{40,232},{48,240},{56,2... | collective-permute-start | bytes 589832 | tf_op jit(solution)/shard_map/ppermute | solution.py:56
  180.7 2.7 %collective-permute-start.19 = (bf16[2,96,512]{2,1,0:T(8,128)(2,1)S(1)}, bf16[2,96,512]{2,1,0:T(8,128)(2,1)S(1)}, u32[]{:S(2)}, u32[]{:S(2)}) collective-permute-start(bf16[2,96,512]{2,1,0:T(8,128)(2,1)S(1)} %pad_maximum_fusion.1), channel_id=1, source_target_pairs={{0,128},{8,136},{16,144},{24,152},{32,160},{40,168},{48,176},{56,1... | collective-permute-start | bytes 589832 | tf_op jit(solution)/shard_map/ppermute | solution.py:56
  183.9 23.6 %collective-permute-done.20 = bf16[2,96,512]{2,1,0:T(8,128)(2,1)S(1)} collective-permute-done((bf16[2,96,512]{2,1,0:T(8,128)(2,1)S(1)}, bf16[2,96,512]{2,1,0:T(8,128)(2,1)S(1)}, u32[]{:S(2)}, u32[]{:S(2)}) %collective-permute-start.20) | collective-permute-done | bytes 196640 | tf_op jit(solution)/shard_map/ppermute | solution.py:56
  207.6 1.4 collective-permute-start.22
  209.7 2.6 %collective-permute-done.22 = bf16[2,96,256]{2,1,0:T(8,128)(2,1)S(1)} collective-permute-done((bf16[2,96,256]{2,1,0:T(8,128)(2,1)S(1)}, bf16[2,96,256]{2,1,0:T(8,128)(2,1)S(1)}, u32[]{:S(2)}, u32[]{:S(2)}) %collective-permute-start.22) | collective-permute-done | bytes 98336 | tf_op jit(solution)/shard_map/ppermute | solution.py:43
  213.0 1.6 collective-permute-done.17.other
  216.1 4.2 %unpack.1 = (bf16[2,3,96,2048]{3,2,1,0:T(8,128)(2,1)}, bf16[2,3,128,256]{3,2,1,0:T(8,128)(2,1)}) custom-call(s32[5]{0:T(128)} %stack.61.idx, bf16[8,3,96,512]{3,2,1,0:T(8,128)(2,1)} %copy-done.1, bf16[3,128,256]{2,1,0:T(8,128)(2,1)} %get-tuple-element.142.own, bf16[3,128,256]{2,1,0:T(8,128)(2,1)} %copy-done.11), custom_call_target="tpu_custom_call" | custom-call | bytes 6291 | tf_op jit(solution)/shard_map/unpack/pallas_call | solution.py:158
  (76 shorter events, 20.5 us)
Async XLA Ops:
  9.4 18.1 %copy-start.2 = (bf16[96,3072]{1,0:T(8,128)(2,1)}, bf16[96,3072]{1,0:T(8,128)(2,1)S(1)}, u32[]{:S(2)}) copy-start(bf16[96,3072]{1,0:T(8,128)(2,1)S(1)} %get-tuple-element.118.refs_0_) | copy-start | bytes 1769476
  9.4 18.1 %collective-permute-start = (bf16[96,3072]{1,0:T(8,128)(2,1)S(1)}, bf16[96,3072]{1,0:T(8,128)(2,1)S(1)}, u32[]{:S(2)}, u32[]{:S(2)}) collective-permute-start(bf16[96,3072]{1,0:T(8,128)(2,1)S(1)} %get-tuple-element.80), channel_id=1, source_target_pairs={{0,1},{1,0},{2,3},{3,2},{4,5},{5,4},{6,7},{7,6},{8,9},{9,8},{10,11... | collective-permute-start | bytes 1769480 | tf_op jit(solution)/shard_map/ppermute | solution.py:43
  11.4 16.1 %collective-permute-start.1 = (bf16[96,3072]{1,0:T(8,128)(2,1)S(1)}, bf16[96,3072]{1,0:T(8,128)(2,1)S(1)}, u32[]{:S(2)}, u32[]{:S(2)}) collective-permute-start(bf16[96,3072]{1,0:T(8,128)(2,1)S(1)} %get-tuple-element.118.refs_0_), channel_id=1, source_target_pairs={{0,2},{1,3},{2,4},{3,5},{4,6},{5,7},{6,0},{7,1},{8,10},{9,11},{10,... | collective-permute-start | bytes 1769480 | tf_op jit(solution)/shard_map/ppermute | solution.py:43
  12.9 14.6 %collective-permute-start.2 = (bf16[96,3072]{1,0:T(8,128)(2,1)S(1)}, bf16[96,3072]{1,0:T(8,128)(2,1)S(1)}, u32[]{:S(2)}, u32[]{:S(2)}) collective-permute-start(bf16[96,3072]{1,0:T(8,128)(2,1)S(1)} %get-tuple-element.118.refs_0_), channel_id=1, source_target_pairs={{0,6},{1,7},{2,0},{3,1},{4,2},{5,3},{6,4},{7,5},{8,14},{9,15},{10,... | collective-permute-start | bytes 1769480 | tf_op jit(solution)/shard_map/ppermute | solution.py:43
  13.4 13.4 %collective-permute-start.3 = (bf16[2,96,256]{2,1,0:T(8,128)(2,1)S(1)}, bf16[2,96,256]{2,1,0:T(8,128)(2,1)S(1)}, u32[]{:S(2)}, u32[]{:S(2)}) collective-permute-start(bf16[2,96,256]{2,1,0:T(8,128)(2,1)S(1)} %pad_maximum_fusion.4), channel_id=1, source_target_pairs={{0,1},{1,0},{2,3},{3,2},{4,5},{5,4},{6,7},{7,6},{8,9},{9,8},{10,11... | collective-permute-start | bytes 294920 | tf_op jit(solution)/shard_map/ppermute | solution.py:43
  27.5 10.1 %copy-start.13 = (bf16[3,128,256]{2,1,0:T(8,128)(2,1)S(1)}, bf16[3,128,256]{2,1,0:T(8,128)(2,1)}, u32[]{:S(2)}) copy-start(bf16[3,128,256]{2,1,0:T(8,128)(2,1)} %get-tuple-element.89) | copy-start | bytes 589828
  27.6 57.3 %copy-start.14 = (s32[2]{0:T(128)S(1)}, s32[2]{0:T(128)}, u32[]{:S(2)}) copy-start(s32[2]{0:T(128)} %param.11) | copy-start | bytes 28
  28.8 53.5 %all-to-all-start = ((bf16[8,4,96,512]{3,2,1,0:T(8,128)(2,1)}), bf16[8,4,96,512]{3,2,1,0:T(8,128)(2,1)S(1)}, u32[]{:S(2)}, u32[]{:S(2)}) async-start(bf16[8,4,96,512]{3,2,1,0:T(8,128)(2,1)} %get-tuple-element.88), calls=%async_computation | async-start | bytes 6291456 | tf_op jit(solution)/shard_map/all_to_all | solution.py:456
  34.9 75.7 %all-gather.3.cloned.1.call-start = ((), (), s32[]{:S(2)}) async-start(), calls=%async_computation.2 | async-start | bytes 3342336 | tf_op jit(solution)/shard_map/all_gather | solution.py:446
  35.6 45.4 %collective-permute-start.4 = (bf16[96,3072]{1,0:T(8,128)(2,1)}, bf16[96,3072]{1,0:T(8,128)(2,1)S(1)}, u32[]{:S(2)}, u32[]{:S(2)}) collective-permute-start(bf16[96,3072]{1,0:T(8,128)(2,1)} %copy-done.4), channel_id=1, source_target_pairs={{0,2},{1,3},{2,4},{3,5},{4,6},{5,7},{6,0},{7,1},{8,10},{9,11},{10,... | collective-permute-start | bytes 1769480 | tf_op jit(solution)/shard_map/ppermute | solution.py:43
  37.1 45.1 %collective-permute-start.5 = (bf16[96,3072]{1,0:T(8,128)(2,1)}, bf16[96,3072]{1,0:T(8,128)(2,1)}, u32[]{:S(2)}, u32[]{:S(2)}) collective-permute-start(bf16[96,3072]{1,0:T(8,128)(2,1)} %copy-done.4), channel_id=1, source_target_pairs={{0,6},{1,7},{2,0},{3,1},{4,2},{5,3},{6,4},{7,5},{8,14},{9,15},{10,... | collective-permute-start | bytes 1769480 | tf_op jit(solution)/shard_map/ppermute | solution.py:43
  37.7 42.4 %collective-permute-start.6 = (bf16[3,128,256]{2,1,0:T(8,128)(2,1)S(1)}, bf16[3,128,256]{2,1,0:T(8,128)(2,1)S(1)}, u32[]{:S(2)}, u32[]{:S(2)}) collective-permute-start(bf16[3,128,256]{2,1,0:T(8,128)(2,1)S(1)} %copy-done.13), channel_id=1, source_target_pairs={{0,1},{1,0},{2,3},{3,2},{4,5},{5,4},{6,7},{7,6},{8,9},{9,8},{10,11... | collective-permute-start | bytes 589832 | tf_op jit(solution)/shard_map/ppermute | solution.py:43
  80.1 5.4 %copy-start.9 = (bf16[3,128,256]{2,1,0:T(8,128)(2,1)}, bf16[3,128,256]{2,1,0:T(8,128)(2,1)S(1)}, u32[]{:S(2)}) copy-start(bf16[3,128,256]{2,1,0:T(8,128)(2,1)S(1)} %collective-permute-done.6.other) | copy-start | bytes 589828
  82.2 16.0 %collective-permute-start.7 = (bf16[96,3072]{1,0:T(8,128)(2,1)}, bf16[96,3072]{1,0:T(8,128)(2,1)}, u32[]{:S(2)}, u32[]{:S(2)}) collective-permute-start(bf16[96,3072]{1,0:T(8,128)(2,1)} %copy-done.5), channel_id=1, source_target_pairs={{0,2},{1,3},{2,4},{3,5},{4,6},{5,7},{6,0},{7,1},{8,10},{9,11},{10,... | collective-permute-start | bytes 1769480 | tf_op jit(solution)/shard_map/ppermute | solution.py:43
  83.6 14.7 %collective-permute-start.8 = (bf16[96,3072]{1,0:T(8,128)(2,1)}, bf16[96,3072]{1,0:T(8,128)(2,1)}, u32[]{:S(2)}, u32[]{:S(2)}) collective-permute-start(bf16[96,3072]{1,0:T(8,128)(2,1)} %collective-permute-done.5.refs_7_), channel_id=1, source_target_pairs={{0,6},{1,7},{2,0},{3,1},{4,2},{5,3},{6,4},{7,5},{8,14},{9,15},{10,... | collective-permute-start | bytes 1769480 | tf_op jit(solution)/shard_map/ppermute | solution.py:43
  110.5 9.3 %collective-permute-start.10 = (bf16[16,2,2,96,256]{4,3,2,1,0:T(8,128)(2,1)}, bf16[16,2,2,96,256]{4,3,2,1,0:T(8,128)(2,1)S(1)}, u32[]{:S(2)}, u32[]{:S(2)}) collective-permute-start(bf16[16,2,2,96,256]{4,3,2,1,0:T(8,128)(2,1)} %bitcast.78), channel_id=1, source_target_pairs={{0,8},{8,0},{16,24},{24,16},{32,40},{40,32},{48,56},{56,48},{64,72... | collective-permute-start | bytes 9437192 | tf_op jit(solution)/shard_map/ppermute | solution.py:56
  110.5 9.3 %collective-permute-start.9 = (bf16[16,96,512]{2,1,0:T(8,128)(2,1)}, bf16[16,96,512]{2,1,0:T(8,128)(2,1)}, u32[]{:S(2)}, u32[]{:S(2)}) collective-permute-start(bf16[16,96,512]{2,1,0:T(8,128)(2,1)} %get-tuple-element.102), channel_id=1, source_target_pairs={{0,8},{8,0},{16,24},{24,16},{32,40},{40,32},{48,56},{56,48},{64,72... | collective-permute-start | bytes 4718600 | tf_op jit(solution)/shard_map/ppermute | solution.py:56
  124.1 14.0 %copy-start.8 = (bf16[16,96,512]{2,1,0:T(8,128)(2,1)S(1)}, bf16[16,96,512]{2,1,0:T(8,128)(2,1)}, u32[]{:S(2)}) copy-start(bf16[16,96,512]{2,1,0:T(8,128)(2,1)} %get-tuple-element.127) | copy-start | bytes 4718596
  124.1 13.3 %collective-permute-start.13 = (bf16[16,96,512]{2,1,0:T(8,128)(2,1)}, bf16[16,96,512]{2,1,0:T(8,128)(2,1)S(1)}, u32[]{:S(2)}, u32[]{:S(2)}) collective-permute-start(bf16[16,96,512]{2,1,0:T(8,128)(2,1)} %get-tuple-element.116), channel_id=1, source_target_pairs={{0,8},{8,0},{16,24},{24,16},{32,40},{40,32},{48,56},{56,48},{64,72... | collective-permute-start | bytes 4718600 | tf_op jit(solution)/shard_map/ppermute | solution.py:56
  124.4 12.9 %collective-permute-start.11 = (bf16[4,96,512]{2,1,0:T(8,128)(2,1)}, bf16[4,96,512]{2,1,0:T(8,128)(2,1)S(1)}, u32[]{:S(2)}, u32[]{:S(2)}) collective-permute-start(bf16[4,96,512]{2,1,0:T(8,128)(2,1)} %get-tuple-element.114), channel_id=1, source_target_pairs={{0,16},{8,24},{16,32},{24,40},{32,48},{40,56},{48,0},{56,8},{64,80... | collective-permute-start | bytes 1179656 | tf_op jit(solution)/shard_map/ppermute | solution.py:56
  125.9 11.5 %collective-permute-start.12 = (bf16[4,96,512]{2,1,0:T(8,128)(2,1)}, bf16[4,96,512]{2,1,0:T(8,128)(2,1)}, u32[]{:S(2)}, u32[]{:S(2)}) collective-permute-start(bf16[4,96,512]{2,1,0:T(8,128)(2,1)} %get-tuple-element.115), channel_id=1, source_target_pairs={{0,48},{8,56},{16,0},{24,8},{32,16},{40,24},{48,32},{56,40},{64,11... | collective-permute-start | bytes 1179656 | tf_op jit(solution)/shard_map/ppermute | solution.py:56
  139.4 16.5 %collective-permute-start.14 = (bf16[4,96,512]{2,1,0:T(8,128)(2,1)}, bf16[4,96,512]{2,1,0:T(8,128)(2,1)}, u32[]{:S(2)}, u32[]{:S(2)}) collective-permute-start(bf16[4,96,512]{2,1,0:T(8,128)(2,1)} %get-tuple-element.132), channel_id=1, source_target_pairs={{0,16},{8,24},{16,32},{24,40},{32,48},{40,56},{48,0},{56,8},{64,80... | collective-permute-start | bytes 1179656 | tf_op jit(solution)/shard_map/ppermute | solution.py:56
  140.2 19.1 %collective-permute-start.15 = (bf16[4,96,512]{2,1,0:T(8,128)(2,1)}, bf16[4,96,512]{2,1,0:T(8,128)(2,1)}, u32[]{:S(2)}, u32[]{:S(2)}) collective-permute-start(bf16[4,96,512]{2,1,0:T(8,128)(2,1)} %get-tuple-element.133), channel_id=1, source_target_pairs={{0,48},{8,56},{16,0},{24,8},{32,16},{40,24},{48,32},{56,40},{64,11... | collective-permute-start | bytes 1179656 | tf_op jit(solution)/shard_map/ppermute | solution.py:56
  142.7 17.6 %collective-permute-start.16 = (bf16[4,96,512]{2,1,0:T(8,128)(2,1)}, bf16[4,96,512]{2,1,0:T(8,128)(2,1)}, u32[]{:S(2)}, u32[]{:S(2)}) collective-permute-start(bf16[4,96,512]{2,1,0:T(8,128)(2,1)} %get-tuple-element.134), channel_id=1, source_target_pairs={{0,32},{8,40},{16,48},{24,56},{32,0},{40,8},{48,16},{56,24},{64,96... | collective-permute-start | bytes 1179656 | tf_op jit(solution)/shard_map/ppermute | solution.py:56
  160.3 54.3 %all-to-all-start.1 = ((bf16[8,3,96,512]{3,2,1,0:T(8,128)(2,1)}), bf16[8,3,96,512]{3,2,1,0:T(8,128)(2,1)S(1)}, u32[]{:S(2)}, u32[]{:S(2)}) async-start(bf16[8,3,96,512]{3,2,1,0:T(8,128)(2,1)} %get-tuple-element.141), calls=%async_computation.1 | async-start | bytes 4718592 | tf_op jit(solution)/shard_map/all_to_all | solution.py:496
  165.1 10.6 %collective-permute-start.18 = (bf16[4,96,512]{2,1,0:T(8,128)(2,1)}, bf16[4,96,512]{2,1,0:T(8,128)(2,1)S(1)}, u32[]{:S(2)}, u32[]{:S(2)}) collective-permute-start(bf16[4,96,512]{2,1,0:T(8,128)(2,1)} %get-tuple-element.153), channel_id=1, source_target_pairs={{0,32},{8,40},{16,48},{24,56},{32,0},{40,8},{48,16},{56,24},{64,96... | collective-permute-start | bytes 1179656 | tf_op jit(solution)/shard_map/ppermute | solution.py:56
  177.0 31.9 %copy-start.12 = (bf16[3,128,256]{2,1,0:T(8,128)(2,1)S(1)}, bf16[3,128,256]{2,1,0:T(8,128)(2,1)}, u32[]{:S(2)}) copy-start(bf16[3,128,256]{2,1,0:T(8,128)(2,1)} %get-tuple-element.143) | copy-start | bytes 589828
  177.1 6.7 %collective-permute-start.21 = (bf16[2,96,512]{2,1,0:T(8,128)(2,1)S(1)}, bf16[2,96,512]{2,1,0:T(8,128)(2,1)S(1)}, u32[]{:S(2)}, u32[]{:S(2)}) collective-permute-start(bf16[2,96,512]{2,1,0:T(8,128)(2,1)S(1)} %pad_maximum_fusion.3), channel_id=1, source_target_pairs={{0,192},{8,200},{16,208},{24,216},{32,224},{40,232},{48,240},{56,2... | collective-permute-start | bytes 589832 | tf_op jit(solution)/shard_map/ppermute | solution.py:56
  180.5 26.9 %collective-permute-start.20 = (bf16[2,96,512]{2,1,0:T(8,128)(2,1)S(1)}, bf16[2,96,512]{2,1,0:T(8,128)(2,1)S(1)}, u32[]{:S(2)}, u32[]{:S(2)}) collective-permute-start(bf16[2,96,512]{2,1,0:T(8,128)(2,1)S(1)} %pad_maximum_fusion.2), channel_id=1, source_target_pairs={{0,64},{8,72},{16,80},{24,88},{32,96},{40,104},{48,112},{56,120},{... | collective-permute-start | bytes 589832 | tf_op jit(solution)/shard_map/ppermute | solution.py:56
  180.7 26.8 %collective-permute-start.19 = (bf16[2,96,512]{2,1,0:T(8,128)(2,1)S(1)}, bf16[2,96,512]{2,1,0:T(8,128)(2,1)S(1)}, u32[]{:S(2)}, u32[]{:S(2)}) collective-permute-start(bf16[2,96,512]{2,1,0:T(8,128)(2,1)S(1)} %pad_maximum_fusion.1), channel_id=1, source_target_pairs={{0,128},{8,136},{16,144},{24,152},{32,160},{40,168},{48,176},{56,1... | collective-permute-start | bytes 589832 | tf_op jit(solution)/shard_map/ppermute | solution.py:56
  207.6 4.7 %collective-permute-start.22 = (bf16[2,96,256]{2,1,0:T(8,128)(2,1)S(1)}, bf16[2,96,256]{2,1,0:T(8,128)(2,1)S(1)}, u32[]{:S(2)}, u32[]{:S(2)}) collective-permute-start(bf16[2,96,256]{2,1,0:T(8,128)(2,1)S(1)} %slice.25), channel_id=1, source_target_pairs={{0,1},{1,0},{2,3},{3,2},{4,5},{5,4},{6,7},{7,6},{8,9},{9,8},{10,11... | collective-permute-start | bytes 294920 | tf_op jit(solution)/shard_map/ppermute | solution.py:43
  209.0 5.7 %collective-permute-start.17 = (bf16[3,128,256]{2,1,0:T(8,128)(2,1)S(1)}, bf16[3,128,256]{2,1,0:T(8,128)(2,1)S(1)}, u32[]{:S(2)}, u32[]{:S(2)}) collective-permute-start(bf16[3,128,256]{2,1,0:T(8,128)(2,1)S(1)} %copy-done.12), channel_id=1, source_target_pairs={{0,1},{1,0},{2,3},{3,2},{4,5},{5,4},{6,7},{7,6},{8,9},{9,8},{10,11... | collective-permute-start | bytes 589832 | tf_op jit(solution)/shard_map/ppermute | solution.py:43
  (9 other events, 14.4 us)
Sparse Core Ops, SparseCore 0:
  38.7 71.8 all-gather.2

commit v3 on v2

--- a/solution.py
+++ b/solution.py
@@ -353,35 +353,34 @@
     )(idx, *cots, cot_text, mine, theirs)
 
 
-def weight_grad_kernel(idx, att, *refs):
-    cots, keep, send = refs[:-2], refs[-2], refs[-1]
-    if len(cots) > 1:
-        cot = jnp.concatenate([c[...] for c in cots], axis=0)
-    else:
-        cot = unfold_text(cots[0][...])
-    part = dot(cot, att[...], TN).reshape(2, 2, BLK, 512)
+def weight_grad_kernel(idx, att_video, att_text, cot_text, *refs):
+    cots, keep, give = refs[:8], refs[8], refs[9]
+    video = jnp.concatenate([c[...] for c in cots], axis=0)
     first = idx[2] == 0
-    keep[...] = jnp.where(first, part[:, 0], part[:, 1]).astype(BF)
-    send[...] = jnp.where(first, part[:, 1], part[:, 0]).astype(BF)
-
-
-def weight_grad(idx, att, cots, name):
-    rows = att.shape[0]
-    out = pl.BlockSpec((2, BLK, 512), lambda i: (i, 0, 0))
-    if len(cots) > 1:
-        specs = [pl.BlockSpec((BLK, 384), lambda i: (0, i))] * len(cots)
-    else:
-        specs = [pl.BlockSpec((None, None, BLK, 512), lambda i: (i, 3, 0, 0))]
+    for stream, (cot, att) in enumerate(
+        ((video, att_video), (unfold_text(cot_text[...]), att_text))
+    ):
+        part = dot(cot, att[...], TN).reshape(2, 2, BLK, 512)
+        keep[stream] = jnp.where(first, part[:, 0], part[:, 1]).astype(BF)
+        give[stream] = jnp.where(first, part[:, 1], part[:, 0]).astype(BF)
+
+
+def weight_grad(idx, att_video, att_text, chunks, cots):
+    def whole(rows):
+        return pl.BlockSpec((rows, 512), lambda i: (0, 0))
+
     return pl.pallas_call(
         weight_grad_kernel,
         grid=(8,),
-        out_shape=[shape_of(16, BLK, 512)] * 2,
-        in_specs=[SMEM, pl.BlockSpec((rows, 512), lambda i: (0, 0))] + specs,
-        out_specs=[out, out],
+        out_shape=[shape_of(2, 16, BLK, 512)] * 2,
+        in_specs=[SMEM, whole(VID), whole(TXT)]
+        + [pl.BlockSpec((None, None, BLK, 512), lambda i: (i, 3, 0, 0))]
+        + [pl.BlockSpec((BLK, 384), lambda i: (0, i))] * 8,
+        out_specs=[pl.BlockSpec((2, 2, BLK, 512), lambda i: (0, i, 0, 0))] * 2,
         compiler_params=params(60),
-        cost_estimate=cost(2 * rows * 512 * 3072, 8 * MB),
-        name=name,
-    )(idx, att, *cots)
+        cost_estimate=cost(2 * SEQ * 512 * 3072, 12 * MB),
+        name="weight_grad",
+    )(idx, att_video, att_text, chunks, *cots)
 
 
 def wide_sum(parts):
@@ -389,13 +388,13 @@
 
 
 def sum_cores(idx, keep, got):
-    keep = keep.reshape(4, 4, BLK, 512)
-    got = got.reshape(4, 4, BLK, 512)
+    keep = keep.reshape(2, 4, 4, BLK, 512)
+    got = got.reshape(2, 4, 4, BLK, 512)
 
     def share(step):
         at = lax.rem(idx[4] + step, 4)
         return wide_sum(
-            [lax.dynamic_index_in_dim(v, at, axis=1, keepdims=False) for v in (keep, got)]
+            [lax.dynamic_index_in_dim(v, at, axis=2, keepdims=False) for v in (keep, got)]
         )
 
     return [share(step).astype(BF) for step in range(4)]
@@ -405,13 +404,10 @@
     return [send_dp(shares[step], 0, step, 0) for step in steps]
 
 
-def sum_far_and_near(idx, totals):
-    zh = idx[3]
-
+def sum_far_and_near(idx, total):
     def slab(step):
-        at = lax.rem(zh + step, 4)
-        return jnp.stack(
-            [lax.dynamic_index_in_dim(t, at, axis=0, keepdims=False) for t in totals]
+        return lax.dynamic_index_in_dim(
+            total, lax.rem(idx[3] + step, 4), axis=1, keepdims=False
         )
 
     arrived = [send_dp(slab(step), step, 0, 0) for step in (2, 1, 3)]
@@ -435,13 +431,13 @@
     cot_own = of_clip(cot_video, zl)
     cot_send = of_clip(cot_video, 1 - zl)
     w_own = jnp.stack([w_out_video.T, w_out_text.T])
-    cot_own, cot_send, w_own = after((cot_own, cot_send, w_own))
+    cot_own, cot_send = after((cot_own, cot_send))
 
     near = [cot_own, send_sp(cot_send, 0, 1)]
     below, above = [send_sp(cot_own, 1, 0)], [send_sp(cot_own, 3, 0)]
     w_pair = jnp.stack([w_own, send_sp(w_own, 0, 1)])
     packed = pack(idx, qkv_video, qkv_text, cot_text)
-    near, below, above, packed, w_pair = after((near, below, above, packed, w_pair))
+    near, below, above, packed = after((near, below, above, packed))
 
     weights = lax.all_gather(
         w_pair,
@@ -464,40 +460,30 @@
 
     cots = near + below + far + above
 
-    text_keep, text_give = weight_grad(idx, att_text, [chunks], "weight_text")
-    text_keep, text_give, weights = after((text_keep, text_give, weights))
+    keep, give = weight_grad(idx, att_video, att_text, chunks, cots)
+    keep, give, weights = after((keep, give, weights))
 
     other_weights = send_dp(weights, 0, 0, 1)
-    text_got = send_dp(text_give, 0, 0, 1)
-    keep, give = weight_grad(idx, att_video, cots, "weight_video")
-    text_got, keep, give, other_weights = after((text_got, keep, give, other_weights))
-
-    text_shares = sum_cores(idx, text_keep, text_got)
-    text_shares, give, cots = after((text_shares, give, cots))
-
-    text_near = send_x(text_shares, (1, 3))
+    give, cots, other_weights = after((give, cots, other_weights))
+
     got = send_dp(give, 0, 0, 1)
     grad_out = project_back(idx, cots, chunks, weights, other_weights)
-    text_near, got, keep, grad_out = after((text_near, got, keep, grad_out))
+    got, keep, grad_out = after((got, keep, grad_out))
 
     shares = sum_cores(idx, keep, got)
-    shares, text_shares, grad_out = after((shares, text_shares, grad_out))
+    shares, grad_out = after((shares, grad_out))
 
     near_sums = send_x(shares, (1, 3))
-    text_far = send_x(text_shares, (2,))
     grads, own, other = backward(
         idx, qk_gains, prob, grad_out, chunks, text_own, text_other
     )
-    near_sums, text_far, grads, other, shares = after(
-        (near_sums, text_far, grads, other, shares)
-    )
+    near_sums, grads, other, shares = after((near_sums, grads, other, shares))
 
     far_sums = send_x(shares, (2,))
     grads = lax.all_to_all(grads, "sp", 0, 0, tiled=True)
     other = send_sp(other, 0, 1)
-    text_total = wide_sum([text_shares[0]] + text_near + text_far).astype(BF)
-    video_total = wide_sum([shares[0]] + near_sums + far_sums).astype(BF)
-    grad_w_text, grad_w_video = sum_far_and_near(idx, (text_total, video_total))
+    total = wide_sum([shares[0]] + near_sums + far_sums).astype(BF)
+    grad_w_video, grad_w_text = sum_far_and_near(idx, total)
     grad_qkv_video, grad_qkv_text = unpack(idx, grads, own, other)
     return (grad_qkv_video, grad_qkv_text, grad_w_video, grad_w_text)
 

time: 230 us -> 225 us (0.978)
  Pallas kernels: 57.1 us -> 51.6 us
  local copies, waits for them, and re-layouts: 7.57 us -> 12.9 us
  other arithmetic: 10.1 us -> 5.65 us
  waiting for transfers between devices: 99.6 us -> 102 us
    ppermute x12 -> x8, waiting for transfers between devices: 38.7 us -> 44.1 us  [send_dp(): return lax.ppermute(value, 'dp', dp_perm(dh, dx, dc))]
    pallas_call x2 -> x1, Pallas kernels: 15.5 us -> 10.1 us  [weight_grad(): pl.pallas_call(weight_grad_kernel, grid=(8,), out_shape=[shape_of(2, 16,...]
    convert_element_type x2 -> x4, other arithmetic: 5.62 us -> 1.85 us  [sum_cores(): return [share(step).astype(BF) for step in range(4)]]
    all_gather x1, waiting for transfers between devices: 5.54 us -> 2.39 us  [body(): lax.all_gather(w_pair, 'dp', axis=0, axis_index_groups=[[2 * n + core for...]
    dynamic_slice x2 -> x1, local copies, waits for them, and re-layouts: 0.08 us -> 3.22 us  [share(): lax.dynamic_index_in_dim(v, at, axis=2, keepdims=False)]
    ppermute x12 -> x8, starting transfers between devices: 14.9 us -> 16 us  [send_dp(): return lax.ppermute(value, 'dp', dp_perm(dh, dx, dc))]
  transfers between devices with their start and end apart: 26 -> 22, of which waited for: 13 -> 14; matrix products, arithmetic and copies ran while one was open for 2% -> 3% of each run, Pallas kernels for 23% -> 21%
where the time goes in v3:
time: 225 us; the launch traced here: 224 us
  waiting for transfers between devices  102 us (45%)
  Pallas kernels  51.6 us (23%)
  starting transfers between devices  38.4 us (17%)
  between operations  14.2 us (6%)
  local copies, waits for them, and re-layouts  12.9 us (6%)
  other arithmetic  5.65 us (3%)
    ppermute x11, waiting for transfers between devices, send_sp(): return lax.ppermute(value, 'sp', sp_perm(dy, dz))  55.1 us
    ppermute x8, waiting for transfers between devices, send_dp(): return lax.ppermute(value, 'dp', dp_perm(dh, dx, dc))  44.1 us
    ppermute x8, starting transfers between devices, send_dp(): return lax.ppermute(value, 'dp', dp_perm(dh, dx, dc))  16 us
    ppermute x11, starting transfers between devices, send_sp(): return lax.ppermute(value, 'sp', sp_perm(dy, dz))  12.7 us
    pallas_call x1, Pallas kernels, forward(): pl.pallas_call(forward_kernel, grid=(4,), out_shape=[shape_of(4, SEQ, SEQ...  12.7 us
    pallas_call x1, Pallas kernels, backward(): pl.pallas_call(backward_kernel, grid=(4,), out_shape=[shape_of(8, 3, BLK,...  12.4 us
    pallas_call x1, Pallas kernels, weight_grad(): pl.pallas_call(weight_grad_kernel, grid=(8,), out_shape=[shape_of(2, 16,...  10.1 us
    pallas_call x1, Pallas kernels, project_back(): pl.pallas_call(grad_out_kernel, grid=(4,), in_specs=[SMEM] + [pl.BlockSpe...  8.04 us
  transfers between devices with their start and end apart: 22, of which 14 were waited for; matrix products, arithmetic and copies ran while one was open for 3% of the time, Pallas kernels for 21%

profile of v3, /device:TPU:8, one launch (start us, length us, event | category | flops | bytes accessed | tf_op | source)
XLA Modules:
  0.0 224.4 jit_solution(10479942634857735492)
XLA Ops:
  8.5 2.0 collective-permute-start
  10.6 1.6 collective-permute-start.1
  13.6 4.2 %pack.1 = (bf16[8,4,96,512]{3,2,1,0:T(8,128)(2,1)}, bf16[3,128,256]{2,1,0:T(8,128)(2,1)}, bf16[3,128,256]{2,1,0:T(8,128)(2,1)}) custom-call(s32[5]{0:T(128)} %stack.41.idx, bf16[2,3,96,2048]{3,2,1,0:T(8,128)(2,1)} %qkv.1, bf16[2,3,128,256]{3,2,1,0:T(8,128)(2,1)} %qt.1, bf16[2,128,384]{2,1,0:T(8,128)(2,1)} %ct.1), custom_call_target="tpu_custom_call" | custom-call | bytes 8388 | tf_op jit(solution)/shard_map/pack/pallas_call | solution.py:116
  17.8 7.0 %collective-permute-done.refs_1_ = bf16[96,3072]{1,0:T(8,128)(2,1)S(1)} collective-permute-done((bf16[96,3072]{1,0:T(8,128)(2,1)S(1)}, bf16[96,3072]{1,0:T(8,128)(2,1)S(1)}, u32[]{:S(2)}, u32[]{:S(2)}) %collective-permute-start) | collective-permute-done | bytes 589856 | tf_op jit(solution)/shard_map/ppermute | solution.py:43
  27.5 4.8 %all-to-all-start = ((bf16[8,4,96,512]{3,2,1,0:T(8,128)(2,1)}), bf16[8,4,96,512]{3,2,1,0:T(8,128)(2,1)S(1)}, u32[]{:S(2)}, u32[]{:S(2)}) async-start(bf16[8,4,96,512]{3,2,1,0:T(8,128)(2,1)} %get-tuple-element.71), calls=%async_computation | async-start | bytes 6291456 | tf_op jit(solution)/shard_map/all_to_all | solution.py:452
  33.0 1.5 collective-permute-start.3
  35.1 1.5 collective-permute-start.5
  36.6 40.4 %collective-permute-done.5.other = bf16[3,128,256]{2,1,0:T(8,128)(2,1)S(1)} collective-permute-done((bf16[3,128,256]{2,1,0:T(8,128)(2,1)}, bf16[3,128,256]{2,1,0:T(8,128)(2,1)S(1)}, u32[]{:S(2)}, u32[]{:S(2)}) %collective-permute-start.5) | collective-permute-done | bytes 196640 | tf_op jit(solution)/shard_map/ppermute | solution.py:43
  82.4 12.7 %forward.1 = (f32[4,896,896]{2,1,0:T(8,128)}, bf16[768,512]{1,0:T(8,128)(2,1)}, bf16[128,512]{1,0:T(8,128)(2,1)}) custom-call(s32[5]{0:T(128)} %stack.41.idx, s32[1]{0:T(128)} %dynamic_slice.48.length, f32[2,2,128]{2,1,0:T(2,128)} %gains.3, bf16[8,4,96,512]{3,2,1,0:T(8,128)(2,1)} %copy-done, bf16[3,128,256]{2,1,0:T(8,128)(2,1)} %get-tuple-element.74.own, ...), custom_call_target="tpu_custom_call" | custom-call | flops 1644167 | bytes 18874 | tf_op jit(solution)/shard_map/forward/pallas_call | solution.py:227
  95.1 10.1 %weight_grad.1 = (bf16[2,16,96,512]{3,2,1,0:T(8,128)(2,1)}, bf16[2,16,96,512]{3,2,1,0:T(8,128)(2,1)}) custom-call(s32[5]{0:T(128)} %stack.41.idx, bf16[768,512]{1,0:T(8,128)(2,1)} %get-tuple-element.80.att_video, bf16[128,512]{1,0:T(8,128)(2,1)} %get-tuple-element.81.att_text, bf16[8,4,96,512]{3,2,1,0:T(8,128)(2,1)} %copy-done, bf16[96,3072]{1,0:T(8,128)(2,1)} %copy-done.2, ...), custom_call_target="tpu_custom_call" | custom-call | flops 2818572 | bytes 12582 | tf_op jit(solution)/shard_map/weight_grad/pallas_call | solution.py:372
  105.2 2.4 %all-gather.3.cloned.1.call-done = bf16[32,2,96,256]{3,2,1,0:T(8,128)(2,1)} async-done(((bf16[2,2,96,256]{3,2,1,0:T(8,128)(2,1)}), bf16[32,2,96,256]{3,2,1,0:T(8,128)(2,1)}) %all-gather.3.cloned.1.call-update) | async-done | bytes 3145744 | tf_op jit(solution)/shard_map/all_gather | solution.py:442
  107.6 5.9 %collective-permute-done.9.refs_10_ = bf16[16,2,2,96,256]{4,3,2,1,0:T(8,128)(2,1)S(1)} collective-permute-done((bf16[16,2,2,96,256]{4,3,2,1,0:T(8,128)(2,1)}, bf16[16,2,2,96,256]{4,3,2,1,0:T(8,128)(2,1)S(1)}, u32[]{:S(2)}, u32[]{:S(2)}) %collective-permute-start.9) | collective-permute-done | bytes 3145760 | tf_op jit(solution)/shard_map/ppermute | solution.py:56
  113.6 1.5 copy-done.3
  115.1 8.0 %project_back.1.grad_out = bf16[896,512]{1,0:T(8,128)(2,1)} custom-call(s32[5]{0:T(128)} %stack.41.idx, bf16[96,3072]{1,0:T(8,128)(2,1)} %copy-done.2, bf16[96,3072]{1,0:T(8,128)(2,1)} %copy-done.5, bf16[96,3072]{1,0:T(8,128)(2,1)} %copy-done.6, bf16[96,3072]{1,0:T(8,128)(2,1)} %copy-done.8, bf16[96,3072]{1,0:T(8,128)(2,1)} %collective-permute-done.6.refs_4_, ...), custom_call_target="tpu_custom_call" | custom-call | flops 2818572 | bytes 13631 | tf_op jit(solution)/shard_map/project_back/pallas_call | solution.py:340
  123.2 3.2 %constant_dynamic-slice_fusion = (bf16[2,4,1,96,512]{4,3,2,1,0:T(8,128)(2,1)S(1)}, bf16[2,4,1,96,512]{4,3,2,1,0:T(8,128)(2,1)S(1)}, bf16[2,4,1,96,512]{4,3,2,1,0...) fusion(bf16[2,4,4,96,512]{4,3,2,1,0:T(8,128)(2,1)} %bitcast.15,, ...), kind=kLoop, calls=%fused_computation.23 | loop fusion | bytes 12582928 | tf_op jit(solution)/shard_map/jit(dynamic_index_in_dim)/dynamic_slice | solution.py:397
  128.2 1.5 collective-permute-start.11
  129.8 1.8 collective-permute-start.12
  131.6 12.4 %backward.1 = (bf16[8,3,96,512]{3,2,1,0:T(8,128)(2,1)}, bf16[3,128,256]{2,1,0:T(8,128)(2,1)}, bf16[3,128,256]{2,1,0:T(8,128)(2,1)}) custom-call(s32[5]{0:T(128)} %stack.41.idx, f32[2,2,128]{2,1,0:T(2,128)} %gains.3, f32[4,896,896]{2,1,0:T(8,128)} %get-tuple-element.107.prob_ref, bf16[896,512]{1,0:T(8,128)(2,1)} %project_back.1.grad_out, ...), custom_call_target="tpu_custom_call" | custom-call | flops 3288334 | bytes 20971 | tf_op jit(solution)/shard_map/backward/pallas_call | solution.py:296
  143.9 5.2 %collective-permute-done.11 = bf16[2,4,96,512]{3,2,0,1:T(8,128)(2,1)S(1)} collective-permute-done((bf16[2,4,96,512]{3,2,0,1:T(8,128)(2,1)S(1)}, bf16[2,4,96,512]{3,2,0,1:T(8,128)(2,1)S(1)}, u32[]{:S(2)}, u32[]{:S(2)}) %collective-permute-start.11) | collective-permute-done | bytes 786464 | tf_op jit(solution)/shard_map/ppermute | solution.py:56
  150.0 4.8 %all-to-all-start.1 = ((bf16[8,3,96,512]{3,2,1,0:T(8,128)(2,1)}), bf16[8,3,96,512]{3,2,1,0:T(8,128)(2,1)S(1)}, u32[]{:S(2)}, u32[]{:S(2)}) async-start(bf16[8,3,96,512]{3,2,1,0:T(8,128)(2,1)} %get-tuple-element.113), calls=%async_computation.1 | async-start | bytes 4718592 | tf_op jit(solution)/shard_map/all_to_all | solution.py:483
  154.8 1.9 collective-permute-start.14
  156.7 18.1 %collective-permute-done.14 = bf16[2,4,96,512]{3,2,0,1:T(8,128)(2,1)} collective-permute-done((bf16[2,4,96,512]{3,2,0,1:T(8,128)(2,1)}, bf16[2,4,96,512]{3,2,0,1:T(8,128)(2,1)}, u32[]{:S(2)}, u32[]{:S(2)}) %collective-permute-start.14) | collective-permute-done | bytes 786464 | tf_op jit(solution)/shard_map/ppermute | solution.py:56
  174.8 2.0 add_convert_fusion
  177.8 6.5 %collective-permute-start.15 = (bf16[2,96,512]{2,1,0:T(8,128)(2,1)S(1)}, bf16[2,96,512]{2,1,0:T(8,128)(2,1)S(1)}, u32[]{:S(2)}, u32[]{:S(2)}) collective-permute-start(bf16[2,96,512]{2,1,0:T(8,128)(2,1)S(1)} %get-tuple-element.132), channel_id=1, source_target_pairs={{0,128},{8,136},{16,144},{24,152},{32,160},{40,168},{48,176},{56,1... | collective-permute-start | bytes 589832 | tf_op jit(solution)/shard_map/ppermute | solution.py:56
  184.3 2.5 %collective-permute-start.16 = (bf16[2,96,512]{2,1,0:T(8,128)(2,1)S(1)}, bf16[2,96,512]{2,1,0:T(8,128)(2,1)S(1)}, u32[]{:S(2)}, u32[]{:S(2)}) collective-permute-start(bf16[2,96,512]{2,1,0:T(8,128)(2,1)S(1)} %get-tuple-element.134), channel_id=1, source_target_pairs={{0,64},{8,72},{16,80},{24,88},{32,96},{40,104},{48,112},{56,120},{... | collective-permute-start | bytes 589832 | tf_op jit(solution)/shard_map/ppermute | solution.py:56
  186.8 1.6 collective-permute-start.17
  188.5 10.5 %collective-permute-done.15 = bf16[2,96,512]{2,1,0:T(8,128)(2,1)S(1)} collective-permute-done((bf16[2,96,512]{2,1,0:T(8,128)(2,1)S(1)}, bf16[2,96,512]{2,1,0:T(8,128)(2,1)S(1)}, u32[]{:S(2)}, u32[]{:S(2)}) %collective-permute-start.15) | collective-permute-done | bytes 196640 | tf_op jit(solution)/shard_map/ppermute | solution.py:56
  199.0 4.4 %collective-permute-done.16 = bf16[2,96,512]{2,1,0:T(8,128)(2,1)S(1)} collective-permute-done((bf16[2,96,512]{2,1,0:T(8,128)(2,1)S(1)}, bf16[2,96,512]{2,1,0:T(8,128)(2,1)S(1)}, u32[]{:S(2)}, u32[]{:S(2)}) %collective-permute-start.16) | collective-permute-done | bytes 196640 | tf_op jit(solution)/shard_map/ppermute | solution.py:56
  204.6 2.0 collective-permute-start.13
  206.6 3.2 %collective-permute-done.18 = bf16[2,96,256]{2,1,0:T(8,128)(2,1)S(1)} collective-permute-done((bf16[2,96,256]{2,1,0:T(8,128)(2,1)S(1)}, bf16[2,96,256]{2,1,0:T(8,128)(2,1)S(1)}, u32[]{:S(2)}, u32[]{:S(2)}) %collective-permute-start.18) | collective-permute-done | bytes 98336 | tf_op jit(solution)/shard_map/ppermute | solution.py:43
  210.5 1.4 collective-permute-done.13.other
  213.3 4.2 %unpack.1 = (bf16[2,3,96,2048]{3,2,1,0:T(8,128)(2,1)}, bf16[2,3,128,256]{3,2,1,0:T(8,128)(2,1)}) custom-call(s32[5]{0:T(128)} %stack.41.idx, bf16[8,3,96,512]{3,2,1,0:T(8,128)(2,1)} %copy-done.1, bf16[3,128,256]{2,1,0:T(8,128)(2,1)} %get-tuple-element.114.own, bf16[3,128,256]{2,1,0:T(8,128)(2,1)} %copy-done.11), custom_call_target="tpu_custom_call" | custom-call | bytes 6291 | tf_op jit(solution)/shard_map/unpack/pallas_call | solution.py:158
  (65 shorter events, 19.2 us)
Async XLA Ops:
  7.2 5.4 %copy-start.12 = (bf16[256,96]{0,1:T(8,128)(2,1)S(1)}, bf16[256,96]{0,1:T(8,128)(2,1)}, u32[]{:S(2)}) copy-start(bf16[256,96]{0,1:T(8,128)(2,1)} %param.13) | copy-start | bytes 147460
  7.2 5.4 %copy-start.13 = (bf16[256,96]{0,1:T(8,128)(2,1)S(1)}, bf16[256,96]{0,1:T(8,128)(2,1)}, u32[]{:S(2)}) copy-start(bf16[256,96]{0,1:T(8,128)(2,1)} %param.12) | copy-start | bytes 147460
  8.5 9.2 %copy-start.2 = (bf16[96,3072]{1,0:T(8,128)(2,1)}, bf16[96,3072]{1,0:T(8,128)(2,1)S(1)}, u32[]{:S(2)}) copy-start(bf16[96,3072]{1,0:T(8,128)(2,1)S(1)} %get-tuple-element.93.refs_0_) | copy-start | bytes 1769476
  8.5 16.3 %collective-permute-start = (bf16[96,3072]{1,0:T(8,128)(2,1)S(1)}, bf16[96,3072]{1,0:T(8,128)(2,1)S(1)}, u32[]{:S(2)}, u32[]{:S(2)}) collective-permute-start(bf16[96,3072]{1,0:T(8,128)(2,1)S(1)} %get-tuple-element.64), channel_id=1, source_target_pairs={{0,1},{1,0},{2,3},{3,2},{4,5},{5,4},{6,7},{7,6},{8,9},{9,8},{10,11... | collective-permute-start | bytes 1769480 | tf_op jit(solution)/shard_map/ppermute | solution.py:43
  10.6 14.8 %collective-permute-start.1 = (bf16[96,3072]{1,0:T(8,128)(2,1)S(1)}, bf16[96,3072]{1,0:T(8,128)(2,1)S(1)}, u32[]{:S(2)}, u32[]{:S(2)}) collective-permute-start(bf16[96,3072]{1,0:T(8,128)(2,1)S(1)} %get-tuple-element.93.refs_0_), channel_id=1, source_target_pairs={{0,2},{1,3},{2,4},{3,5},{4,6},{5,7},{6,0},{7,1},{8,10},{9,11},{10,... | collective-permute-start | bytes 1769480 | tf_op jit(solution)/shard_map/ppermute | solution.py:43
  12.1 14.5 %collective-permute-start.2 = (bf16[96,3072]{1,0:T(8,128)(2,1)S(1)}, bf16[96,3072]{1,0:T(8,128)(2,1)S(1)}, u32[]{:S(2)}, u32[]{:S(2)}) collective-permute-start(bf16[96,3072]{1,0:T(8,128)(2,1)S(1)} %get-tuple-element.93.refs_0_), channel_id=1, source_target_pairs={{0,6},{1,7},{2,0},{3,1},{4,2},{5,3},{6,4},{7,5},{8,14},{9,15},{10,... | collective-permute-start | bytes 1769480 | tf_op jit(solution)/shard_map/ppermute | solution.py:43
  12.6 19.7 %collective-permute-start.8 = (bf16[2,96,256]{2,1,0:T(8,128)(2,1)S(1)}, bf16[2,96,256]{2,1,0:T(8,128)(2,1)S(1)}, u32[]{:S(2)}, u32[]{:S(2)}) collective-permute-start(bf16[2,96,256]{2,1,0:T(8,128)(2,1)S(1)} %get-tuple-element.138), channel_id=1, source_target_pairs={{0,1},{1,0},{2,3},{3,2},{4,5},{5,4},{6,7},{7,6},{8,9},{9,8},{10,11... | collective-permute-start | bytes 294920 | tf_op jit(solution)/shard_map/ppermute | solution.py:43
  24.8 1.8 copy-start.5
  25.3 1.3 copy-start.6
  26.6 55.1 %copy-start.14 = (s32[2]{0:T(128)S(1)}, s32[2]{0:T(128)}, u32[]{:S(2)}) copy-start(s32[2]{0:T(128)} %param.11) | copy-start | bytes 28
  27.5 51.7 %all-to-all-start = ((bf16[8,4,96,512]{3,2,1,0:T(8,128)(2,1)}), bf16[8,4,96,512]{3,2,1,0:T(8,128)(2,1)S(1)}, u32[]{:S(2)}, u32[]{:S(2)}) async-start(bf16[8,4,96,512]{3,2,1,0:T(8,128)(2,1)} %get-tuple-element.71), calls=%async_computation | async-start | bytes 6291456 | tf_op jit(solution)/shard_map/all_to_all | solution.py:452
  32.3 75.3 %all-gather.3.cloned.1.call-start = ((), (), s32[]{:S(2)}) async-start(), calls=%async_computation.2 | async-start | bytes 3342336 | tf_op jit(solution)/shard_map/all_gather | solution.py:442
  33.0 44.9 %collective-permute-start.3 = (bf16[96,3072]{1,0:T(8,128)(2,1)}, bf16[96,3072]{1,0:T(8,128)(2,1)S(1)}, u32[]{:S(2)}, u32[]{:S(2)}) collective-permute-start(bf16[96,3072]{1,0:T(8,128)(2,1)} %copy-done.5), channel_id=1, source_target_pairs={{0,2},{1,3},{2,4},{3,5},{4,6},{5,7},{6,0},{7,1},{8,10},{9,11},{10,... | collective-permute-start | bytes 1769480 | tf_op jit(solution)/shard_map/ppermute | solution.py:43
  34.5 44.6 %collective-permute-start.4 = (bf16[96,3072]{1,0:T(8,128)(2,1)}, bf16[96,3072]{1,0:T(8,128)(2,1)}, u32[]{:S(2)}, u32[]{:S(2)}) collective-permute-start(bf16[96,3072]{1,0:T(8,128)(2,1)} %copy-done.5), channel_id=1, source_target_pairs={{0,6},{1,7},{2,0},{3,1},{4,2},{5,3},{6,4},{7,5},{8,14},{9,15},{10,... | collective-permute-start | bytes 1769480 | tf_op jit(solution)/shard_map/ppermute | solution.py:43
  35.1 41.8 %collective-permute-start.5 = (bf16[3,128,256]{2,1,0:T(8,128)(2,1)}, bf16[3,128,256]{2,1,0:T(8,128)(2,1)S(1)}, u32[]{:S(2)}, u32[]{:S(2)}) collective-permute-start(bf16[3,128,256]{2,1,0:T(8,128)(2,1)} %get-tuple-element.72), channel_id=1, source_target_pairs={{0,1},{1,0},{2,3},{3,2},{4,5},{5,4},{6,7},{7,6},{8,9},{9,8},{10,11... | collective-permute-start | bytes 589832 | tf_op jit(solution)/shard_map/ppermute | solution.py:43
  76.9 5.4 %copy-start.9 = (bf16[3,128,256]{2,1,0:T(8,128)(2,1)}, bf16[3,128,256]{2,1,0:T(8,128)(2,1)S(1)}, u32[]{:S(2)}) copy-start(bf16[3,128,256]{2,1,0:T(8,128)(2,1)S(1)} %collective-permute-done.5.other) | copy-start | bytes 589828
  79.1 3.3 %copy-start = (bf16[8,4,96,512]{3,2,1,0:T(8,128)(2,1)}, bf16[8,4,96,512]{3,2,1,0:T(8,128)(2,1)S(1)}, u32[]{:S(2)}) copy-start(bf16[8,4,96,512]{3,2,1,0:T(8,128)(2,1)S(1)} %all-to-all-done.chunks.cot_text.refs_8_) | copy-start | bytes 9437188
  79.1 16.0 %collective-permute-start.6 = (bf16[96,3072]{1,0:T(8,128)(2,1)}, bf16[96,3072]{1,0:T(8,128)(2,1)}, u32[]{:S(2)}, u32[]{:S(2)}) collective-permute-start(bf16[96,3072]{1,0:T(8,128)(2,1)} %copy-done.6), channel_id=1, source_target_pairs={{0,2},{1,3},{2,4},{3,5},{4,6},{5,7},{6,0},{7,1},{8,10},{9,11},{10,... | collective-permute-start | bytes 1769480 | tf_op jit(solution)/shard_map/ppermute | solution.py:43
  80.5 14.6 %collective-permute-start.7 = (bf16[96,3072]{1,0:T(8,128)(2,1)}, bf16[96,3072]{1,0:T(8,128)(2,1)}, u32[]{:S(2)}, u32[]{:S(2)}) collective-permute-start(bf16[96,3072]{1,0:T(8,128)(2,1)} %collective-permute-done.4.refs_7_), channel_id=1, source_target_pairs={{0,6},{1,7},{2,0},{3,1},{4,2},{5,3},{6,4},{7,5},{8,14},{9,15},{10,... | collective-permute-start | bytes 1769480 | tf_op jit(solution)/shard_map/ppermute | solution.py:43
  107.6 5.9 %collective-permute-start.9 = (bf16[16,2,2,96,256]{4,3,2,1,0:T(8,128)(2,1)}, bf16[16,2,2,96,256]{4,3,2,1,0:T(8,128)(2,1)S(1)}, u32[]{:S(2)}, u32[]{:S(2)}) collective-permute-start(bf16[16,2,2,96,256]{4,3,2,1,0:T(8,128)(2,1)} %bitcast.46), channel_id=1, source_target_pairs={{0,8},{8,0},{16,24},{24,16},{32,40},{40,32},{48,56},{56,48},{64,72... | collective-permute-start | bytes 9437192 | tf_op jit(solution)/shard_map/ppermute | solution.py:56
  113.5 1.7 copy-start.3
  113.5 9.7 %collective-permute-start.10 = (bf16[2,16,96,512]{3,2,1,0:T(8,128)(2,1)}, bf16[2,16,96,512]{3,2,1,0:T(8,128)(2,1)}, u32[]{:S(2)}, u32[]{:S(2)}) collective-permute-start(bf16[2,16,96,512]{3,2,1,0:T(8,128)(2,1)} %get-tuple-element.91), channel_id=1, source_target_pairs={{0,8},{8,0},{16,24},{24,16},{32,40},{40,32},{48,56},{56,48},{64,72... | collective-permute-start | bytes 9437192 | tf_op jit(solution)/shard_map/ppermute | solution.py:56
  128.2 20.9 %collective-permute-start.11 = (bf16[2,4,96,512]{3,2,0,1:T(8,128)(2,1)S(1)}, bf16[2,4,96,512]{3,2,0,1:T(8,128)(2,1)S(1)}, u32[]{:S(2)}, u32[]{:S(2)}) collective-permute-start(bf16[2,4,96,512]{3,2,0,1:T(8,128)(2,1)S(1)} %fusion.1), channel_id=1, source_target_pairs={{0,16},{8,24},{16,32},{24,40},{32,48},{40,56},{48,0},{56,8},{64,80... | collective-permute-start | bytes 2359304 | tf_op jit(solution)/shard_map/ppermute | solution.py:56
  129.8 19.4 %collective-permute-start.12 = (bf16[2,4,96,512]{3,2,0,1:T(8,128)(2,1)S(1)}, bf16[2,4,96,512]{3,2,0,1:T(8,128)(2,1)}, u32[]{:S(2)}, u32[]{:S(2)}) collective-permute-start(bf16[2,4,96,512]{3,2,0,1:T(8,128)(2,1)S(1)} %fusion.3), channel_id=1, source_target_pairs={{0,48},{8,56},{16,0},{24,8},{32,16},{40,24},{48,32},{56,40},{64,11... | collective-permute-start | bytes 2359304 | tf_op jit(solution)/shard_map/ppermute | solution.py:56
  150.0 61.9 %all-to-all-start.1 = ((bf16[8,3,96,512]{3,2,1,0:T(8,128)(2,1)}), bf16[8,3,96,512]{3,2,1,0:T(8,128)(2,1)S(1)}, u32[]{:S(2)}, u32[]{:S(2)}) async-start(bf16[8,3,96,512]{3,2,1,0:T(8,128)(2,1)} %get-tuple-element.113), calls=%async_computation.1 | async-start | bytes 4718592 | tf_op jit(solution)/shard_map/all_to_all | solution.py:483
  154.8 20.0 %collective-permute-start.14 = (bf16[2,4,96,512]{3,2,0,1:T(8,128)(2,1)}, bf16[2,4,96,512]{3,2,0,1:T(8,128)(2,1)}, u32[]{:S(2)}, u32[]{:S(2)}) collective-permute-start(bf16[2,4,96,512]{3,2,0,1:T(8,128)(2,1)} %fusion.2), channel_id=1, source_target_pairs={{0,32},{8,40},{16,48},{24,56},{32,0},{40,8},{48,16},{56,24},{64,96... | collective-permute-start | bytes 2359304 | tf_op jit(solution)/shard_map/ppermute | solution.py:56
  177.8 21.2 %collective-permute-start.15 = (bf16[2,96,512]{2,1,0:T(8,128)(2,1)S(1)}, bf16[2,96,512]{2,1,0:T(8,128)(2,1)S(1)}, u32[]{:S(2)}, u32[]{:S(2)}) collective-permute-start(bf16[2,96,512]{2,1,0:T(8,128)(2,1)S(1)} %get-tuple-element.132), channel_id=1, source_target_pairs={{0,128},{8,136},{16,144},{24,152},{32,160},{40,168},{48,176},{56,1... | collective-permute-start | bytes 589832 | tf_op jit(solution)/shard_map/ppermute | solution.py:56
  184.3 19.1 %collective-permute-start.16 = (bf16[2,96,512]{2,1,0:T(8,128)(2,1)S(1)}, bf16[2,96,512]{2,1,0:T(8,128)(2,1)S(1)}, u32[]{:S(2)}, u32[]{:S(2)}) collective-permute-start(bf16[2,96,512]{2,1,0:T(8,128)(2,1)S(1)} %get-tuple-element.134), channel_id=1, source_target_pairs={{0,64},{8,72},{16,80},{24,88},{32,96},{40,104},{48,112},{56,120},{... | collective-permute-start | bytes 589832 | tf_op jit(solution)/shard_map/ppermute | solution.py:56
  186.8 16.6 %collective-permute-start.17 = (bf16[2,96,512]{2,1,0:T(8,128)(2,1)S(1)}, bf16[2,96,512]{2,1,0:T(8,128)(2,1)S(1)}, u32[]{:S(2)}, u32[]{:S(2)}) collective-permute-start(bf16[2,96,512]{2,1,0:T(8,128)(2,1)S(1)} %get-tuple-element.133), channel_id=1, source_target_pairs={{0,192},{8,200},{16,208},{24,216},{32,224},{40,232},{48,240},{56,2... | collective-permute-start | bytes 589832 | tf_op jit(solution)/shard_map/ppermute | solution.py:56
  204.5 5.3 %collective-permute-start.18 = (bf16[2,96,256]{2,1,0:T(8,128)(2,1)S(1)}, bf16[2,96,256]{2,1,0:T(8,128)(2,1)S(1)}, u32[]{:S(2)}, u32[]{:S(2)}) collective-permute-start(bf16[2,96,256]{2,1,0:T(8,128)(2,1)S(1)} %slice.25), channel_id=1, source_target_pairs={{0,1},{1,0},{2,3},{3,2},{4,5},{5,4},{6,7},{7,6},{8,9},{9,8},{10,11... | collective-permute-start | bytes 294920 | tf_op jit(solution)/shard_map/ppermute | solution.py:43
  204.6 7.3 %collective-permute-start.13 = (bf16[3,128,256]{2,1,0:T(8,128)(2,1)}, bf16[3,128,256]{2,1,0:T(8,128)(2,1)S(1)}, u32[]{:S(2)}, u32[]{:S(2)}) collective-permute-start(bf16[3,128,256]{2,1,0:T(8,128)(2,1)} %get-tuple-element.115), channel_id=1, source_target_pairs={{0,1},{1,0},{2,3},{3,2},{4,5},{5,4},{6,7},{7,6},{8,9},{9,8},{10,11... | collective-permute-start | bytes 589832 | tf_op jit(solution)/shard_map/ppermute | solution.py:43
  211.9 1.5 copy-start.1
  (5 other events, 4.1 us)
Sparse Core Ops, SparseCore 0:
  35.5 72.0 all-gather.2

commit v4 on v3

--- a/solution.py
+++ b/solution.py
@@ -404,17 +404,17 @@
     return [send_dp(shares[step], 0, step, 0) for step in steps]
 
 
-def sum_far_and_near(idx, total):
+def sum_far_and_near(idx, total, beside):
     def slab(step):
         return lax.dynamic_index_in_dim(
             total, lax.rem(idx[3] + step, 4), axis=1, keepdims=False
         )
 
     arrived = [send_dp(slab(step), step, 0, 0) for step in (2, 1, 3)]
-    total = wide_sum([slab(0)] + arrived)
+    total, beside = lax.optimization_barrier((wide_sum([slab(0)] + arrived), beside))
     last = send_sp(total[:, :, 256:].astype(BF), 0, 1)
     total = wide_sum([total[:, :, :256], last])
-    return [total[n].T for n in range(2)]
+    return total[0].T, total[1].T, beside
 
 
 def body(qkv_video, qkv_text, qk_gains, text_len, w_out_video, w_out_text, cot_video, cot_text):
@@ -483,7 +483,7 @@
     grads = lax.all_to_all(grads, "sp", 0, 0, tiled=True)
     other = send_sp(other, 0, 1)
     total = wide_sum([shares[0]] + near_sums + far_sums).astype(BF)
-    grad_w_video, grad_w_text = sum_far_and_near(idx, total)
+    grad_w_video, grad_w_text, other = sum_far_and_near(idx, total, other)
     grad_qkv_video, grad_qkv_text = unpack(idx, grads, own, other)
     return (grad_qkv_video, grad_qkv_text, grad_w_video, grad_w_text)
 

time: 225 us -> 225 us (level)
  transfers between devices with their start and end apart: 22 -> 22, of which waited for: 14 -> 13; matrix products, arithmetic and copies ran while one was open for 3% -> 3% of each run, Pallas kernels for 21% -> 21%
where the time goes in v4:
time: 225 us; the launch traced here: 224 us
  waiting for transfers between devices  102 us (45%)
  Pallas kernels  51.6 us (23%)
  starting transfers between devices  38 us (17%)
  between operations  14.2 us (6%)
  local copies, waits for them, and re-layouts  12.8 us (6%)
  other arithmetic  5.75 us (3%)
    ppermute x11, waiting for transfers between devices, send_sp(): return lax.ppermute(value, 'sp', sp_perm(dy, dz))  55 us
    ppermute x8, waiting for transfers between devices, send_dp(): return lax.ppermute(value, 'dp', dp_perm(dh, dx, dc))  44.4 us
    ppermute x8, starting transfers between devices, send_dp(): return lax.ppermute(value, 'dp', dp_perm(dh, dx, dc))  16 us
    pallas_call x1, Pallas kernels, forward(): pl.pallas_call(forward_kernel, grid=(4,), out_shape=[shape_of(4, SEQ, SEQ...  12.7 us
    ppermute x11, starting transfers between devices, send_sp(): return lax.ppermute(value, 'sp', sp_perm(dy, dz))  12.4 us
    pallas_call x1, Pallas kernels, backward(): pl.pallas_call(backward_kernel, grid=(4,), out_shape=[shape_of(8, 3, BLK,...  12.4 us
    pallas_call x1, Pallas kernels, weight_grad(): pl.pallas_call(weight_grad_kernel, grid=(8,), out_shape=[shape_of(2, 16,...  10.1 us
    pallas_call x1, Pallas kernels, project_back(): pl.pallas_call(grad_out_kernel, grid=(4,), in_specs=[SMEM] + [pl.BlockSpe...  8.04 us
  transfers between devices with their start and end apart: 22, of which 13 were waited for; matrix products, arithmetic and copies ran while one was open for 3% of the time, Pallas kernels for 21%

profile of v4, /device:TPU:8, one launch (start us, length us, event | category | flops | bytes accessed | tf_op | source)
XLA Modules:
  0.0 224.1 jit_solution(16593109455392016710)
XLA Ops:
  8.5 2.0 collective-permute-start
  10.6 1.6 collective-permute-start.1
  13.6 4.2 %pack.1 = (bf16[8,4,96,512]{3,2,1,0:T(8,128)(2,1)}, bf16[3,128,256]{2,1,0:T(8,128)(2,1)}, bf16[3,128,256]{2,1,0:T(8,128)(2,1)}) custom-call(s32[5]{0:T(128)} %stack.41.idx, bf16[2,3,96,2048]{3,2,1,0:T(8,128)(2,1)} %qkv.1, bf16[2,3,128,256]{3,2,1,0:T(8,128)(2,1)} %qt.1, bf16[2,128,384]{2,1,0:T(8,128)(2,1)} %ct.1), custom_call_target="tpu_custom_call" | custom-call | bytes 8388 | tf_op jit(solution)/shard_map/pack/pallas_call | solution.py:116
  17.8 7.0 %collective-permute-done.refs_1_ = bf16[96,3072]{1,0:T(8,128)(2,1)S(1)} collective-permute-done((bf16[96,3072]{1,0:T(8,128)(2,1)S(1)}, bf16[96,3072]{1,0:T(8,128)(2,1)S(1)}, u32[]{:S(2)}, u32[]{:S(2)}) %collective-permute-start) | collective-permute-done | bytes 589856 | tf_op jit(solution)/shard_map/ppermute | solution.py:43
  27.5 4.8 %all-to-all-start = ((bf16[8,4,96,512]{3,2,1,0:T(8,128)(2,1)}), bf16[8,4,96,512]{3,2,1,0:T(8,128)(2,1)S(1)}, u32[]{:S(2)}, u32[]{:S(2)}) async-start(bf16[8,4,96,512]{3,2,1,0:T(8,128)(2,1)} %get-tuple-element.73), calls=%async_computation | async-start | bytes 6291456 | tf_op jit(solution)/shard_map/all_to_all | solution.py:452
  33.0 1.5 collective-permute-start.3
  35.1 1.5 collective-permute-start.5
  36.6 40.4 %collective-permute-done.5.other = bf16[3,128,256]{2,1,0:T(8,128)(2,1)S(1)} collective-permute-done((bf16[3,128,256]{2,1,0:T(8,128)(2,1)}, bf16[3,128,256]{2,1,0:T(8,128)(2,1)S(1)}, u32[]{:S(2)}, u32[]{:S(2)}) %collective-permute-start.5) | collective-permute-done | bytes 196640 | tf_op jit(solution)/shard_map/ppermute | solution.py:43
  82.4 12.7 %forward.1 = (f32[4,896,896]{2,1,0:T(8,128)}, bf16[768,512]{1,0:T(8,128)(2,1)}, bf16[128,512]{1,0:T(8,128)(2,1)}) custom-call(s32[5]{0:T(128)} %stack.41.idx, s32[1]{0:T(128)} %dynamic_slice.48.length, f32[2,2,128]{2,1,0:T(2,128)} %gains.3, bf16[8,4,96,512]{3,2,1,0:T(8,128)(2,1)} %copy-done, bf16[3,128,256]{2,1,0:T(8,128)(2,1)} %get-tuple-element.76.own, ...), custom_call_target="tpu_custom_call" | custom-call | flops 1644167 | bytes 18874 | tf_op jit(solution)/shard_map/forward/pallas_call | solution.py:227
  95.1 10.1 %weight_grad.1 = (bf16[2,16,96,512]{3,2,1,0:T(8,128)(2,1)}, bf16[2,16,96,512]{3,2,1,0:T(8,128)(2,1)}) custom-call(s32[5]{0:T(128)} %stack.41.idx, bf16[768,512]{1,0:T(8,128)(2,1)} %get-tuple-element.82.att_video, bf16[128,512]{1,0:T(8,128)(2,1)} %get-tuple-element.83.att_text, bf16[8,4,96,512]{3,2,1,0:T(8,128)(2,1)} %copy-done, bf16[96,3072]{1,0:T(8,128)(2,1)} %copy-done.2, ...), custom_call_target="tpu_custom_call" | custom-call | flops 2818572 | bytes 12582 | tf_op jit(solution)/shard_map/weight_grad/pallas_call | solution.py:372
  105.2 2.4 %all-gather.3.cloned.1.call-done = bf16[32,2,96,256]{3,2,1,0:T(8,128)(2,1)} async-done(((bf16[2,2,96,256]{3,2,1,0:T(8,128)(2,1)}), bf16[32,2,96,256]{3,2,1,0:T(8,128)(2,1)}) %all-gather.3.cloned.1.call-update) | async-done | bytes 3145744 | tf_op jit(solution)/shard_map/all_gather | solution.py:442
  107.6 5.9 %collective-permute-done.9.refs_10_ = bf16[16,2,2,96,256]{4,3,2,1,0:T(8,128)(2,1)S(1)} collective-permute-done((bf16[16,2,2,96,256]{4,3,2,1,0:T(8,128)(2,1)}, bf16[16,2,2,96,256]{4,3,2,1,0:T(8,128)(2,1)S(1)}, u32[]{:S(2)}, u32[]{:S(2)}) %collective-permute-start.9) | collective-permute-done | bytes 3145760 | tf_op jit(solution)/shard_map/ppermute | solution.py:56
  113.6 1.5 copy-done.3
  115.1 8.0 %project_back.1.grad_out = bf16[896,512]{1,0:T(8,128)(2,1)} custom-call(s32[5]{0:T(128)} %stack.41.idx, bf16[96,3072]{1,0:T(8,128)(2,1)} %copy-done.2, bf16[96,3072]{1,0:T(8,128)(2,1)} %copy-done.5, bf16[96,3072]{1,0:T(8,128)(2,1)} %copy-done.6, bf16[96,3072]{1,0:T(8,128)(2,1)} %copy-done.8, bf16[96,3072]{1,0:T(8,128)(2,1)} %collective-permute-done.6.refs_4_, ...), custom_call_target="tpu_custom_call" | custom-call | flops 2818572 | bytes 13631 | tf_op jit(solution)/shard_map/project_back/pallas_call | solution.py:340
  123.2 3.2 %constant_dynamic-slice_fusion = (bf16[2,4,1,96,512]{4,3,2,1,0:T(8,128)(2,1)S(1)}, bf16[2,4,1,96,512]{4,3,2,1,0:T(8,128)(2,1)S(1)}, bf16[2,4,1,96,512]{4,3,2,1,0...) fusion(bf16[2,4,4,96,512]{4,3,2,1,0:T(8,128)(2,1)} %bitcast.15,, ...), kind=kLoop, calls=%fused_computation.23 | loop fusion | bytes 12582928 | tf_op jit(solution)/shard_map/jit(dynamic_index_in_dim)/dynamic_slice | solution.py:397
  128.2 1.5 collective-permute-start.11
  129.8 1.8 collective-permute-start.12
  131.6 12.4 %backward.1 = (bf16[8,3,96,512]{3,2,1,0:T(8,128)(2,1)}, bf16[3,128,256]{2,1,0:T(8,128)(2,1)}, bf16[3,128,256]{2,1,0:T(8,128)(2,1)}) custom-call(s32[5]{0:T(128)} %stack.41.idx, f32[2,2,128]{2,1,0:T(2,128)} %gains.3, f32[4,896,896]{2,1,0:T(8,128)} %get-tuple-element.109.prob_ref, bf16[896,512]{1,0:T(8,128)(2,1)} %project_back.1.grad_out, ...), custom_call_target="tpu_custom_call" | custom-call | flops 3288334 | bytes 20971 | tf_op jit(solution)/shard_map/backward/pallas_call | solution.py:296
  143.9 5.2 %collective-permute-done.11 = bf16[2,4,96,512]{3,2,0,1:T(8,128)(2,1)S(1)} collective-permute-done((bf16[2,4,96,512]{3,2,0,1:T(8,128)(2,1)S(1)}, bf16[2,4,96,512]{3,2,0,1:T(8,128)(2,1)S(1)}, u32[]{:S(2)}, u32[]{:S(2)}) %collective-permute-start.11) | collective-permute-done | bytes 786464 | tf_op jit(solution)/shard_map/ppermute | solution.py:56
  150.0 4.8 %all-to-all-start.1 = ((bf16[8,3,96,512]{3,2,1,0:T(8,128)(2,1)}), bf16[8,3,96,512]{3,2,1,0:T(8,128)(2,1)S(1)}, u32[]{:S(2)}, u32[]{:S(2)}) async-start(bf16[8,3,96,512]{3,2,1,0:T(8,128)(2,1)} %get-tuple-element.115), calls=%async_computation.1 | async-start | bytes 4718592 | tf_op jit(solution)/shard_map/all_to_all | solution.py:483
  154.8 1.9 collective-permute-start.13
  156.7 18.1 %collective-permute-done.13 = bf16[2,4,96,512]{3,2,0,1:T(8,128)(2,1)} collective-permute-done((bf16[2,4,96,512]{3,2,0,1:T(8,128)(2,1)}, bf16[2,4,96,512]{3,2,0,1:T(8,128)(2,1)}, u32[]{:S(2)}, u32[]{:S(2)}) %collective-permute-start.13) | collective-permute-done | bytes 786464 | tf_op jit(solution)/shard_map/ppermute | solution.py:56
  174.8 2.0 add_convert_fusion
  177.8 6.5 %collective-permute-start.14 = (bf16[2,96,512]{2,1,0:T(8,128)(2,1)S(1)}, bf16[2,96,512]{2,1,0:T(8,128)(2,1)S(1)}, u32[]{:S(2)}, u32[]{:S(2)}) collective-permute-start(bf16[2,96,512]{2,1,0:T(8,128)(2,1)S(1)} %get-tuple-element.136), channel_id=1, source_target_pairs={{0,128},{8,136},{16,144},{24,152},{32,160},{40,168},{48,176},{56,1... | collective-permute-start | bytes 589832 | tf_op jit(solution)/shard_map/ppermute | solution.py:56
  184.3 2.5 %collective-permute-start.15 = (bf16[2,96,512]{2,1,0:T(8,128)(2,1)S(1)}, bf16[2,96,512]{2,1,0:T(8,128)(2,1)S(1)}, u32[]{:S(2)}, u32[]{:S(2)}) collective-permute-start(bf16[2,96,512]{2,1,0:T(8,128)(2,1)S(1)} %get-tuple-element.138), channel_id=1, source_target_pairs={{0,64},{8,72},{16,80},{24,88},{32,96},{40,104},{48,112},{56,120},{... | collective-permute-start | bytes 589832 | tf_op jit(solution)/shard_map/ppermute | solution.py:56
  186.8 1.6 collective-permute-start.16
  188.5 1.5 collective-permute-start.17
  190.0 9.2 %collective-permute-done.14 = bf16[2,96,512]{2,1,0:T(8,128)(2,1)S(1)} collective-permute-done((bf16[2,96,512]{2,1,0:T(8,128)(2,1)S(1)}, bf16[2,96,512]{2,1,0:T(8,128)(2,1)S(1)}, u32[]{:S(2)}, u32[]{:S(2)}) %collective-permute-start.14) | collective-permute-done | bytes 196640 | tf_op jit(solution)/shard_map/ppermute | solution.py:56
  199.2 5.9 %collective-permute-done.15 = bf16[2,96,512]{2,1,0:T(8,128)(2,1)S(1)} collective-permute-done((bf16[2,96,512]{2,1,0:T(8,128)(2,1)S(1)}, bf16[2,96,512]{2,1,0:T(8,128)(2,1)S(1)}, u32[]{:S(2)}, u32[]{:S(2)}) %collective-permute-start.15) | collective-permute-done | bytes 196640 | tf_op jit(solution)/shard_map/ppermute | solution.py:56
  206.6 4.4 %collective-permute-done.18 = bf16[2,96,256]{2,1,0:T(8,128)(2,1)S(1)} collective-permute-done((bf16[2,96,256]{2,1,0:T(8,128)(2,1)S(1)}, bf16[2,96,256]{2,1,0:T(8,128)(2,1)S(1)}, u32[]{:S(2)}, u32[]{:S(2)}) %collective-permute-start.18) | collective-permute-done | bytes 98336 | tf_op jit(solution)/shard_map/ppermute | solution.py:43
  211.7 1.4 copy-done.1
  213.1 4.2 %unpack.1 = (bf16[2,3,96,2048]{3,2,1,0:T(8,128)(2,1)}, bf16[2,3,128,256]{3,2,1,0:T(8,128)(2,1)}) custom-call(s32[5]{0:T(128)} %stack.41.idx, bf16[8,3,96,512]{3,2,1,0:T(8,128)(2,1)} %copy-done.1, bf16[3,128,256]{2,1,0:T(8,128)(2,1)} %get-tuple-element.116.own, bf16[3,128,256]{2,1,0:T(8,128)(2,1)} %copy-done.11), custom_call_target="tpu_custom_call" | custom-call | bytes 6291 | tf_op jit(solution)/shard_map/unpack/pallas_call | solution.py:158
  (65 shorter events, 18.1 us)
Async XLA Ops:
  7.2 5.4 %copy-start.12 = (bf16[256,96]{0,1:T(8,128)(2,1)S(1)}, bf16[256,96]{0,1:T(8,128)(2,1)}, u32[]{:S(2)}) copy-start(bf16[256,96]{0,1:T(8,128)(2,1)} %param.13) | copy-start | bytes 147460
  7.2 5.4 %copy-start.13 = (bf16[256,96]{0,1:T(8,128)(2,1)S(1)}, bf16[256,96]{0,1:T(8,128)(2,1)}, u32[]{:S(2)}) copy-start(bf16[256,96]{0,1:T(8,128)(2,1)} %param.12) | copy-start | bytes 147460
  8.5 9.2 %copy-start.2 = (bf16[96,3072]{1,0:T(8,128)(2,1)}, bf16[96,3072]{1,0:T(8,128)(2,1)S(1)}, u32[]{:S(2)}) copy-start(bf16[96,3072]{1,0:T(8,128)(2,1)S(1)} %get-tuple-element.95.refs_0_) | copy-start | bytes 1769476
  8.5 16.3 %collective-permute-start = (bf16[96,3072]{1,0:T(8,128)(2,1)S(1)}, bf16[96,3072]{1,0:T(8,128)(2,1)S(1)}, u32[]{:S(2)}, u32[]{:S(2)}) collective-permute-start(bf16[96,3072]{1,0:T(8,128)(2,1)S(1)} %get-tuple-element.66), channel_id=1, source_target_pairs={{0,1},{1,0},{2,3},{3,2},{4,5},{5,4},{6,7},{7,6},{8,9},{9,8},{10,11... | collective-permute-start | bytes 1769480 | tf_op jit(solution)/shard_map/ppermute | solution.py:43
  10.6 14.8 %collective-permute-start.1 = (bf16[96,3072]{1,0:T(8,128)(2,1)S(1)}, bf16[96,3072]{1,0:T(8,128)(2,1)S(1)}, u32[]{:S(2)}, u32[]{:S(2)}) collective-permute-start(bf16[96,3072]{1,0:T(8,128)(2,1)S(1)} %get-tuple-element.95.refs_0_), channel_id=1, source_target_pairs={{0,2},{1,3},{2,4},{3,5},{4,6},{5,7},{6,0},{7,1},{8,10},{9,11},{10,... | collective-permute-start | bytes 1769480 | tf_op jit(solution)/shard_map/ppermute | solution.py:43
  12.1 14.5 %collective-permute-start.2 = (bf16[96,3072]{1,0:T(8,128)(2,1)S(1)}, bf16[96,3072]{1,0:T(8,128)(2,1)S(1)}, u32[]{:S(2)}, u32[]{:S(2)}) collective-permute-start(bf16[96,3072]{1,0:T(8,128)(2,1)S(1)} %get-tuple-element.95.refs_0_), channel_id=1, source_target_pairs={{0,6},{1,7},{2,0},{3,1},{4,2},{5,3},{6,4},{7,5},{8,14},{9,15},{10,... | collective-permute-start | bytes 1769480 | tf_op jit(solution)/shard_map/ppermute | solution.py:43
  12.6 19.7 %collective-permute-start.8 = (bf16[2,96,256]{2,1,0:T(8,128)(2,1)S(1)}, bf16[2,96,256]{2,1,0:T(8,128)(2,1)S(1)}, u32[]{:S(2)}, u32[]{:S(2)}) collective-permute-start(bf16[2,96,256]{2,1,0:T(8,128)(2,1)S(1)} %get-tuple-element.142), channel_id=1, source_target_pairs={{0,1},{1,0},{2,3},{3,2},{4,5},{5,4},{6,7},{7,6},{8,9},{9,8},{10,11... | collective-permute-start | bytes 294920 | tf_op jit(solution)/shard_map/ppermute | solution.py:43
  24.8 1.8 copy-start.5
  26.6 55.1 %copy-start.14 = (s32[2]{0:T(128)S(1)}, s32[2]{0:T(128)}, u32[]{:S(2)}) copy-start(s32[2]{0:T(128)} %param.11) | copy-start | bytes 28
  27.5 51.7 %all-to-all-start = ((bf16[8,4,96,512]{3,2,1,0:T(8,128)(2,1)}), bf16[8,4,96,512]{3,2,1,0:T(8,128)(2,1)S(1)}, u32[]{:S(2)}, u32[]{:S(2)}) async-start(bf16[8,4,96,512]{3,2,1,0:T(8,128)(2,1)} %get-tuple-element.73), calls=%async_computation | async-start | bytes 6291456 | tf_op jit(solution)/shard_map/all_to_all | solution.py:452
  32.3 75.3 %all-gather.3.cloned.1.call-start = ((), (), s32[]{:S(2)}) async-start(), calls=%async_computation.2 | async-start | bytes 3342336 | tf_op jit(solution)/shard_map/all_gather | solution.py:442
  33.0 44.9 %collective-permute-start.3 = (bf16[96,3072]{1,0:T(8,128)(2,1)}, bf16[96,3072]{1,0:T(8,128)(2,1)S(1)}, u32[]{:S(2)}, u32[]{:S(2)}) collective-permute-start(bf16[96,3072]{1,0:T(8,128)(2,1)} %copy-done.5), channel_id=1, source_target_pairs={{0,2},{1,3},{2,4},{3,5},{4,6},{5,7},{6,0},{7,1},{8,10},{9,11},{10,... | collective-permute-start | bytes 1769480 | tf_op jit(solution)/shard_map/ppermute | solution.py:43
  34.5 44.6 %collective-permute-start.4 = (bf16[96,3072]{1,0:T(8,128)(2,1)}, bf16[96,3072]{1,0:T(8,128)(2,1)}, u32[]{:S(2)}, u32[]{:S(2)}) collective-permute-start(bf16[96,3072]{1,0:T(8,128)(2,1)} %copy-done.5), channel_id=1, source_target_pairs={{0,6},{1,7},{2,0},{3,1},{4,2},{5,3},{6,4},{7,5},{8,14},{9,15},{10,... | collective-permute-start | bytes 1769480 | tf_op jit(solution)/shard_map/ppermute | solution.py:43
  35.1 41.8 %collective-permute-start.5 = (bf16[3,128,256]{2,1,0:T(8,128)(2,1)}, bf16[3,128,256]{2,1,0:T(8,128)(2,1)S(1)}, u32[]{:S(2)}, u32[]{:S(2)}) collective-permute-start(bf16[3,128,256]{2,1,0:T(8,128)(2,1)} %get-tuple-element.74), channel_id=1, source_target_pairs={{0,1},{1,0},{2,3},{3,2},{4,5},{5,4},{6,7},{7,6},{8,9},{9,8},{10,11... | collective-permute-start | bytes 589832 | tf_op jit(solution)/shard_map/ppermute | solution.py:43
  76.9 5.4 %copy-start.9 = (bf16[3,128,256]{2,1,0:T(8,128)(2,1)}, bf16[3,128,256]{2,1,0:T(8,128)(2,1)S(1)}, u32[]{:S(2)}) copy-start(bf16[3,128,256]{2,1,0:T(8,128)(2,1)S(1)} %collective-permute-done.5.other) | copy-start | bytes 589828
  79.1 3.3 %copy-start = (bf16[8,4,96,512]{3,2,1,0:T(8,128)(2,1)}, bf16[8,4,96,512]{3,2,1,0:T(8,128)(2,1)S(1)}, u32[]{:S(2)}) copy-start(bf16[8,4,96,512]{3,2,1,0:T(8,128)(2,1)S(1)} %all-to-all-done.chunks.cot_text.refs_8_) | copy-start | bytes 9437188
  79.1 16.0 %collective-permute-start.6 = (bf16[96,3072]{1,0:T(8,128)(2,1)}, bf16[96,3072]{1,0:T(8,128)(2,1)}, u32[]{:S(2)}, u32[]{:S(2)}) collective-permute-start(bf16[96,3072]{1,0:T(8,128)(2,1)} %copy-done.6), channel_id=1, source_target_pairs={{0,2},{1,3},{2,4},{3,5},{4,6},{5,7},{6,0},{7,1},{8,10},{9,11},{10,... | collective-permute-start | bytes 1769480 | tf_op jit(solution)/shard_map/ppermute | solution.py:43
  80.5 14.6 %collective-permute-start.7 = (bf16[96,3072]{1,0:T(8,128)(2,1)}, bf16[96,3072]{1,0:T(8,128)(2,1)}, u32[]{:S(2)}, u32[]{:S(2)}) collective-permute-start(bf16[96,3072]{1,0:T(8,128)(2,1)} %collective-permute-done.4.refs_7_), channel_id=1, source_target_pairs={{0,6},{1,7},{2,0},{3,1},{4,2},{5,3},{6,4},{7,5},{8,14},{9,15},{10,... | collective-permute-start | bytes 1769480 | tf_op jit(solution)/shard_map/ppermute | solution.py:43
  107.6 5.9 %collective-permute-start.9 = (bf16[16,2,2,96,256]{4,3,2,1,0:T(8,128)(2,1)}, bf16[16,2,2,96,256]{4,3,2,1,0:T(8,128)(2,1)S(1)}, u32[]{:S(2)}, u32[]{:S(2)}) collective-permute-start(bf16[16,2,2,96,256]{4,3,2,1,0:T(8,128)(2,1)} %bitcast.46), channel_id=1, source_target_pairs={{0,8},{8,0},{16,24},{24,16},{32,40},{40,32},{48,56},{56,48},{64,72... | collective-permute-start | bytes 9437192 | tf_op jit(solution)/shard_map/ppermute | solution.py:56
  113.5 1.7 copy-start.3
  113.5 9.7 %collective-permute-start.10 = (bf16[2,16,96,512]{3,2,1,0:T(8,128)(2,1)}, bf16[2,16,96,512]{3,2,1,0:T(8,128)(2,1)}, u32[]{:S(2)}, u32[]{:S(2)}) collective-permute-start(bf16[2,16,96,512]{3,2,1,0:T(8,128)(2,1)} %get-tuple-element.93), channel_id=1, source_target_pairs={{0,8},{8,0},{16,24},{24,16},{32,40},{40,32},{48,56},{56,48},{64,72... | collective-permute-start | bytes 9437192 | tf_op jit(solution)/shard_map/ppermute | solution.py:56
  128.2 20.9 %collective-permute-start.11 = (bf16[2,4,96,512]{3,2,0,1:T(8,128)(2,1)S(1)}, bf16[2,4,96,512]{3,2,0,1:T(8,128)(2,1)S(1)}, u32[]{:S(2)}, u32[]{:S(2)}) collective-permute-start(bf16[2,4,96,512]{3,2,0,1:T(8,128)(2,1)S(1)} %fusion.1), channel_id=1, source_target_pairs={{0,16},{8,24},{16,32},{24,40},{32,48},{40,56},{48,0},{56,8},{64,80... | collective-permute-start | bytes 2359304 | tf_op jit(solution)/shard_map/ppermute | solution.py:56
  129.8 19.4 %collective-permute-start.12 = (bf16[2,4,96,512]{3,2,0,1:T(8,128)(2,1)S(1)}, bf16[2,4,96,512]{3,2,0,1:T(8,128)(2,1)}, u32[]{:S(2)}, u32[]{:S(2)}) collective-permute-start(bf16[2,4,96,512]{3,2,0,1:T(8,128)(2,1)S(1)} %fusion.3), channel_id=1, source_target_pairs={{0,48},{8,56},{16,0},{24,8},{32,16},{40,24},{48,32},{56,40},{64,11... | collective-permute-start | bytes 2359304 | tf_op jit(solution)/shard_map/ppermute | solution.py:56
  150.0 61.7 %all-to-all-start.1 = ((bf16[8,3,96,512]{3,2,1,0:T(8,128)(2,1)}), bf16[8,3,96,512]{3,2,1,0:T(8,128)(2,1)S(1)}, u32[]{:S(2)}, u32[]{:S(2)}) async-start(bf16[8,3,96,512]{3,2,1,0:T(8,128)(2,1)} %get-tuple-element.115), calls=%async_computation.1 | async-start | bytes 4718592 | tf_op jit(solution)/shard_map/all_to_all | solution.py:483
  154.8 20.0 %collective-permute-start.13 = (bf16[2,4,96,512]{3,2,0,1:T(8,128)(2,1)}, bf16[2,4,96,512]{3,2,0,1:T(8,128)(2,1)}, u32[]{:S(2)}, u32[]{:S(2)}) collective-permute-start(bf16[2,4,96,512]{3,2,0,1:T(8,128)(2,1)} %fusion.2), channel_id=1, source_target_pairs={{0,32},{8,40},{16,48},{24,56},{32,0},{40,8},{48,16},{56,24},{64,96... | collective-permute-start | bytes 2359304 | tf_op jit(solution)/shard_map/ppermute | solution.py:56
  177.8 21.4 %collective-permute-start.14 = (bf16[2,96,512]{2,1,0:T(8,128)(2,1)S(1)}, bf16[2,96,512]{2,1,0:T(8,128)(2,1)S(1)}, u32[]{:S(2)}, u32[]{:S(2)}) collective-permute-start(bf16[2,96,512]{2,1,0:T(8,128)(2,1)S(1)} %get-tuple-element.136), channel_id=1, source_target_pairs={{0,128},{8,136},{16,144},{24,152},{32,160},{40,168},{48,176},{56,1... | collective-permute-start | bytes 589832 | tf_op jit(solution)/shard_map/ppermute | solution.py:56
  184.3 20.8 %collective-permute-start.15 = (bf16[2,96,512]{2,1,0:T(8,128)(2,1)S(1)}, bf16[2,96,512]{2,1,0:T(8,128)(2,1)S(1)}, u32[]{:S(2)}, u32[]{:S(2)}) collective-permute-start(bf16[2,96,512]{2,1,0:T(8,128)(2,1)S(1)} %get-tuple-element.138), channel_id=1, source_target_pairs={{0,64},{8,72},{16,80},{24,88},{32,96},{40,104},{48,112},{56,120},{... | collective-permute-start | bytes 589832 | tf_op jit(solution)/shard_map/ppermute | solution.py:56
  186.8 18.3 %collective-permute-start.16 = (bf16[2,96,512]{2,1,0:T(8,128)(2,1)S(1)}, bf16[2,96,512]{2,1,0:T(8,128)(2,1)}, u32[]{:S(2)}, u32[]{:S(2)}) collective-permute-start(bf16[2,96,512]{2,1,0:T(8,128)(2,1)S(1)} %get-tuple-element.137), channel_id=1, source_target_pairs={{0,192},{8,200},{16,208},{24,216},{32,224},{40,232},{48,240},{56,2... | collective-permute-start | bytes 589832 | tf_op jit(solution)/shard_map/ppermute | solution.py:56
  188.5 17.8 %collective-permute-start.17 = (bf16[3,128,256]{2,1,0:T(8,128)(2,1)}, bf16[3,128,256]{2,1,0:T(8,128)(2,1)S(1)}, u32[]{:S(2)}, u32[]{:S(2)}) collective-permute-start(bf16[3,128,256]{2,1,0:T(8,128)(2,1)} %get-tuple-element.121), channel_id=1, source_target_pairs={{0,1},{1,0},{2,3},{3,2},{4,5},{5,4},{6,7},{7,6},{8,9},{9,8},{10,11... | collective-permute-start | bytes 589832 | tf_op jit(solution)/shard_map/ppermute | solution.py:43
  206.3 5.5 %copy-start.11 = (bf16[3,128,256]{2,1,0:T(8,128)(2,1)}, bf16[3,128,256]{2,1,0:T(8,128)(2,1)S(1)}, u32[]{:S(2)}) copy-start(bf16[3,128,256]{2,1,0:T(8,128)(2,1)S(1)} %collective-permute-done.17.other) | copy-start | bytes 589828
  206.3 4.7 %collective-permute-start.18 = (bf16[2,96,256]{2,1,0:T(8,128)(2,1)S(1)}, bf16[2,96,256]{2,1,0:T(8,128)(2,1)S(1)}, u32[]{:S(2)}, u32[]{:S(2)}) collective-permute-start(bf16[2,96,256]{2,1,0:T(8,128)(2,1)S(1)} %slice.24), channel_id=1, source_target_pairs={{0,1},{1,0},{2,3},{3,2},{4,5},{5,4},{6,7},{7,6},{8,9},{9,8},{10,11... | collective-permute-start | bytes 294920 | tf_op jit(solution)/shard_map/ppermute | solution.py:43
  211.7 1.4 copy-start.1
  (5 other events, 4.7 us)
Sparse Core Ops, SparseCore 0:
  35.5 72.0 all-gather.2
